TPU v7x, 32 devices: a whole 2x2x4 slice. The times are simulated.
32 devices in a mesh: dp: 16 (over z, y, x), tensor: 2 (over core).
Axes of the slice: x: 2, y: 2, z: 4, core: 2. Of those that a mesh axis runs over, the one named last changes fastest.
Arguments:
- hidden_in: bfloat16 [2, 16, 512, 768], P(None, 'dp'), may hold values from -6 to 6
- lengths: int32 [2, 16], P(None, 'dp'), may hold values from 16 to 512, as said below
- labels: int32 [2, 16], P(None, 'dp'), may hold values from 0 to 2
- out_cot: bfloat16 [2, 16, 512, 768], P(None, 'dp'), may hold values from -6 to 6
- input_weight: bfloat16 [3, 768, 768], P(None, 'dp', 'tensor'), may hold values from -0.21875 to 0.21875
- input_bias: bfloat16 [2, 768], P(None, ('tensor', 'dp')), may hold values from -3 to 3
- out_weight: bfloat16 [768, 768], P('tensor', 'dp'), may hold values from -1.75 to 1.75
- out_bias: bfloat16 [768], P('dp'), may hold values from -3 to 3
- first_gain: bfloat16 [768], P('dp'), may hold values from 0.5 to 1.5
- first_shift: bfloat16 [768], P('dp'), may hold values from -2 to 2
- up_weight: bfloat16 [768, 3072], P('dp', 'tensor'), may hold values from -0.21875 to 0.21875
- up_bias: bfloat16 [3072], P(('tensor', 'dp')), may hold values from -3 to 3
- down_weight: bfloat16 [3072, 768], P('tensor', 'dp'), may hold values from -0.21875 to 0.21875
- down_bias: bfloat16 [768], P('dp'), may hold values from -3 to 3
- second_gain: bfloat16 [768], P('dp'), may hold values from 0.5 to 1.5
- second_shift: bfloat16 [768], P('dp'), may hold values from -2 to 2
- pool_weight: bfloat16 [768, 768], P('dp'), may hold values from -0.21875 to 0.21875
- pool_bias: bfloat16 [768], P('dp'), may hold values from -3 to 3
- class_weight: bfloat16 [768, 3], P('dp'), may hold values from -0.4375 to 0.4375
- class_bias: bfloat16 [3], replicated, may hold values from -3 to 3
Outputs:
- block_out: bfloat16 [2, 16, 512, 768], P(None, 'dp')
- logits: float32 [2, 16, 3], P(None, 'dp')
- hidden_gradient: bfloat16 [2, 16, 512, 768], P(None, 'dp')
- input_weight_gradient: float32 [3, 768, 768], P(None, 'dp', 'tensor')
- input_bias_gradient: float32 [2, 768], P(None, ('tensor', 'dp'))
- out_weight_gradient: float32 [768, 768], P('tensor', 'dp')
- out_bias_gradient: float32 [768], P('dp')
- first_gain_gradient: float32 [768], P('dp')
- first_shift_gradient: float32 [768], P('dp')
- up_weight_gradient: float32 [768, 3072], P('dp', 'tensor')
- up_bias_gradient: float32 [3072], P(('tensor', 'dp'))
- down_weight_gradient: float32 [3072, 768], P('tensor', 'dp')
- down_bias_gradient: float32 [768], P('dp')
- second_gain_gradient: float32 [768], P('dp')
- second_shift_gradient: float32 [768], P('dp')
- pool_weight_gradient: float32 [768, 768], P('dp')
- pool_bias_gradient: float32 [768], P('dp')
- class_weight_gradient: float32 [768, 3], P('dp')
- class_bias_gradient: float32 [3], replicated
Inputs may be any that keep to these rules, and one draw needn't show every extreme that they name: `lengths`: each sequence's valid tokens; in every draw some sequence has exactly 512 and some exactly 16.
All inputs are finite; a program needn't handle non-finite values.
Results may differ from a plain program's by a relative error of at most 0.023.
Values may be sent and summed in bfloat16 or wider, within the bound.
No kernel may reach another device: no remote copies, remote signals or barrier semaphores. Data moves between devices by JAX's collectives and lax.ppermute only.
A program may use at most 192 MiB of HBM per device.

v0:
```python
import functools
import math

import jax
import jax.numpy as jnp
from jax import lax
from jax.experimental import pallas as pl
from jax.experimental.pallas import tpu as pltpu
from jax.sharding import PartitionSpec as P

HD = 64
LANES = 128
BLOCKS = 16
EPS = 1e-06
BF = jnp.bfloat16
F32 = jnp.float32
NN = ((1,), (0,))
NT = ((1,), (1,))
TN = ((0,), (0,))
HBM = pl.BlockSpec(memory_space=pltpu.HBM)
SCALARS = pl.BlockSpec(memory_space=pltpu.SMEM)
VMEM = pl.BlockSpec(memory_space=pltpu.VMEM)
MIB = 1024 * 1024
FLOPS_PER_MICROSECOND = 1_150_000_000

OUT_B, GAIN_1, SHIFT_1, DOWN_B, GAIN_2, SHIFT_2, POOL_B, CLASS, QUERY_B, VALUE_B, UP_B = (
    0, 1, 2, 3, 4, 5, 6, 7, 10, 11, 12,
)
SHARED, PAIR_ROW, UP_ROW, CLASS_ROW = 10, 10, 11, 12


def dot(left, right, dims=NN):
    return lax.dot_general(left, right, (dims, ((), ())), preferred_element_type=F32)


def begin(source, target, sem):
    copy = pltpu.make_async_copy(source, target, sem)
    copy.start()
    return copy


def row_block(me, mask, rows):
    return pl.ds(pl.multiple_of((me ^ mask) * rows, 16), rows)


def load(pieces, target, sems, columns=None):
    cut, width = pieces[0].shape
    start, width = columns or (0, width)
    for i, piece in enumerate(pieces):
        begin(piece.at[:, pl.ds(start, width)], target.at[i // 2, pl.ds(i % 2 * cut, cut), :], sems.at[i])


def landed(target, sem):
    pltpu.make_async_copy(target, target, sem).wait()


def loaded(target, h, sems):
    cut = target.shape[1] // 2
    for i in range(2):
        landed(target.at[h, pl.ds(i * cut, cut), :], sems.at[2 * h + i])


def to_blocks(source, target, masks, me):
    rows = source.shape[0] // BLOCKS
    for j in range(BLOCKS):
        target[j * rows : (j + 1) * rows, :] = source[row_block(me, masks[j], rows), :]


def to_rows(source, target, masks, me):
    rows = target.shape[0] // BLOCKS
    for j in range(BLOCKS):
        target[row_block(me, masks[j], rows), :] = source[j * rows : (j + 1) * rows, :]


def row_product(matrices, rights):
    return sum(dot(matrices[h], rights[h], NT) for h in range(2))


def pair_product(lefts, rights, lower, upper):
    cut = lefts[0].shape[0] // 2
    columns = rights[0].shape[1]
    for i, target in enumerate((lower, upper)):
        span = slice(i * cut, (i + 1) * cut)
        total = dot(lefts[0][span, :], rights[0][...]) + dot(lefts[1][span, :], rights[1][...])
        target[:, 0:columns] = total.astype(BF)


def mean(array):
    return jnp.mean(array, -1, keepdims=True)


def normalize(total):
    centered = total - mean(total)
    root = lax.rsqrt(mean(centered * centered) + EPS)
    return centered * root, root


def norm_backward(delta, normed, root, gain):
    scaled = delta * gain
    return root * (scaled - mean(scaled) - normed * mean(scaled * normed))


def column_sum(array):
    return jnp.sum(array, 0, keepdims=True)


def unpack_vectors(extra, vec, h):
    width = vec.shape[1]
    rows, part = width // BLOCKS, width // BLOCKS // 2
    for b in range(BLOCKS):
        own = extra[b * rows : b * rows + 16, :]
        if h == 0:
            vec[0:SHARED, b * rows : (b + 1) * rows] = own[0:SHARED, 0:rows]
        at = h * width // 2 + b * part
        vec[QUERY_B : QUERY_B + 1, at : at + part] = own[PAIR_ROW : PAIR_ROW + 1, 0:part]
        vec[VALUE_B : VALUE_B + 1, at : at + part] = own[PAIR_ROW : PAIR_ROW + 1, part:rows]
        row, at = UP_B + 2 * h + b // (BLOCKS // 2), b % (BLOCKS // 2) * 2 * rows
        vec[row : row + 1, at : at + 2 * rows] = own[UP_ROW : UP_ROW + 1, 0 : 2 * rows]


def pack_vectors(sums, query, value, up, extra):
    width = sums.shape[1]
    rows, part = width // BLOCKS, width // BLOCKS // 2
    extra[...] = jnp.zeros(extra.shape, F32)
    for b in range(BLOCKS):
        top = b * rows
        extra[top : top + SHARED, 0:rows] = sums[0:SHARED, b * rows : (b + 1) * rows]
        at = b * part
        extra[top + PAIR_ROW : top + PAIR_ROW + 1, 0:part] = query[:, at : at + part]
        extra[top + PAIR_ROW : top + PAIR_ROW + 1, part:rows] = value[:, at : at + part]
        at = b * 2 * rows
        extra[top + UP_ROW : top + UP_ROW + 1, 0 : 2 * rows] = up[:, at : at + 2 * rows]
        extra[top + CLASS_ROW : top + CLASS_ROW + 1, :] = sums[SHARED : SHARED + 1, 0:LANES]


def prepare_kernel(masks_p, masks_q, info, hidden, *refs):
    outs, (rows_p, rows_q, x, other_x, flip, held, sems) = refs[0:4], refs[4:]
    me, core = info[0], info[1]
    begin(hidden.at[core], x, sems.at[0])
    begin(hidden.at[1 - core], other_x, sems.at[1])
    for i, source in enumerate((x, other_x)):
        landed(source, sems.at[i])
        flip[...] = source[...].T
        for n, masks in enumerate((masks_p, masks_q)):
            to_blocks(flip, held.at[2 * i + n], masks, me)
            begin(held.at[2 * i + n], outs[2 * i + n], sems.at[2 + 2 * i + n])
    rows_p[...] = held[0].T
    rows_q[...] = held[1].T
    for i in range(4):
        landed(held.at[i], sems.at[2 + i])


def attend_kernel(masks_p, masks_q, info, hidden, rows_p, rows_q, *refs):
    qk, vo = refs[0:4], refs[4:8]
    q, k, v, att_own, att_other, p, first, first_p = refs[8:16]
    normed, root, vec = refs[16:19]
    x, wa, wb, att, flip, wide, extra, sems = refs[19:]
    me, core = info[0], info[1]
    count = info[2 + core]
    length, width = x.shape
    half = width // 2
    load(vo, wb, sems.at[pl.ds(2, 4)])
    load(qk, wa, sems.at[pl.ds(6, 4)])
    begin(hidden.at[core], x, sems.at[0])
    rows = width // BLOCKS
    for h in range(2):
        loaded(wb, h, sems.at[pl.ds(2, 4)])
        for j in range(BLOCKS):
            piece = wb[h, j * rows : (j + 1) * rows, width:]
            extra[row_block(me, masks_q[j], rows), :] = piece.astype(F32)
        unpack_vectors(extra, vec, h)
    for h in range(2):
        own = slice(h * half, (h + 1) * half)
        loaded(wa, h, sems.at[pl.ds(6, 4)])
        both = dot(rows_p[...], wa[h])
        q[:, own] = (both[:, :half] + vec[QUERY_B : QUERY_B + 1, own]).astype(BF) * (1.0 / math.sqrt(HD))
        k[:, own] = both[:, half:].astype(BF)
        v[:, own] = (dot(rows_q[...], wb[h, :, 0:half]) + vec[VALUE_B : VALUE_B + 1, own]).astype(BF)
    keys = lax.broadcasted_iota(jnp.int32, (1, length), 1)
    bias = jnp.where(keys < count, 0.0, -1e30).astype(F32)
    lane = lax.broadcasted_iota(jnp.int32, (1, LANES), 1)
    for pair in range(width // LANES):
        cols = slice(pair * LANES, (pair + 1) * LANES)
        q_pair, k_pair, v_pair = q[:, cols], k[:, cols], v[:, cols]
        acc = None
        for a in range(2):
            mine = (lane < HD) if a == 0 else (lane >= HD)
            scores = dot(jnp.where(mine, q_pair, 0.0).astype(BF), k_pair, NT) + bias
            weights = jnp.exp(scores - jnp.max(scores, -1, keepdims=True))
            probs = (weights * (1.0 / jnp.sum(weights, -1, keepdims=True))).astype(BF)
            p[pair, a] = probs
            term = dot(probs, jnp.where(mine, v_pair, 0.0).astype(BF))
            acc = term if acc is None else acc + term
        att[:, cols] = acc.astype(BF)
    att_own[...] = att[:, :half]
    att_other[...] = att[:, half:]
    to_rows(row_product([wb[h, :, half:width] for h in range(2)], (att[:, :half], att[:, half:])), wide, masks_q, me)
    landed(x, sems.at[0])
    own_normed, own_root = normalize(x[...].astype(F32) + wide[...].T + vec[OUT_B : OUT_B + 1, :])
    normed[...] = own_normed
    root[...] = jnp.broadcast_to(own_root, root.shape)
    low = (own_normed * vec[GAIN_1 : GAIN_1 + 1, :] + vec[SHIFT_1 : SHIFT_1 + 1, :]).astype(BF)
    first[...] = low
    flip[...] = low.T
    to_blocks(flip, first_p, masks_p, me)


def up_kernel(vec, first_p, *refs):
    pieces = refs[0:4]
    active, other_active, slope, w, sems = refs[4:]
    width = first_p.shape[0]
    half = active.shape[1]
    load(pieces, w, sems, (0, half))
    left = first_p[...].T
    chunk = 256
    for h, target in enumerate((active, other_active)):
        loaded(w, h, sems)
        for c in range(half // chunk):
            cols = slice(c * chunk, (c + 1) * chunk)
            at = h * half + c * chunk
            row, lane = UP_B + at // width, at % width
            hidden = dot(left, w[h, :, cols]) + vec[row : row + 1, lane : lane + chunk]
            cdf = 0.5 + 0.5 * lax.erf(hidden * math.sqrt(0.5))
            density = jnp.exp(hidden * hidden * -0.5) * (1.0 / math.sqrt(2.0 * math.pi))
            target[:, cols] = (hidden * cdf).astype(BF)
            slope[:, at : at + chunk] = (cdf + hidden * density).astype(BF)


def ramp_kernel(masks, pool_masks, info, class_bias, vec, cotangent, active, other_active, first, *refs):
    pieces, pool_pieces = refs[0:4], refs[4:8]
    block, ramp, feed_r, second, grads, w = refs[8:14]
    cot, right, pool, flip, wide, slim, z, sems = refs[14:]
    me, core = info[0], info[1]
    count, label = info[2 + core], info[4 + core]
    length, width = first.shape
    half = width // 2
    cut = w.shape[2]
    load(pieces, w, sems.at[pl.ds(0, 4)])
    begin(other_active, right, sems.at[8])
    load(pool_pieces, pool, sems.at[pl.ds(4, 4)], (cut, half))
    begin(cotangent.at[core], cot, sems.at[9])
    loaded(w, 0, sems)
    part = dot(w[0], active[...], NT)
    landed(right, sems.at[8])
    loaded(w, 1, sems)
    to_rows(part + dot(w[1], right[...], NT), wide, masks, me)
    total = first[...].astype(F32) + wide[...].T + vec[DOWN_B : DOWN_B + 1, :]
    gain, shift = vec[GAIN_2 : GAIN_2 + 1, :], vec[SHIFT_2 : SHIFT_2 + 1, :]
    normed, root = normalize(total)
    ids = lax.broadcasted_iota(jnp.int32, (length, 1), 0)
    block[...] = jnp.where(ids < count, normed * gain + shift, 0.0).astype(BF)
    for h in range(2):
        loaded(pool, h, sems.at[pl.ds(4, 4)])
    head = (normed[0:8, :] * gain + shift).astype(BF)
    sides = [pl.ds(pl.multiple_of(side * half, LANES), half) for side in (core, 1 - core)]
    slim[:, 0:8] = head.astype(F32).T
    for j in range(BLOCKS):
        at = slice(j * (width // BLOCKS), (j + 1) * (width // BLOCKS))
        slim[at, LANES : LANES + 8] = slim[row_block(me, pool_masks[j], width // BLOCKS), 0:8]
    head_t = slim[:, LANES : LANES + 8].astype(BF)
    for h in range(2):
        z[:, sides[h]] = dot(head_t, pool[h], TN)
    pooled_wide = jnp.tanh(z[...] + vec[POOL_B : POOL_B + 1, :])
    pooled = pooled_wide.astype(BF).astype(F32)
    class_rows = [vec[CLASS + c : CLASS + c + 1, :] for c in range(3)]
    logits = [
        jnp.sum(pooled * class_rows[c], -1, keepdims=True) + class_bias[c] for c in range(3)
    ]
    top = jnp.maximum(jnp.maximum(logits[0], logits[1]), logits[2])
    powers = [jnp.exp(l - top) for l in logits]
    power_sum = powers[0] + powers[1] + powers[2]
    deltas = [powers[c] / power_sum - jnp.where(label == c, 1.0, 0.0) for c in range(3)]
    pre = sum(deltas[c] * class_rows[c] for c in range(3)) * (1.0 - pooled_wide * pooled_wide)
    pre_high = pre.astype(BF)
    z[0:8, :] = pre_high.astype(F32)
    high = [z[:, side].astype(BF) for side in sides]
    z[0:8, :] = pre - pre_high.astype(F32)
    low = [z[:, side].astype(BF) for side in sides]
    slim[:, 0:8] = row_product(pool, high) + row_product(pool, low)
    for j in range(BLOCKS):
        at = slice(j * (width // BLOCKS), (j + 1) * (width // BLOCKS))
        slim[row_block(me, pool_masks[j], width // BLOCKS), LANES : LANES + 8] = slim[at, 0:8]
    head_delta = slim[:, LANES : LANES + 8].T[0:1, :]
    lane = lax.broadcasted_iota(jnp.int32, (1, width), 1)
    tail = jnp.zeros((1, width), F32)
    for c in range(3):
        tail = jnp.where(lane == c, deltas[c][0:1], tail)
        tail = jnp.where(lane == LANES + c, logits[c][0:1], tail)
    ramp[0:1, :] = head[0:1, :].astype(F32)
    ramp[1:2, :] = pooled[0:1, :]
    ramp[2:3, :] = pre[0:1, :]
    ramp[3:4, :] = tail
    ramp[4:8, :] = jnp.zeros((4, width), F32)
    landed(cot, sems.at[9])
    delta = jnp.where(ids < count, cot[...].astype(F32), 0.0) + jnp.where(ids == 0, head_delta, 0.0)
    grads[0:1, :] = column_sum(delta * normed)
    grads[1:2, :] = column_sum(delta)
    dsecond = norm_backward(delta, normed, root, gain)
    grads[2:3, :] = column_sum(dsecond)
    grads[3:4, :] = pre[0:1, :]
    for c in range(3):
        grads[4 + c : 5 + c, :] = deltas[c][0:1] * pooled[0:1, :]
    grads[7:8, :] = tail
    second[...] = dsecond
    flip[...] = dsecond.astype(BF).T
    to_blocks(flip, feed_r, masks, me)


def hidden_kernel(feed_r, slope, w, delta, other_delta):
    half = delta.shape[1]
    left = feed_r[...].T
    chunk = 512
    for h, target in ((1, other_delta), (0, delta)):
        for c in range(half // chunk):
            cols = slice(c * chunk, (c + 1) * chunk)
            at = h * half + c * chunk
            target[:, cols] = (dot(left, w[h, :, cols]) * slope[:, at : at + chunk].astype(F32)).astype(BF)


def down_grad_kernel(masks, info, ramp, ramp_other, left_in, left_other_in, right, right_other_in, *refs):
    lower, upper, logits, left, left_other, right_other, wide, slim, sems = refs
    loads = ((left_in, left), (left_other_in, left_other), (right_other_in, right_other))
    for i, (source, target) in enumerate(loads):
        begin(source, target, sems.at[i])
    width, columns = left.shape[0], right.shape[1]
    half = width // 2
    own = pl.ds(pl.multiple_of(info[1] * half, LANES), half)
    classes = logits.shape[1]
    pair = [r[3:4, LANES : LANES + classes] for r in (ramp, ramp_other)]
    logits[0:1, :] = jnp.where(info[1] == 0, pair[0], pair[1])
    logits[1:2, :] = jnp.where(info[1] == 0, pair[1], pair[0])
    none = jnp.zeros((14, width), F32)
    wide[...] = jnp.concatenate([ramp[0:1, :], ramp_other[0:1, :], none], 0).T
    to_blocks(wide, slim, masks, info[0])
    heads = slim[...].astype(BF)
    pres = jnp.concatenate([ramp[2:3, own], ramp_other[2:3, own], none[:, :half]], 0).astype(BF)
    for i, target in enumerate((lower, upper)):
        target[:, columns:] = dot(heads[i * half : (i + 1) * half], pres).astype(BF)
    for i, (_, target) in enumerate(loads):
        landed(target, sems.at[i])
    pair_product((left, left_other), (right, right_other), lower, upper)


def up_grad_kernel(left, left_other, right, right_other_in, *refs):
    lower, upper, sums, right_other, sems = refs
    begin(right_other_in, right_other, sems.at[0])
    own_sum = column_sum(right[...].astype(F32))
    landed(right_other, sems.at[0])
    sums[...] = own_sum + column_sum(right_other[...].astype(F32))
    pair_product((left, left_other), (right, right_other), lower, upper)


def branch_kernel(masks_p, masks_q, info, vec, sums_in, delta, other_delta, second, normed, root, wu, *refs):
    vo = refs[0:4]
    total_out, datt, branch_p, grads = refs[4:8]
    wo, right, flip, rows_q, wide, sems = refs[8:]
    me = info[0]
    width = normed.shape[1]
    half = width // 2
    begin(other_delta, right, sems.at[4])
    load(vo, wo, sems.at[pl.ds(0, 4)], (half, half))
    gain = vec[GAIN_1 : GAIN_1 + 1, :]
    part = dot(wu[0], delta[...], NT)
    landed(right, sems.at[4])
    to_rows(part + dot(wu[1], right[...], NT), wide, masks_p, me)
    dfirst = second[...] + wide[...].T
    own_normed = normed[...]
    total = norm_backward(dfirst, own_normed, root[:, 0:1], gain)
    total_out[...] = total
    flip[...] = total.astype(BF).T
    to_blocks(flip, branch_p, masks_p, me)
    to_blocks(flip, rows_q, masks_q, me)
    grads[0:1, :] = column_sum(total)
    grads[1:2, :] = column_sum(dfirst * own_normed)
    grads[2:3, :] = column_sum(dfirst)
    grads[3 : SHARED + 1, :] = sums_in[...]
    grads[SHARED + 1 :, :] = jnp.zeros((grads.shape[0] - SHARED - 1, width), F32)
    left = rows_q[...].T
    for h in range(2):
        loaded(wo, h, sems)
        datt[:, h * half : (h + 1) * half] = dot(left, wo[h]).astype(BF)


def back_kernel(q, k, v, att_own, att_other, datt, p, *refs):
    own_out, other_out = refs[0:2]
    att, dq, dk, dv = refs[2:]
    length, width = q.shape
    half = width // 2
    att[:, :half] = att_own[...]
    att[:, half:] = att_other[...]
    lane = lax.broadcasted_iota(jnp.int32, (1, LANES), 1)
    pairs = width // LANES

    for pair in range(pairs):
        cols = slice(pair * LANES, (pair + 1) * LANES)
        do = datt[:, cols]
        product = do.astype(F32) * att[:, cols].astype(F32)
        k_pair, v_pair = k[:, cols], v[:, cols]
        q_t = q[:, cols].T
        do_t = do.T
        dq_sum = None
        dk_parts, dv_parts = [], []
        for a in range(2):
            mine = (lane < HD) if a == 0 else (lane >= HD)
            shift = jnp.sum(jnp.where(mine, product, 0.0), -1, keepdims=True)
            dprobs = dot(jnp.where(mine, do, 0.0).astype(BF), v_pair, NT)
            probs = p[pair, a]
            dscores = (probs.astype(F32) * (dprobs - shift)).astype(BF)
            term = dot(dscores, jnp.where(mine, k_pair, 0.0).astype(BF))
            dq_sum = term if dq_sum is None else dq_sum + term
            own = slice(a * HD, (a + 1) * HD)
            dk_parts.append(dot(q_t[own], dscores))
            dv_parts.append(dot(do_t[own], probs))
        dq[:, cols] = (dq_sum * (1.0 / math.sqrt(HD))).astype(BF)
        dk[:, cols] = jnp.concatenate(dk_parts, 0).T.astype(BF)
        dv[:, cols] = jnp.concatenate(dv_parts, 0).T.astype(BF)
    for h, out in ((1, other_out), (0, own_out)):
        for i, source in enumerate((dq, dk, dv)):
            out[:, i * half : (i + 1) * half] = source[:, h * half : (h + 1) * half]


def out_grad_kernel(branch_t, other_branch_t, att, other_att, grad):
    grad[...] = (dot(branch_t[...], att[...]) + dot(other_branch_t[...], other_att[...])).astype(BF)


def input_grad_kernel(
    masks_p, info, sums_in, sums_other, up_sums, x_p, x_q, other_p, other_q, delta, other_delta, out_grad, *refs
):
    qk_pieces, vo_pieces = refs[0:2], refs[2:4]
    extra = refs[4]
    me = info[0]
    width = x_p.shape[0]
    half = width // 2
    rows = width // BLOCKS
    columns = column_sum(delta[...].astype(F32)) + column_sum(other_delta[...].astype(F32))
    pack_vectors(sums_in[...] + sums_other[...], columns[:, :half], columns[:, width:], up_sums[...], extra)
    for i, target in enumerate(vo_pieces):
        span = slice(i * half, (i + 1) * half)
        total = dot(x_p[span, :], delta[:, width:]) + dot(other_p[span, :], other_delta[:, width:])
        target[:, 0:half] = total.astype(BF)
        target[:, half:width] = out_grad[span, :]
        for j in range(BLOCKS // 2):
            at = row_block(me, masks_p[i * (BLOCKS // 2) + j], rows)
            target[j * rows : (j + 1) * rows, width:] = extra[at, :].astype(BF)
    pair_product((x_q, other_q), (delta.at[:, pl.ds(0, width)], other_delta.at[:, pl.ds(0, width)]), *qk_pieces)


def hop_kernel(*refs):
    sent, kept = refs[-2:]
    at = 0
    for own, arrived in zip(refs[0:-2:2], refs[1:-2:2]):
        half, _, width = sent.shape[0], 0, own.shape[2]
        cols = slice(at, at + width)
        sent[:, :, cols] = own[half:] + arrived[half:]
        kept[:, :, cols] = own[:half] + arrived[:half]
        at += width


def finish_kernel(kept, arrived, input_out, out_out, pair_out, up_out, class_bias_out, class_out, *vectors):
    share = kept[0].astype(F32) + arrived[0].astype(F32)
    rows, half = input_out.shape[1:]
    for i in range(3):
        input_out[i] = share[:, i * half : (i + 1) * half]
    out_out[...] = share[:, 3 * half : 4 * half].T
    extra = share[:, 4 * half :]
    for i, target in enumerate(vectors):
        target[...] = extra[i : i + 1, 0:rows]
    pair_out[0:1, :] = extra[PAIR_ROW : PAIR_ROW + 1, 0 : rows // 2]
    pair_out[1:2, :] = extra[PAIR_ROW : PAIR_ROW + 1, rows // 2 : rows]
    up_out[...] = extra[UP_ROW : UP_ROW + 1, 0 : 2 * rows]
    class_bias_out[...] = extra[CLASS_ROW : CLASS_ROW + 1, 0 : class_bias_out.shape[1]]
    class_out[...] = extra[:, 0:rows].T[:, len(vectors) : SHARED]


def arrange_kernel(info, block_own, block_other, grad_own, grad_other, block_out, grad_out, held, sems):
    core = info[1]
    moves = (
        (block_own, block_out, core),
        (block_other, block_out, 1 - core),
        (grad_own, grad_out, core),
        (grad_other, grad_out, 1 - core),
    )
    for i, (source, _, _) in enumerate(moves):
        begin(source, held.at[i], sems.at[i])
    for i, (_, target, side) in enumerate(moves):
        landed(held.at[i], sems.at[i])
        begin(held.at[i], target.at[side], sems.at[4 + i])
    for i in range(4):
        landed(held.at[i], sems.at[4 + i])


def input_kernel(masks_p, masks_q, info, own, other, total, *refs):
    qk, vo = refs[0:4], refs[4:8]
    out, wa, wv, wide, wide_v, sems = refs[8:]
    me = info[0]
    width = total.shape[1]
    half = width // 2
    load(vo, wv, sems.at[pl.ds(0, 4)], (0, half))
    load(qk, wa, sems.at[pl.ds(4, 4)])
    for h in range(2):
        loaded(wv, h, sems.at[pl.ds(0, 4)])
    to_rows(row_product(wv, (own[:, width:], other[:, width:])), wide_v, masks_q, me)
    for h in range(2):
        loaded(wa, h, sems.at[pl.ds(4, 4)])
    to_rows(row_product(wa, (own[:, :width], other[:, :width])), wide, masks_p, me)
    out[...] = (total[...] + (wide[...] + wide_v[...]).T).astype(BF)


def costing(micros):
    return pl.CostEstimate(flops=micros * FLOPS_PER_MICROSECOND, bytes_accessed=1024, transcendentals=0)


def call(body, name, micros, mib, in_specs, outs, scratch, sems, args):
    return pl.pallas_call(
        body,
        name=name,
        in_specs=in_specs,
        out_specs=[spec for _, spec in outs],
        out_shape=[shape for shape, _ in outs],
        scratch_shapes=[pltpu.VMEM(s, d) for s, d in scratch] + [pltpu.SemaphoreType.DMA((sems,))] * (sems > 0),
        compiler_params=pltpu.CompilerParams(vmem_limit_bytes=mib * MIB),
        cost_estimate=costing(micros),
    )(*args)


def orders(size):
    bits = [1 << k for k in range(size.bit_length() - 1)]
    high = bits[2:][::-1]
    x_last, y_last = high + [2, 1], high + [1, 2]
    return (x_last, y_last, x_last, [1] + high + [2]), (y_last, x_last, x_last, [1] + high + [2])


def block_mask(index, order):
    mask = 0
    for k, bit in enumerate(order):
        if (index >> k) & 1:
            mask ^= bit
    return mask


def swap(array, mask):
    size = lax.axis_size("dp")
    return lax.ppermute(array, "dp", [(i, i ^ mask) for i in range(size)])


def swap_core(array):
    return lax.ppermute(array, "tensor", [(0, 1), (1, 0)])


def after(array, *others):
    return lax.optimization_barrier((array, *others))[0]


def join(left, right):
    return jnp.concatenate([left, right], 0)


def gather_blocks(shard, order):
    held = shard[None]
    for mask in order:
        held = join(held, swap(held, mask))
    return held


def hop(blocks, arrived):
    half = blocks.shape[0] // 2
    return blocks[half:] + arrived[half:], blocks[:half] + arrived[:half]


def scatter_blocks(blocks, order):
    for mask in order[::-1]:
        half = blocks.shape[0] // 2
        blocks = blocks[:half] + swap(blocks[half:], mask)
    return blocks[0]


def in_order(blocks, order, me):
    size = len(blocks)
    place = [0] * size
    for j in range(size):
        place[block_mask(j, order)] = j
    chosen = jnp.array(place)[jnp.arange(size) ^ me]
    return jnp.take(blocks, chosen, axis=0)


def out_of_order(blocks, order, me):
    owners = jnp.array([block_mask(j, order) for j in range(len(blocks))]) ^ me
    return jnp.take(blocks, owners, axis=0)


def extra_columns(shared, pair, up, rows):
    def lanes(array):
        return jnp.pad(array, ((0, 0), (0, 0), (0, LANES - array.shape[2])))

    columns = jnp.concatenate([lanes(shared), lanes(pair), lanes(up)], 1)
    return jnp.pad(columns, ((0, 0), (0, rows - columns.shape[1]), (0, 0)))


def per_device(
    hidden_in,
    lengths,
    labels,
    out_cot,
    input_weight,
    input_bias,
    out_weight,
    out_bias,
    first_gain,
    first_shift,
    up_weight,
    up_bias,
    down_weight,
    down_bias,
    second_gain,
    second_shift,
    pool_weight,
    pool_bias,
    class_weight,
    class_bias,
):
    size = lax.axis_size("dp")
    me = lax.axis_index("dp")
    core = lax.axis_index("tensor")
    length, width = hidden_in.shape[2:]
    rows = width // size
    half = input_weight.shape[2]
    hidden_half = up_weight.shape[1]
    hidden_width = 2 * hidden_half
    classes = class_bias.shape[0]
    pairs = width // LANES
    block = width // BLOCKS
    lower = BLOCKS // 2
    direct = size == BLOCKS
    (order_a, order_b, order_u, order_d), (back_a, back_b, back_u, back_d) = orders(size)

    def kernel_masks(order):
        return [block_mask(j, order) if direct else j for j in range(BLOCKS)]

    (a_masks, b_masks, u_masks, d_masks), back_masks = [[kernel_masks(o) for o in part] for part in orders(size)]

    inputs = hidden_in.reshape(2, length, width)
    cotangents = out_cot.reshape(2, length, width)
    info = jnp.concatenate(
        [
            jnp.stack([me if direct else jnp.zeros_like(me), core]).astype(jnp.int32),
            lengths.reshape(-1),
            labels.reshape(-1),
        ]
    )

    def shape(*dims, dtype=BF):
        return jax.ShapeDtypeStruct(dims, dtype)

    def of(s):
        return (s.shape, s.dtype)

    def in_vmem(*shapes):
        return [(s, VMEM) for s in shapes]

    def in_hbm(*shapes):
        return [(s, HBM) for s in shapes]

    row = shape(length, width)
    flat = shape(width, length)
    x_p, x_q, other_p, other_q, rows_p, rows_q = call(
        functools.partial(prepare_kernel, a_masks, b_masks),
        "prepare",
        0,
        8,
        [SCALARS, HBM],
        in_hbm(flat, flat, flat, flat) + in_vmem(row, row),
        [of(row), of(row), of(flat), ((4, width, length), BF)],
        6,
        (info, inputs),
    )

    pool_half = lax.dynamic_slice_in_dim(pool_weight, core * half, half, 1)
    a_shard = jnp.concatenate([input_weight[0], input_weight[1]], 1)
    vo_shard = jnp.concatenate([input_weight[2], out_weight.T], 1)
    u_shard = jnp.concatenate([up_weight, pool_half], 1)
    d_shard = down_weight.T
    shared = jnp.concatenate(
        [
            jnp.stack(
                [out_bias, first_gain, first_shift, down_bias, second_gain, second_shift, pool_bias]
            ),
            class_weight.T,
        ],
        0,
    )
    def with_other(lo, hi):
        return flat_rows(lo, hi, swap_core(lo), swap_core(hi))

    def flat_rows(*arrays):
        return tuple(array.reshape(-1, array.shape[2]) for array in arrays)

    def by_block(arrays):
        return [array.reshape(lower, block, array.shape[1]) for array in arrays]

    if direct:
        extra = extra_columns(
            shared[None], input_bias.reshape(1, 1, rows), up_bias.reshape(1, 1, 2 * rows), rows
        )
        b_shard = jnp.concatenate([vo_shard, after(extra, a_shard, d_shard)[0]], 1)
        a0, b0, u0, d0 = a_shard[None], b_shard[None], u_shard[None], d_shard[None]
        z1, z0 = order_a[0], order_a[1]
        a1, b1, d1 = swap(a0, z1), swap(b0, z1), swap(d0, 1)
        a2, b2 = join(a0, a1), join(b0, b1)
        a2_in, b2_in = swap(a2, z0), swap(b2, z0)
        u1 = swap(after(u0, a2, b2), z1)
        a4, b4 = join(a2, a2_in), join(b2, b2_in)
        a4_in, b4_in = swap(a4, 2), swap(b4, 1)
        u2 = after(join(u0, u1), a4, b4)
        d2 = after(join(d0, d1), a4, b4)
        u2_in, d2_in = swap(u2, z0), swap(d2, z1)
        u4 = join(u2, u2_in)
        u4_in = swap(u4, 2)
        a8, b8 = join(a4, a4_in), join(b4, b4_in)
        a8_in, b8_in = swap(a8, 1), swap(b8, 2)
        a8_other, b8_other = swap_core(a8), swap_core(b8)
        d4 = after(join(d2, d2_in), a8, b8)
        d4_in = swap(d4, z0)
        u8 = after(join(u4, u4_in), a8_in, b8, rows_q)
        u8_in = swap(u8, 1)
        d8 = after(join(d4, d4_in), b8_in, u8)
        d8_in = swap(d8, 2)
        info = after(info, u8, d8)
        qk = flat_rows(a8, a8_in, a8_other, swap_core(a8_in))
        vo = flat_rows(b8, b8_in, b8_other, swap_core(b8_in))
        pieces = [(u8, u8_in), (d8, d8_in)]
    else:

        def whole(shard, order):
            return in_order(gather_blocks(shard, order), order, me)

        def cut(array):
            blocks = array.reshape(BLOCKS, block, -1)
            return blocks[:lower], blocks[lower:]

        shared = whole(shared, order_a).transpose(1, 0, 2).reshape(-1, BLOCKS, block)
        pair = whole(input_bias, order_a).transpose(1, 0, 2).reshape(2, BLOCKS, block // 2)
        extra = extra_columns(
            shared.transpose(1, 0, 2),
            pair.transpose(1, 0, 2).reshape(BLOCKS, 1, block),
            whole(up_bias, order_a).reshape(BLOCKS, 1, 2 * block),
            block,
        )
        vo = cut(whole(vo_shard, order_b))
        vo = jnp.concatenate([vo[0], extra[:lower]], 2), jnp.concatenate([vo[1], extra[lower:]], 2)
        qk, vo = with_other(*cut(whole(a_shard, order_a))), with_other(*vo)
        pieces = [cut(whole(u_shard, order_u)), cut(whole(d_shard, order_d))]

    wide = shape(length, hidden_width)
    norm = shape(length, width, dtype=F32)
    roots = shape(length, LANES, dtype=F32)
    eight = shape(8, width, dtype=F32)
    vectors = shape(16, width, dtype=F32)
    probs = shape(pairs, 2, length, length)

    def grad(columns):
        return [shape(half, columns)] * 2

    part = width + LANES
    slim = shape(length, half)
    halved = shape(length, hidden_half)
    thirds = shape(length, 3 * half)
    matrix = shape(width, hidden_width)

    def blocks_of(columns):
        return shape(2, width, columns)

    q, k, v, att, att_other, p, first, first_p, normed, root, vec = call(
        functools.partial(attend_kernel, a_masks, b_masks),
        "attend",
        0,
        18,
        [SCALARS, HBM, VMEM, VMEM] + [HBM] * 8,
        in_vmem(row, row, row, slim, slim, probs, row, flat, norm, roots, vectors),
        [of(row), of(blocks_of(width)), of(blocks_of(part)), of(row), of(flat), ((width, length), F32)]
        + [((width, LANES), F32)],
        10,
        (info, inputs, rows_p, rows_q, *qk, *vo),
    )
    (up_lo, up_hi), (down_lo, down_hi) = pieces
    up_hi, down_hi = after(up_hi, first), after(down_hi, first)
    up = with_other(up_lo, up_hi)
    down = with_other(down_lo, down_hi)
    first_in, att_in = swap_core(first_p), swap_core(att_other)
    act, act_other, slope, up_matrix = call(
        up_kernel,
        "up",
        0,
        4,
        [VMEM, VMEM] + [HBM] * 4,
        in_vmem(halved, halved, wide, blocks_of(hidden_half)),
        [],
        4,
        (vec, first_p, *up),
    )
    act_in = swap_core(act_other)
    block_out, ramp, feed, second, sums_two, down_matrix = call(
        functools.partial(ramp_kernel, d_masks, u_masks),
        "ramp",
        15,
        14,
        [SCALARS, SCALARS, VMEM, HBM, VMEM, HBM, VMEM] + [HBM] * 8,
        in_vmem(row, eight, flat, norm, eight, blocks_of(hidden_half)),
        [of(row), of(halved), of(blocks_of(half)), of(flat), ((width, length), F32), ((width, 2 * LANES), F32)]
        + [of(eight)],
        10,
        (info, class_bias.astype(F32), vec, cotangents, act, act_other, first, *down, *up),
    )
    feed_in, ramp_in = swap_core(feed), swap_core(ramp)
    delta, delta_other = call(
        hidden_kernel,
        "hidden",
        400,
        5,
        [VMEM] * 3,
        in_vmem(halved, halved),
        [],
        0,
        (after(feed, act_in, first_in, att_in), slope, down_matrix),
    )
    delta_in = swap_core(delta_other)
    *down_grad, logits_out = call(
        functools.partial(down_grad_kernel, back_masks[3]),
        "down_grad",
        400,
        6,
        [SCALARS, VMEM, VMEM, HBM, HBM, VMEM, HBM],
        in_vmem(*grad(hidden_half + half), shape(2, classes, dtype=F32)),
        [of(flat), of(flat), of(halved), ((width, 16), F32), ((width, 16), F32)],
        3,
        (after(info, delta), ramp, ramp_in, feed, feed_in, act, act_in),
    )

    def first_hop(pieces, order):
        return swap(pieces[1], order[-1]) if direct else None

    def add(*streams):
        columns = sum(own.shape[2] for own, _ in streams)
        return call(
            hop_kernel,
            "hop",
            0,
            2,
            [VMEM] * (2 * len(streams)),
            in_vmem(*[shape(streams[0][0].shape[0] // 2, block, columns)] * 2),
            [],
            0,
            tuple(array for stream in streams for array in stream),
        )

    def next_hop(kept, arrived, mask, start):
        if not direct:
            return kept, None
        sent, kept = add((after(kept, start), arrived))
        return kept, swap(sent, mask)

    down_grad = by_block(down_grad)
    down_arrived = first_hop(down_grad, back_d)
    *up_grad, up_sums = call(
        up_grad_kernel,
        "up_grad",
        0,
        6,
        [VMEM] * 3 + [HBM],
        in_vmem(*grad(hidden_half), shape(1, hidden_half, dtype=F32)),
        [of(halved)],
        1,
        (after(first_p, down_grad[0]), first_in, delta, delta_in),
    )
    up_grad = by_block(up_grad)
    up_arrived = first_hop(up_grad, back_u)
    block_in = swap_core(after(block_out, up_sums))
    total, datt, branch, sums_one = call(
        functools.partial(branch_kernel, u_masks, b_masks),
        "branch",
        0,
        11,
        [SCALARS] + [VMEM] * 3 + [HBM] + [VMEM] * 4 + [HBM] * 4,
        in_vmem(norm, row, flat, vectors),
        [of(blocks_of(half)), of(halved), of(flat), of(flat), ((width, length), F32)],
        5,
        (after(info, up_grad[0]), vec, sums_two, delta, delta_other, second, normed, root, up_matrix, *vo),
    )
    branch_in, sums_in = swap_core(branch), swap_core(sums_one)
    dqkv, dqkv_other = call(
        back_kernel,
        "back",
        0,
        10,
        [VMEM] * 7,
        in_vmem(thirds, thirds),
        [of(row)] * 4,
        0,
        (q, k, v, att, att_other, after(datt, block_in), p),
    )
    dqkv_in = swap_core(dqkv_other)
    (input_delta,) = call(
        functools.partial(input_kernel, a_masks, b_masks),
        "input",
        0,
        9,
        [SCALARS] + [VMEM] * 3 + [HBM] * 8,
        in_vmem(row),
        [of(blocks_of(width)), of(blocks_of(half)), ((width, length), F32), ((width, length), F32)],
        8,
        (info, dqkv, dqkv_other, total, *qk, *vo),
    )
    up_kept, up_arrived = next_hop(up_grad[0], up_arrived, back_u[2], input_delta)
    (out_grad,) = call(
        out_grad_kernel,
        "out_grad",
        0,
        3,
        [VMEM] * 4,
        in_vmem(shape(width, half)),
        [],
        0,
        (after(branch, dqkv, sums_in, up_kept), branch_in, att, att_in),
    )
    input_grads = call(
        functools.partial(input_grad_kernel, back_masks[1]),
        "input_grad",
        0,
        4,
        [SCALARS] + [VMEM] * 10,
        in_vmem(*grad(width), *grad(part)),
        [((width, LANES), F32)],
        0,
        (info, sums_one, sums_in, up_sums, x_p, x_q, other_p, other_q, dqkv, dqkv_in, out_grad),
    )
    qk_grad, vo_grad = by_block(input_grads[:2]), by_block(input_grads[2:])
    qk_arrived, vo_arrived = first_hop(qk_grad, back_a), first_hop(vo_grad, back_b)
    input_delta_in = swap_core(input_delta)
    down_kept, down_arrived = next_hop(down_grad[0], down_arrived, back_d[2], qk_grad[0])
    up_kept, up_arrived = next_hop(up_kept, up_arrived, back_u[1], down_kept)
    qk_kept, qk_arrived = next_hop(qk_grad[0], qk_arrived, back_a[2], down_kept)
    vo_kept, vo_arrived = next_hop(vo_grad[0], vo_arrived, back_b[2], down_kept)
    down_kept, down_arrived = next_hop(down_kept, down_arrived, back_d[1], vo_kept)
    blocks_out, input_grad = call(
        arrange_kernel,
        "arrange",
        0,
        4,
        [SCALARS] + [HBM] * 4,
        in_hbm(*[shape(2, length, width)] * 2),
        [((4, length, width), BF)],
        8,
        (after(info, qk_kept, vo_kept), block_out, block_in, input_delta, input_delta_in),
    )
    if direct:
        sent, kept = add((after(qk_kept, blocks_out), qk_arrived), (vo_kept, vo_arrived))
        arrived = swap(sent, back_a[1])
        down_kept, down_arrived = next_hop(down_kept, down_arrived, back_d[0], kept)
        up_kept, up_arrived = next_hop(up_kept, up_arrived, back_u[0], kept)
        sent, kept = add((after(kept, down_kept, up_kept), arrived))
        arrived = swap(sent, back_a[0])
        down_kept, up_kept = after(down_kept, kept), after(up_kept, kept)
        down_share, up_share = (down_kept + down_arrived)[0], (up_kept + up_arrived)[0]
        kept = after(kept, down_share, up_share)
    else:

        def spread(pieces, order):
            return scatter_blocks(out_of_order(join(*pieces).reshape(size, rows, -1), order, me), order)

        down_share, up_share = spread(down_grad, back_d), spread(up_grad, back_u)
        qk_share = spread(qk_grad, back_a)
    down_share, pool_share = down_share[:, :hidden_half], down_share[:, hidden_half:]
    pool_shares = pool_share, swap_core(pool_share)
    pool_grad = jnp.where(
        core == 0, jnp.concatenate(pool_shares, 1), jnp.concatenate(pool_shares[::-1], 1)
    ).astype(F32)
    if direct:
        input_share, out_share, pair_share, up_bias_share, class_bias_grad, class_grad, *vector_grads = call(
            finish_kernel,
            "finish",
            0,
            2,
            [VMEM] * 2,
            in_vmem(
                shape(3, rows, half, dtype=F32),
                shape(half, rows, dtype=F32),
                shape(2, rows // 2, dtype=F32),
                shape(1, 2 * rows, dtype=F32),
                shape(1, classes, dtype=F32),
                shape(rows, classes, dtype=F32),
                *[shape(1, rows, dtype=F32)] * 7,
            ),
            [],
            0,
            (kept, arrived),
        )
        up_bias_share, class_bias_grad = up_bias_share.reshape(-1), class_bias_grad.reshape(-1)
        vector_grads = [array.reshape(-1) for array in vector_grads]
    else:
        vo_share = spread([piece[:, :, :width] for piece in vo_grad], back_b)
        extra_sum = lax.psum(join(*[piece[:, :, width:] for piece in vo_grad]).astype(F32), "dp")

        def own(array, count):
            return lax.dynamic_slice_in_dim(array, me * count, count, array.ndim - 1)

        vector_grads = own(extra_sum[:, :SHARED, :block].transpose(1, 0, 2).reshape(SHARED, width), rows)
        pair_sums = extra_sum[:, PAIR_ROW, :block].reshape(BLOCKS, 2, block // 2)
        pair_share = own(pair_sums.transpose(1, 0, 2).reshape(2, half), rows // 2)
        up_bias_share = own(extra_sum[:, UP_ROW, : 2 * block].reshape(-1), 2 * rows)
        class_bias_grad = extra_sum[0, CLASS_ROW, :classes]
        vector_grads, class_grad = vector_grads[:7], vector_grads[7:].T
        input_share = jnp.stack([qk_share[:, :half], qk_share[:, half:], vo_share[:, :half]])
        out_share = vo_share[:, half:width].T
    return (
        blocks_out[:, None],
        logits_out[:, None],
        input_grad[:, None],
        input_share.astype(F32),
        pair_share.astype(F32),
        out_share.astype(F32),
        vector_grads[0],
        vector_grads[1],
        vector_grads[2],
        up_share.astype(F32),
        up_bias_share.astype(F32),
        down_share.T.astype(F32),
        vector_grads[5],
        vector_grads[3],
        vector_grads[4],
        pool_grad,
        vector_grads[6],
        class_grad,
        class_bias_grad.astype(F32),
    )


def solution(mesh):
    placed = (
        P(None, "dp", None, None),
        P(None, "dp"),
        P(None, "dp"),
        P(None, "dp", None, None),
        P(None, "dp", "tensor"),
        P(None, ("tensor", "dp")),
        P("tensor", "dp"),
        P("dp"),
        P("dp"),
        P("dp"),
        P("dp", "tensor"),
        P(("tensor", "dp")),
        P("tensor", "dp"),
        P("dp"),
        P("dp"),
        P("dp"),
        P("dp", None),
        P("dp"),
        P("dp", None),
        P(),
    )
    return jax.shard_map(
        per_device,
        mesh=mesh,
        in_specs=placed,
        out_specs=(
            P(None, "dp", None, None),
            P(None, "dp", None),
            P(None, "dp", None, None),
            P(None, "dp", "tensor"),
            P(None, ("tensor", "dp")),
            P("tensor", "dp"),
            P("dp"),
            P("dp"),
            P("dp"),
            P("dp", "tensor"),
            P(("tensor", "dp")),
            P("tensor", "dp"),
            P("dp"),
            P("dp"),
            P("dp"),
            P("dp", None),
            P("dp"),
            P("dp", None),
            P(),
        ),
        check_vma=False,
    )
```

profile of v0, /device:TPU:0, one launch (start us, length us, event | category | flops | bytes accessed | tf_op | source)
XLA Modules:
  0.0 242.3 jit_solution(6570500342276783993)
XLA Ops:
  0.7 0.8 slice_bitcast_fusion
  1.5 4.1 %collective-permute-start = (bf16[1,48,768]{2,1,0:T(8,128)(2,1)S(1)}, bf16[1,48,768]{2,1,0:T(8,128)(2,1)S(1)}, u32[]{:S(2)}, u32[]{:S(2)}) collective-permute-start(bf16[1,48,768]{2,1,0:T(8,128)(2,1)S(1)} %fusion.7), channel_id=1, source_target_pairs={{0,16},{2,18},{4,20},{6,22},{8,24},{10,26},{12,28},{14,30},{16,0},... | collective-permute-start | bytes 221192 | tf_op jit(solution)/shard_map/ppermute | solution.py:543
  6.4 1.6 concatenate.69
  8.6 0.8 maximum_bitcast_fusion.1
  9.6 1.9 collective-permute-start.3
  11.5 4.3 %collective-permute-done.1 = bf16[1,48,896]{2,1,0:T(8,128)(2,1)S(1)} collective-permute-done((bf16[1,48,896]{2,1,0:T(8,128)(2,1)S(1)}, bf16[1,48,896]{2,1,0:T(8,128)(2,1)S(1)}, u32[]{:S(2)}, u32[]{:S(2)}) %collective-permute-start.1) | collective-permute-done | bytes 86048 | tf_op jit(solution)/shard_map/ppermute | solution.py:543
  15.8 1.7 collective-permute-start.4
  17.5 0.9 maximum_bitcast_fusion
  19.9 3.3 %collective-permute-done.4 = bf16[2,48,896]{2,1,0:T(8,128)(2,1)S(1)} collective-permute-done((bf16[2,48,896]{2,1,0:T(8,128)(2,1)S(1)}, bf16[2,48,896]{2,1,0:T(8,128)(2,1)S(1)}, u32[]{:S(2)}, u32[]{:S(2)}) %collective-permute-start.4) | collective-permute-done | bytes 172064 | tf_op jit(solution)/shard_map/ppermute | solution.py:543
  23.3 4.9 %collective-permute-done.2 = bf16[1,48,1920]{2,1,0:T(8,128)(2,1)S(1)} collective-permute-done((bf16[1,48,1920]{2,1,0:T(8,128)(2,1)S(1)}, bf16[1,48,1920]{2,1,0:T(8,128)(2,1)S(1)}, u32[]{:S(2)}, u32[]{:S(2)}) %collective-permute-start.2) | collective-permute-done | bytes 184352 | tf_op jit(solution)/shard_map/ppermute | solution.py:543
  28.4 1.6 collective-permute-start.10
  29.9 1.5 collective-permute-start.7
  31.4 4.6 %collective-permute-done.5 = bf16[2,48,1920]{2,1,0:T(8,128)(2,1)S(1)} collective-permute-done((bf16[2,48,1920]{2,1,0:T(8,128)(2,1)S(1)}, bf16[2,48,1920]{2,1,0:T(8,128)(2,1)S(1)}, u32[]{:S(2)}, u32[]{:S(2)}) %collective-permute-start.5) | collective-permute-done | bytes 368672 | tf_op jit(solution)/shard_map/ppermute | solution.py:543
  36.0 0.9 pad_maximum_fusion.2
  37.0 1.5 collective-permute-start.6
  38.7 2.1 prepare.1
  40.9 1.6 collective-permute-start.9
  42.4 1.0 pad_maximum_fusion.4
  44.1 6.7 %collective-permute-done.11 = bf16[2,48,1536]{2,1,0:T(8,128)(2,1)} collective-permute-done((bf16[2,48,1536]{2,1,0:T(8,128)(2,1)S(1)}, bf16[2,48,1536]{2,1,0:T(8,128)(2,1)}, u32[]{:S(2)}, u32[]{:S(2)}) %collective-permute-start.11) | collective-permute-done | bytes 294944 | tf_op jit(solution)/shard_map/ppermute | solution.py:543
  50.8 1.0 pad_maximum_fusion.5
  52.0 1.3 collective-permute-start.13
  53.3 1.5 collective-permute-start.12
  54.8 1.3 pad_maximum_fusion
  56.1 5.7 %collective-permute-done.8 = bf16[8,48,768]{2,1,0:T(8,128)(2,1)S(1)} collective-permute-done((bf16[8,48,768]{2,1,0:T(8,128)(2,1)S(1)}, bf16[8,48,768]{2,1,0:T(8,128)(2,1)S(1)}, u32[]{:S(2)}, u32[]{:S(2)}) %collective-permute-start.8) | collective-permute-done | bytes 589856 | tf_op jit(solution)/shard_map/ppermute | solution.py:543
  61.8 1.5 collective-permute-start.18
  63.3 2.4 %collective-permute-done.12 = bf16[4,48,1536]{2,1,0:T(8,128)(2,1)S(1)} collective-permute-done((bf16[4,48,1536]{2,1,0:T(8,128)(2,1)S(1)}, bf16[4,48,1536]{2,1,0:T(8,128)(2,1)S(1)}, u32[]{:S(2)}, u32[]{:S(2)}) %collective-permute-start.12) | collective-permute-done | bytes 589856 | tf_op jit(solution)/shard_map/ppermute | solution.py:543
  65.8 1.8 collective-permute-done.13
  67.7 1.2 collective-permute-start.21
  69.5 1.6 collective-permute-done.16
  71.2 1.7 collective-permute-done.15
  72.9 13.1 %attend.1 = (bf16[512,768]{1,0:T(8,128)(2,1)S(1)}, bf16[512,768]{1,0:T(8,128)(2,1)S(1)}, bf16[512,768]{1,0:T(8,128)(2,1)S(1)}, bf16[512,384]{1,0:T(8,128)(2,1)S(...) custom-call(s32[6]{0:T(128)S(1)} %pad_add_fusion.info, ...), custom_call_target="tpu_custom_call" | custom-call | bytes 1024 | tf_op jit(solution)/shard_map/attend/pallas_call | solution.py:514
  86.2 5.0 %collective-permute-done.18 = bf16[8,48,1920]{2,1,0:T(8,128)(2,1)S(1)} collective-permute-done((bf16[8,48,1920]{2,1,0:T(8,128)(2,1)S(1)}, bf16[8,48,1920]{2,1,0:T(8,128)(2,1)S(1)}, u32[]{:S(2)}, u32[]{:S(2)}) %collective-permute-start.18) | collective-permute-done | bytes 1474592 | tf_op jit(solution)/shard_map/ppermute | solution.py:543
  91.6 1.2 collective-permute-done.21
  93.5 0.9 collective-permute-done.20
  94.4 6.7 %up.1 = (bf16[512,1536]{1,0:T(8,128)(2,1)S(1)}, bf16[512,1536]{1,0:T(8,128)(2,1)}, bf16[512,3072]{1,0:T(8,128)(2,1)S(1)}, bf16[2,768,1536]{2,1,0:T(8,128)(2,1)S(1)}) custom-call(f32[16,768]{1,0:T(8,128)S(1)} %get-tuple-element.141.vec, bf16[768,512]{1,0:T(8,128)(2,1)S(1)} %get-tuple-element.156.first_p.left, bf16[384,1920]{1,0:T(8,128)(2,1)S(1)} %bitcast.96, ...), custom_call_target="tpu_custom_call" | custom-call | bytes 1024 | tf_op jit(solution)/shard_map/up/pallas_call | solution.py:514
  101.1 1.6 copy-done.23
  102.9 10.3 %ramp.1 = (bf16[512,768]{1,0:T(8,128)(2,1)S(1)}, f32[8,768]{1,0:T(8,128)}, bf16[768,512]{1,0:T(8,128)(2,1)}, f32[512,768]{1,0:T(8,128)S(1)}, f32[8,768]{1,0:T(8,128)S(1)}, /*index=5*/bf16[2,768,1536]{2,1,0:T(8,128)(2,1)S(1)}) custom-call(s32[6]{0:T(128)S(1)} %pad_add_fusion.info, f32[3]{0:T(128)S(1)} %convert_element_type.23.class_bias, ...), custom_call_target="tpu_custom_call" | custom-call | flops 17250000896 | bytes 1024 | tf_op jit(solution)/shard_map/ramp/pallas_call | solution.py:514
  113.8 1.2 copy-done.26
  115.0 1.9 copy-done.24
  116.9 3.9 %hidden.1 = (bf16[512,1536]{1,0:T(8,128)(2,1)S(1)}, bf16[512,1536]{1,0:T(8,128)(2,1)}) custom-call(bf16[768,512]{1,0:T(8,128)(2,1)} %get-tuple-element.149.feed_r.left_in, bf16[512,3072]{1,0:T(8,128)(2,1)S(1)} %copy-done.24, bf16[2,768,1536]{2,1,0:T(8,128)(2,1)S(1)} %get-tuple-element.151.w), custom_call_target="tpu_custom_call" | custom-call | flops 460000002048 | bytes 1024 | tf_op jit(solution)/shard_map/hidden/pallas_call | solution.py:514
  121.2 14.4 %down_grad.1 = (bf16[384,1920]{1,0:T(8,128)(2,1)S(1)}, bf16[384,1920]{1,0:T(8,128)(2,1)S(1)}, f32[2,3]{1,0:T(2,128)}) custom-call(s32[6]{0:T(128)S(1)} %pad_add_fusion.info, f32[8,768]{1,0:T(8,128)} %get-tuple-element.154.ramp, f32[8,768]{1,0:T(8,128)} %collective-permute-done.27.ramp_other, bf16[768,512]{1,0:T(8,128)(2,1)} %get-tuple-element.149.feed_r.left_in, ...), custom_call_target="tpu_custom_call" | custom-call | flops 460000002048 | bytes 1024 | tf_op jit(solution)/shard_map/down_grad/pallas_call | solution.py:514
  135.7 4.3 %up_grad.1 = (bf16[384,1536]{1,0:T(8,128)(2,1)S(1)}, bf16[384,1536]{1,0:T(8,128)(2,1)S(1)}, f32[1,1536]{1,0:T(1,128)S(1)}) custom-call(bf16[768,512]{1,0:T(8,128)(2,1)S(1)} %get-tuple-element.156.first_p.left, bf16[768,512]{1,0:T(8,128)(2,1)S(1)} %collective-permute-done.25.left_other, bf16[512,1536]{1,0:T(8,128)(2,1)S(1)} %get-tuple-element.152.right.delta, ...), custom_call_target="tpu_custom_call" | custom-call | bytes 1024 | tf_op jit(solution)/shard_map/up_grad/pallas_call | solution.py:514
  140.2 1.5 collective-permute-start.35
  142.3 7.2 %branch.1 = (f32[512,768]{1,0:T(8,128)S(1)}, bf16[512,768]{1,0:T(8,128)(2,1)S(1)}, bf16[768,512]{1,0:T(8,128)(2,1)S(1)}, f32[16,768]{1,0:T(8,128)S(1)}) custom-call(s32[6]{0:T(128)S(1)} %copy-done.22, f32[16,768]{1,0:T(8,128)S(1)} %copy-done.20, f32[8,768]{1,0:T(8,128)S(1)} %get-tuple-element.160.sums_in, ...), custom_call_target="tpu_custom_call" | custom-call | bytes 1024 | tf_op jit(solution)/shard_map/branch/pallas_call | solution.py:514
  149.5 6.8 %back.1 = (bf16[512,1152]{1,0:T(8,128)(2,1)S(1)}, bf16[512,1152]{1,0:T(8,128)(2,1)S(1)}) custom-call(bf16[512,768]{1,0:T(8,128)(2,1)S(1)} %get-tuple-element.171.q, bf16[512,768]{1,0:T(8,128)(2,1)S(1)} %get-tuple-element.172.k, bf16[512,768]{1,0:T(8,128)(2,1)S(1)} %get-tuple-element.173.v, bf16[512,384]{1,0:T(8,128)(2,1)S(1)} %get-tuple-element.174.att_own.att, ...), custom_call_target="tpu_custom_call" | custom-call | bytes 1024 | tf_op jit(solution)/shard_map/back/pallas_call | solution.py:514
  157.0 4.3 %input.1.grad_own = bf16[512,768]{1,0:T(8,128)(2,1)S(1)} custom-call(s32[6]{0:T(128)S(1)} %copy-done.22, bf16[512,1152]{1,0:T(8,128)(2,1)S(1)} %get-tuple-element.180.own.delta, bf16[512,1152]{1,0:T(8,128)(2,1)S(1)} %get-tuple-element.181.other, f32[512,768]{1,0:T(8,128)S(1)} %get-tuple-element.183.total, bf16[384,768]{1,0:T(8,128)(2,1)S(1)} %bitcast.99, ...), custom_call_target="tpu_custom_call" | custom-call | bytes 1024 | tf_op jit(solution)/shard_map/input/pallas_call | solution.py:514
  161.3 8.4 %collective-permute-done.33.refs_1_ = bf16[8,48,1536]{2,1,0:T(8,128)(2,1)S(1)} collective-permute-done((bf16[8,48,1536]{2,1,0:T(8,128)(2,1)S(1)}, bf16[8,48,1536]{2,1,0:T(8,128)(2,1)S(1)}, u32[]{:S(2)}, u32[]{:S(2)}) %collective-permute-start.33) | collective-permute-done | bytes 1179680 | tf_op jit(solution)/shard_map/ppermute | solution.py:543
  169.9 1.0 out_grad.1
  170.9 2.8 %input_grad.1 = (bf16[384,768]{1,0:T(8,128)(2,1)S(1)}, bf16[384,768]{1,0:T(8,128)(2,1)S(1)}, bf16[384,896]{1,0:T(8,128)(2,1)S(1)}, bf16[384,896]{1,0:T(8,128)(2,1)S(1)}) custom-call(s32[6]{0:T(128)S(1)} %copy-done.22, f32[16,768]{1,0:T(8,128)S(1)} %get-tuple-element.165.sums_in, f32[16,768]{1,0:T(8,128)S(1)} %collective-permute-done.30.sums_other, ...), custom_call_target="tpu_custom_call" | custom-call | bytes 1024 | tf_op jit(solution)/shard_map/input_grad/pallas_call | solution.py:514
  175.0 1.5 collective-permute-start.41
  176.5 1.0 collective-permute-start.36
  177.5 1.0 collective-permute-start.43
  178.5 11.8 %collective-permute-done.37.refs_1_ = bf16[8,48,896]{2,1,0:T(8,128)(2,1)S(1)} collective-permute-done((bf16[8,48,896]{2,1,0:T(8,128)(2,1)S(1)}, bf16[8,48,896]{2,1,0:T(8,128)(2,1)S(1)}, u32[]{:S(2)}, u32[]{:S(2)}) %collective-permute-start.37) | collective-permute-done | bytes 688160 | tf_op jit(solution)/shard_map/ppermute | solution.py:543
  191.0 1.8 collective-permute-done.36.refs_1_
  192.8 1.6 collective-permute-start.39
  194.5 2.6 %collective-permute-start.42 = (bf16[2,48,1920]{2,1,0:T(8,128)(2,1)S(1)}, bf16[2,48,1920]{2,1,0:T(8,128)(2,1)S(1)}, u32[]{:S(2)}, u32[]{:S(2)}) collective-permute-start(bf16[2,48,1920]{2,1,0:T(8,128)(2,1)S(1)} %get-tuple-element.211), channel_id=1, source_target_pairs={{0,16},{2,18},{4,20},{6,22},{8,24},{10,26},{12,28},{14,30},{16,0},... | collective-permute-start | bytes 1105928 | tf_op jit(solution)/shard_map/ppermute | solution.py:543
  197.1 2.5 %arrange.1 = (bf16[2,512,768]{2,1,0:T(8,128)(2,1)}, bf16[2,512,768]{2,1,0:T(8,128)(2,1)}) custom-call(s32[6]{0:T(128)S(1)} %copy-done.22, bf16[512,768]{1,0:T(8,128)(2,1)S(1)} %get-tuple-element.177.block_own, bf16[512,768]{1,0:T(8,128)(2,1)S(1)} %collective-permute-done.31.block_other, bf16[512,768]{1,0:T(8,128)(2,1)S(1)} %input.1.grad_own, ...), custom_call_target="tpu_custom_call" | custom-call | bytes 1024 | tf_op jit(solution)/shard_map/arrange/pallas_call | solution.py:514
  199.6 11.4 %collective-permute-done.40.refs_3_ = bf16[4,48,896]{2,1,0:T(8,128)(2,1)S(1)} collective-permute-done((bf16[4,48,896]{2,1,0:T(8,128)(2,1)S(1)}, bf16[4,48,896]{2,1,0:T(8,128)(2,1)S(1)}, u32[]{:S(2)}, u32[]{:S(2)}) %collective-permute-start.40) | collective-permute-done | bytes 344096 | tf_op jit(solution)/shard_map/ppermute | solution.py:543
  211.8 1.5 collective-permute-start.44
  213.4 1.6 collective-permute-start.46
  214.9 10.3 %collective-permute-done.44.refs_1_ = bf16[2,48,1536]{2,1,0:T(8,128)(2,1)S(1)} collective-permute-done((bf16[2,48,1536]{2,1,0:T(8,128)(2,1)S(1)}, bf16[2,48,1536]{2,1,0:T(8,128)(2,1)S(1)}, u32[]{:S(2)}, u32[]{:S(2)}) %collective-permute-start.44) | collective-permute-done | bytes 294944 | tf_op jit(solution)/shard_map/ppermute | solution.py:543
  225.3 3.6 %collective-permute-start.47 = (bf16[1,48,1536]{2,1,0:T(8,128)(2,1)S(1)}, bf16[1,48,1536]{2,1,0:T(8,128)(2,1)S(1)}, u32[]{:S(2)}, u32[]{:S(2)}) collective-permute-start(bf16[1,48,1536]{2,1,0:T(8,128)(2,1)S(1)} %get-tuple-element.225), channel_id=1, source_target_pairs={{0,16},{2,18},{4,20},{6,22},{8,24},{10,26},{12,28},{14,30},{16,0},... | collective-permute-start | bytes 442376 | tf_op jit(solution)/shard_map/ppermute | solution.py:543
  229.2 8.0 %collective-permute-done.47 = bf16[1,48,1536]{2,1,0:T(8,128)(2,1)S(1)} collective-permute-done((bf16[1,48,1536]{2,1,0:T(8,128)(2,1)S(1)}, bf16[1,48,1536]{2,1,0:T(8,128)(2,1)S(1)}, u32[]{:S(2)}, u32[]{:S(2)}) %collective-permute-start.47) | collective-permute-done | bytes 147488 | tf_op jit(solution)/shard_map/ppermute | solution.py:543
  239.9 0.8 finish.1
  (162 shorter events, 16.2 us)
Async XLA Ops:
  1.5 8.0 %collective-permute-start = (bf16[1,48,768]{2,1,0:T(8,128)(2,1)S(1)}, bf16[1,48,768]{2,1,0:T(8,128)(2,1)S(1)}, u32[]{:S(2)}, u32[]{:S(2)}) collective-permute-start(bf16[1,48,768]{2,1,0:T(8,128)(2,1)S(1)} %fusion.7), channel_id=1, source_target_pairs={{0,16},{2,18},{4,20},{6,22},{8,24},{10,26},{12,28},{14,30},{16,0},... | collective-permute-start | bytes 221192 | tf_op jit(solution)/shard_map/ppermute | solution.py:543
  9.4 6.3 %collective-permute-start.1 = (bf16[1,48,896]{2,1,0:T(8,128)(2,1)S(1)}, bf16[1,48,896]{2,1,0:T(8,128)(2,1)S(1)}, u32[]{:S(2)}, u32[]{:S(2)}) collective-permute-start(bf16[1,48,896]{2,1,0:T(8,128)(2,1)S(1)} %maximum_bitcast_fusion.1), channel_id=1, source_target_pairs={{0,16},{2,18},{4,20},{6,22},{8,24},{10,26},{12,28},{14,30},{16,0},... | collective-permute-start | bytes 258056 | tf_op jit(solution)/shard_map/ppermute | solution.py:543
  9.5 18.8 %copy-start.32 = (bf16[1536,48]{0,1:T(8,128)(2,1)S(1)}, bf16[1536,48]{0,1:T(8,128)(2,1)}, u32[]{:S(2)}) copy-start(bf16[1536,48]{0,1:T(8,128)(2,1)} %param.32) | copy-start | bytes 442372
  9.6 9.6 %collective-permute-start.3 = (bf16[2,48,768]{2,1,0:T(8,128)(2,1)S(1)}, bf16[2,48,768]{2,1,0:T(8,128)(2,1)S(1)}, u32[]{:S(2)}, u32[]{:S(2)}) collective-permute-start(bf16[2,48,768]{2,1,0:T(8,128)(2,1)S(1)} %pad_maximum_fusion.11), channel_id=1, source_target_pairs={{0,8},{2,10},{4,12},{6,14},{8,0},{10,2},{12,4},{14,6},{16,24},{18,... | collective-permute-start | bytes 442376 | tf_op jit(solution)/shard_map/ppermute | solution.py:543
  15.8 7.5 %collective-permute-start.4 = (bf16[2,48,896]{2,1,0:T(8,128)(2,1)S(1)}, bf16[2,48,896]{2,1,0:T(8,128)(2,1)S(1)}, u32[]{:S(2)}, u32[]{:S(2)}) collective-permute-start(bf16[2,48,896]{2,1,0:T(8,128)(2,1)S(1)} %pad_maximum_fusion.10), channel_id=1, source_target_pairs={{0,8},{2,10},{4,12},{6,14},{8,0},{10,2},{12,4},{14,6},{16,24},{18,... | collective-permute-start | bytes 516104 | tf_op jit(solution)/shard_map/ppermute | solution.py:543
  18.4 9.8 %collective-permute-start.2 = (bf16[1,48,1920]{2,1,0:T(8,128)(2,1)S(1)}, bf16[1,48,1920]{2,1,0:T(8,128)(2,1)S(1)}, u32[]{:S(2)}, u32[]{:S(2)}) collective-permute-start(bf16[1,48,1920]{2,1,0:T(8,128)(2,1)S(1)} %maximum_bitcast_fusion), channel_id=1, source_target_pairs={{0,16},{2,18},{4,20},{6,22},{8,24},{10,26},{12,28},{14,30},{16,0},... | collective-permute-start | bytes 552968 | tf_op jit(solution)/shard_map/ppermute | solution.py:543
  23.3 15.3 %copy-start.33 = (s32[2,1]{0,1:T(1,128)S(1)}, s32[2,1]{0,1:T(1,128)}, u32[]{:S(2)}) copy-start(s32[2,1]{0,1:T(1,128)} %param.22) | copy-start | bytes 28
  23.3 15.3 %copy-start.34 = (s32[2,1]{0,1:T(1,128)S(1)}, s32[2,1]{0,1:T(1,128)}, u32[]{:S(2)}) copy-start(s32[2,1]{0,1:T(1,128)} %param.21) | copy-start | bytes 28
  23.3 15.4 %copy-start.2 = (bf16[2,1,512,768]{3,2,1,0:T(8,128)(2,1)S(1)}, bf16[2,1,512,768]{3,2,1,0:T(8,128)(2,1)}, u32[]{:S(2)}) copy-start(bf16[2,1,512,768]{3,2,1,0:T(8,128)(2,1)} %param.20) | copy-start | bytes 4718596
  28.3 7.8 %collective-permute-start.5 = (bf16[2,48,1920]{2,1,0:T(8,128)(2,1)S(1)}, bf16[2,48,1920]{2,1,0:T(8,128)(2,1)S(1)}, u32[]{:S(2)}, u32[]{:S(2)}) collective-permute-start(bf16[2,48,1920]{2,1,0:T(8,128)(2,1)S(1)} %pad_maximum_fusion.6), channel_id=1, source_target_pairs={{0,8},{2,10},{4,12},{6,14},{8,0},{10,2},{12,4},{14,6},{16,24},{18,... | collective-permute-start | bytes 1105928 | tf_op jit(solution)/shard_map/ppermute | solution.py:543
  28.4 10.1 %collective-permute-start.10 = (bf16[1,48,1536]{2,1,0:T(8,128)(2,1)S(1)}, bf16[1,48,1536]{2,1,0:T(8,128)(2,1)S(1)}, u32[]{:S(2)}, u32[]{:S(2)}) collective-permute-start(bf16[1,48,1536]{2,1,0:T(8,128)(2,1)S(1)} %bitcast.125), channel_id=1, source_target_pairs={{0,2},{2,0},{4,6},{6,4},{8,10},{10,8},{12,14},{14,12},{16,18},{18,... | collective-permute-start | bytes 442376 | tf_op jit(solution)/shard_map/ppermute | solution.py:543
  29.9 12.5 %collective-permute-start.7 = (bf16[4,48,768]{2,1,0:T(8,128)(2,1)}, bf16[4,48,768]{2,1,0:T(8,128)(2,1)}, u32[]{:S(2)}, u32[]{:S(2)}) collective-permute-start(bf16[4,48,768]{2,1,0:T(8,128)(2,1)} %pad_maximum_fusion.8), channel_id=1, source_target_pairs={{0,4},{2,6},{4,0},{6,2},{8,12},{10,14},{12,8},{14,10},{16,20},{18,... | collective-permute-start | bytes 884744 | tf_op jit(solution)/shard_map/ppermute | solution.py:543
  37.0 17.8 %collective-permute-start.6 = (bf16[4,48,1920]{2,1,0:T(8,128)(2,1)}, bf16[4,48,1920]{2,1,0:T(8,128)(2,1)}, u32[]{:S(2)}, u32[]{:S(2)}) collective-permute-start(bf16[4,48,1920]{2,1,0:T(8,128)(2,1)} %pad_maximum_fusion.2), channel_id=1, source_target_pairs={{0,4},{2,6},{4,0},{6,2},{8,12},{10,14},{12,8},{14,10},{16,20},{18,... | collective-permute-start | bytes 2211848 | tf_op jit(solution)/shard_map/ppermute | solution.py:543
  38.5 12.3 %collective-permute-start.11 = (bf16[2,48,1536]{2,1,0:T(8,128)(2,1)S(1)}, bf16[2,48,1536]{2,1,0:T(8,128)(2,1)}, u32[]{:S(2)}, u32[]{:S(2)}) collective-permute-start(bf16[2,48,1536]{2,1,0:T(8,128)(2,1)S(1)} %pad_maximum_fusion.9), channel_id=1, source_target_pairs={{0,16},{2,18},{4,20},{6,22},{8,24},{10,26},{12,28},{14,30},{16,0},... | collective-permute-start | bytes 884744 | tf_op jit(solution)/shard_map/ppermute | solution.py:543
  38.7 82.5 %copy-start.21 = (s32[6]{0:T(128)}, s32[6]{0:T(128)S(1)}, u32[]{:S(2)}) copy-start(s32[6]{0:T(128)S(1)} %pad_add_fusion.info) | copy-start | bytes 76
  40.9 11.1 %collective-permute-start.9 = (bf16[4,48,896]{2,1,0:T(8,128)(2,1)S(1)}, bf16[4,48,896]{2,1,0:T(8,128)(2,1)S(1)}, u32[]{:S(2)}, u32[]{:S(2)}) collective-permute-start(bf16[4,48,896]{2,1,0:T(8,128)(2,1)S(1)} %pad_maximum_fusion.7), channel_id=1, source_target_pairs={{0,2},{2,0},{4,6},{6,4},{8,10},{10,8},{12,14},{14,12},{16,18},{18,... | collective-permute-start | bytes 1032200 | tf_op jit(solution)/shard_map/ppermute | solution.py:543
  43.5 29.5 %copy-start.9 = (bf16[8,48,768]{2,1,0:T(8,128)(2,1)}, bf16[8,48,768]{2,1,0:T(8,128)(2,1)S(1)}, u32[]{:S(2)}) copy-start(bf16[8,48,768]{2,1,0:T(8,128)(2,1)S(1)} %pad_maximum_fusion.4) | copy-start | bytes 1769476
  43.5 18.3 %collective-permute-start.8 = (bf16[8,48,768]{2,1,0:T(8,128)(2,1)S(1)}, bf16[8,48,768]{2,1,0:T(8,128)(2,1)S(1)}, u32[]{:S(2)}, u32[]{:S(2)}) collective-permute-start(bf16[8,48,768]{2,1,0:T(8,128)(2,1)S(1)} %pad_maximum_fusion.4), channel_id=1, source_target_pairs={{0,2},{2,0},{4,6},{6,4},{8,10},{10,8},{12,14},{14,12},{16,18},{18,... | collective-permute-start | bytes 1769480 | tf_op jit(solution)/shard_map/ppermute | solution.py:543
  52.0 15.7 %collective-permute-start.13 = (bf16[8,48,896]{2,1,0:T(8,128)(2,1)S(1)}, bf16[8,48,896]{2,1,0:T(8,128)(2,1)S(1)}, u32[]{:S(2)}, u32[]{:S(2)}) collective-permute-start(bf16[8,48,896]{2,1,0:T(8,128)(2,1)S(1)} %pad_maximum_fusion.3), channel_id=1, source_target_pairs={{0,4},{2,6},{4,0},{6,2},{8,12},{10,14},{12,8},{14,10},{16,20},{18,... | collective-permute-start | bytes 2064392 | tf_op jit(solution)/shard_map/ppermute | solution.py:543
  53.3 12.4 %collective-permute-start.12 = (bf16[4,48,1536]{2,1,0:T(8,128)(2,1)S(1)}, bf16[4,48,1536]{2,1,0:T(8,128)(2,1)S(1)}, u32[]{:S(2)}, u32[]{:S(2)}) collective-permute-start(bf16[4,48,1536]{2,1,0:T(8,128)(2,1)S(1)} %pad_maximum_fusion.5), channel_id=1, source_target_pairs={{0,8},{2,10},{4,12},{6,14},{8,0},{10,2},{12,4},{14,6},{16,24},{18,... | collective-permute-start | bytes 1769480 | tf_op jit(solution)/shard_map/ppermute | solution.py:543
  61.8 24.3 %copy-start.11 = (bf16[8,48,768]{2,1,0:T(8,128)(2,1)}, bf16[8,48,768]{2,1,0:T(8,128)(2,1)S(1)}, u32[]{:S(2)}) copy-start(bf16[8,48,768]{2,1,0:T(8,128)(2,1)S(1)} %collective-permute-done.8) | copy-start | bytes 1769476
  61.8 29.3 %collective-permute-start.18 = (bf16[8,48,1920]{2,1,0:T(8,128)(2,1)S(1)}, bf16[8,48,1920]{2,1,0:T(8,128)(2,1)S(1)}, u32[]{:S(2)}, u32[]{:S(2)}) collective-permute-start(bf16[8,48,1920]{2,1,0:T(8,128)(2,1)S(1)} %pad_maximum_fusion), channel_id=1, source_target_pairs={{0,2},{2,0},{4,6},{6,4},{8,10},{10,8},{12,14},{14,12},{16,18},{18,... | collective-permute-start | bytes 4423688 | tf_op jit(solution)/shard_map/ppermute | solution.py:543
  63.3 6.1 %collective-permute-start.14 = (bf16[8,48,768]{2,1,0:T(8,128)(2,1)S(1)}, bf16[8,48,768]{2,1,0:T(8,128)(2,1)S(1)}, u32[]{:S(2)}, u32[]{:S(2)}) collective-permute-start(bf16[8,48,768]{2,1,0:T(8,128)(2,1)S(1)} %pad_maximum_fusion.4), channel_id=1, source_target_pairs={{0,1},{1,0},{2,3},{3,2},{4,5},{5,4},{6,7},{7,6},{8,9},{9,8},{10,11... | collective-permute-start | bytes 1769480 | tf_op jit(solution)/shard_map/ppermute | solution.py:547
  67.7 18.4 %copy-start.3 = (bf16[8,48,896]{2,1,0:T(8,128)(2,1)}, bf16[8,48,896]{2,1,0:T(8,128)(2,1)S(1)}, u32[]{:S(2)}) copy-start(bf16[8,48,896]{2,1,0:T(8,128)(2,1)S(1)} %collective-permute-done.13) | copy-start | bytes 2064388
  67.7 25.2 %collective-permute-start.21 = (bf16[8,48,1536]{2,1,0:T(8,128)(2,1)S(1)}, bf16[8,48,1536]{2,1,0:T(8,128)(2,1)S(1)}, u32[]{:S(2)}, u32[]{:S(2)}) collective-permute-start(bf16[8,48,1536]{2,1,0:T(8,128)(2,1)S(1)} %pad_maximum_fusion.1), channel_id=1, source_target_pairs={{0,4},{2,6},{4,0},{6,2},{8,12},{10,14},{12,8},{14,10},{16,20},{18,... | collective-permute-start | bytes 3538952 | tf_op jit(solution)/shard_map/ppermute | solution.py:543
  68.9 2.1 collective-permute-start.16
  68.9 4.0 %collective-permute-start.17 = (bf16[8,48,896]{2,1,0:T(8,128)(2,1)S(1)}, bf16[8,48,896]{2,1,0:T(8,128)(2,1)S(1)}, u32[]{:S(2)}, u32[]{:S(2)}) collective-permute-start(bf16[8,48,896]{2,1,0:T(8,128)(2,1)S(1)} %collective-permute-done.13), channel_id=1, source_target_pairs={{0,1},{1,0},{2,3},{3,2},{4,5},{5,4},{6,7},{7,6},{8,9},{9,8},{10,11... | collective-permute-start | bytes 2064392 | tf_op jit(solution)/shard_map/ppermute | solution.py:547
  69.4 16.7 %copy-start.13 = (bf16[8,48,768]{2,1,0:T(8,128)(2,1)}, bf16[8,48,768]{2,1,0:T(8,128)(2,1)S(1)}, u32[]{:S(2)}) copy-start(bf16[8,48,768]{2,1,0:T(8,128)(2,1)S(1)} %collective-permute-done.14) | copy-start | bytes 1769476
  69.4 3.5 %collective-permute-start.15 = (bf16[8,48,768]{2,1,0:T(8,128)(2,1)S(1)}, bf16[8,48,768]{2,1,0:T(8,128)(2,1)S(1)}, u32[]{:S(2)}, u32[]{:S(2)}) collective-permute-start(bf16[8,48,768]{2,1,0:T(8,128)(2,1)S(1)} %collective-permute-done.8), channel_id=1, source_target_pairs={{0,1},{1,0},{2,3},{3,2},{4,5},{5,4},{6,7},{7,6},{8,9},{9,8},{10,11... | collective-permute-start | bytes 1769480 | tf_op jit(solution)/shard_map/ppermute | solution.py:547
  71.1 15.0 %copy-start.5 = (bf16[8,48,896]{2,1,0:T(8,128)(2,1)}, bf16[8,48,896]{2,1,0:T(8,128)(2,1)S(1)}, u32[]{:S(2)}) copy-start(bf16[8,48,896]{2,1,0:T(8,128)(2,1)S(1)} %collective-permute-done.16) | copy-start | bytes 2064388
  71.1 22.3 %collective-permute-start.19 = (bf16[8,48,1920]{2,1,0:T(8,128)(2,1)S(1)}, bf16[8,48,1920]{2,1,0:T(8,128)(2,1)S(1)}, u32[]{:S(2)}, u32[]{:S(2)}) collective-permute-start(bf16[8,48,1920]{2,1,0:T(8,128)(2,1)S(1)} %pad_maximum_fusion), channel_id=1, source_target_pairs={{0,1},{1,0},{2,3},{3,2},{4,5},{5,4},{6,7},{7,6},{8,9},{9,8},{10,11... | collective-permute-start | bytes 4423688 | tf_op jit(solution)/shard_map/ppermute | solution.py:547
  72.9 13.2 %copy-start.15 = (bf16[8,48,768]{2,1,0:T(8,128)(2,1)}, bf16[8,48,768]{2,1,0:T(8,128)(2,1)S(1)}, u32[]{:S(2)}) copy-start(bf16[8,48,768]{2,1,0:T(8,128)(2,1)S(1)} %collective-permute-done.15) | copy-start | bytes 1769476
  72.9 13.2 %copy-start.7 = (bf16[8,48,896]{2,1,0:T(8,128)(2,1)}, bf16[8,48,896]{2,1,0:T(8,128)(2,1)S(1)}, u32[]{:S(2)}) copy-start(bf16[8,48,896]{2,1,0:T(8,128)(2,1)S(1)} %collective-permute-done.17) | copy-start | bytes 2064388
  72.9 20.0 %copy-start.35 = (bf16[3]{0:T(256)(128)(2,1)S(1)}, bf16[3]{0:T(256)(128)(2,1)}, u32[]{:S(2)}) copy-start(bf16[3]{0:T(256)(128)(2,1)} %param.39) | copy-start | bytes 22
  86.1 16.7 %copy-start.19 = (f32[16,768]{1,0:T(8,128)}, f32[16,768]{1,0:T(8,128)S(1)}, u32[]{:S(2)}) copy-start(f32[16,768]{1,0:T(8,128)S(1)} %get-tuple-element.141.vec) | copy-start | bytes 147460
  91.1 3.3 %collective-permute-start.20 = (bf16[8,48,1920]{2,1,0:T(8,128)(2,1)S(1)}, bf16[8,48,1920]{2,1,0:T(8,128)(2,1)S(1)}, u32[]{:S(2)}, u32[]{:S(2)}) collective-permute-start(bf16[8,48,1920]{2,1,0:T(8,128)(2,1)S(1)} %collective-permute-done.18), channel_id=1, source_target_pairs={{0,1},{1,0},{2,3},{3,2},{4,5},{5,4},{6,7},{7,6},{8,9},{9,8},{10,11... | collective-permute-start | bytes 4423688 | tf_op jit(solution)/shard_map/ppermute | solution.py:547
  91.1 11.7 %collective-permute-start.22 = (bf16[8,48,1536]{2,1,0:T(8,128)(2,1)S(1)}, bf16[8,48,1536]{2,1,0:T(8,128)(2,1)S(1)}, u32[]{:S(2)}, u32[]{:S(2)}) collective-permute-start(bf16[8,48,1536]{2,1,0:T(8,128)(2,1)S(1)} %pad_maximum_fusion.1), channel_id=1, source_target_pairs={{0,1},{1,0},{2,3},{3,2},{4,5},{5,4},{6,7},{7,6},{8,9},{9,8},{10,11... | collective-permute-start | bytes 3538952 | tf_op jit(solution)/shard_map/ppermute | solution.py:547
  92.9 10.0 %collective-permute-start.23 = (bf16[8,48,1536]{2,1,0:T(8,128)(2,1)S(1)}, bf16[8,48,1536]{2,1,0:T(8,128)(2,1)S(1)}, u32[]{:S(2)}, u32[]{:S(2)}) collective-permute-start(bf16[8,48,1536]{2,1,0:T(8,128)(2,1)S(1)} %collective-permute-done.21), channel_id=1, source_target_pairs={{0,1},{1,0},{2,3},{3,2},{4,5},{5,4},{6,7},{7,6},{8,9},{9,8},{10,11... | collective-permute-start | bytes 3538952 | tf_op jit(solution)/shard_map/ppermute | solution.py:547
  92.9 20.9 %collective-permute-start.25 = (bf16[768,512]{1,0:T(8,128)(2,1)S(1)}, bf16[768,512]{1,0:T(8,128)(2,1)S(1)}, u32[]{:S(2)}, u32[]{:S(2)}) collective-permute-start(bf16[768,512]{1,0:T(8,128)(2,1)S(1)} %get-tuple-element.156.first_p.left), channel_id=1, source_target_pairs={{0,1},{1,0},{2,3},{3,2},{4,5},{5,4},{6,7},{7,6},{8,9},{9,8},{10,11... | collective-permute-start | bytes 2359304 | tf_op jit(solution)/shard_map/ppermute | solution.py:547
  93.4 20.4 %collective-permute-start.26 = (bf16[512,384]{1,0:T(8,128)(2,1)S(1)}, bf16[512,384]{1,0:T(8,128)(2,1)S(1)}, u32[]{:S(2)}, u32[]{:S(2)}) collective-permute-start(bf16[512,384]{1,0:T(8,128)(2,1)S(1)} %get-tuple-element.148.att_other), channel_id=1, source_target_pairs={{0,1},{1,0},{2,3},{3,2},{4,5},{5,4},{6,7},{7,6},{8,9},{9,8},{10,11... | collective-permute-start | bytes 1179656 | tf_op jit(solution)/shard_map/ppermute | solution.py:547
  102.7 11.1 %collective-permute-start.24 = (bf16[512,1536]{1,0:T(8,128)(2,1)}, bf16[512,1536]{1,0:T(8,128)(2,1)S(1)}, u32[]{:S(2)}, u32[]{:S(2)}) collective-permute-start(bf16[512,1536]{1,0:T(8,128)(2,1)} %get-tuple-element.145.other_active), channel_id=1, source_target_pairs={{0,1},{1,0},{2,3},{3,2},{4,5},{5,4},{6,7},{7,6},{8,9},{9,8},{10,11... | collective-permute-start | bytes 4718600 | tf_op jit(solution)/shard_map/ppermute | solution.py:547
  113.2 8.0 %collective-permute-start.28 = (bf16[768,512]{1,0:T(8,128)(2,1)}, bf16[768,512]{1,0:T(8,128)(2,1)}, u32[]{:S(2)}, u32[]{:S(2)}) collective-permute-start(bf16[768,512]{1,0:T(8,128)(2,1)} %get-tuple-element.149.feed_r.left_in), channel_id=1, source_target_pairs={{0,1},{1,0},{2,3},{3,2},{4,5},{5,4},{6,7},{7,6},{8,9},{9,8},{10,11... | collective-permute-start | bytes 2359304 | tf_op jit(solution)/shard_map/ppermute | solution.py:547
  113.6 7.6 %collective-permute-start.27 = (f32[8,768]{1,0:T(8,128)}, f32[8,768]{1,0:T(8,128)}, u32[]{:S(2)}, u32[]{:S(2)}) collective-permute-start(f32[8,768]{1,0:T(8,128)} %get-tuple-element.154.ramp), channel_id=1, source_target_pairs={{0,1},{1,0},{2,3},{3,2},{4,5},{5,4},{6,7},{7,6},{8,9},{9,8},{10,11... | collective-permute-start | bytes 73736 | tf_op jit(solution)/shard_map/ppermute | solution.py:547
  120.8 15.0 %collective-permute-start.29 = (bf16[512,1536]{1,0:T(8,128)(2,1)}, bf16[512,1536]{1,0:T(8,128)(2,1)}, u32[]{:S(2)}, u32[]{:S(2)}) collective-permute-start(bf16[512,1536]{1,0:T(8,128)(2,1)} %get-tuple-element.157.other_delta), channel_id=1, source_target_pairs={{0,1},{1,0},{2,3},{3,2},{4,5},{5,4},{6,7},{7,6},{8,9},{9,8},{10,11... | collective-permute-start | bytes 4718600 | tf_op jit(solution)/shard_map/ppermute | solution.py:547
  140.0 9.4 %collective-permute-start.31 = (bf16[512,768]{1,0:T(8,128)(2,1)S(1)}, bf16[512,768]{1,0:T(8,128)(2,1)S(1)}, u32[]{:S(2)}, u32[]{:S(2)}) collective-permute-start(bf16[512,768]{1,0:T(8,128)(2,1)S(1)} %get-tuple-element.177.block_own), channel_id=1, source_target_pairs={{0,1},{1,0},{2,3},{3,2},{4,5},{5,4},{6,7},{7,6},{8,9},{9,8},{10,11... | collective-permute-start | bytes 2359304 | tf_op jit(solution)/shard_map/ppermute | solution.py:547
  140.2 34.6 %collective-permute-start.35 = (bf16[8,48,1920]{2,1,0:T(8,128)(2,1)S(1)}, bf16[8,48,1920]{2,1,0:T(8,128)(2,1)S(1)}, u32[]{:S(2)}, u32[]{:S(2)}) collective-permute-start(bf16[8,48,1920]{2,1,0:T(8,128)(2,1)S(1)} %bitcast.118), channel_id=1, source_target_pairs={{0,4},{2,6},{4,0},{6,2},{8,12},{10,14},{12,8},{14,10},{16,20},{18,... | collective-permute-start | bytes 4423688 | tf_op jit(solution)/shard_map/ppermute | solution.py:543
  141.8 28.0 %collective-permute-start.33 = (bf16[8,48,1536]{2,1,0:T(8,128)(2,1)S(1)}, bf16[8,48,1536]{2,1,0:T(8,128)(2,1)S(1)}, u32[]{:S(2)}, u32[]{:S(2)}) collective-permute-start(bf16[8,48,1536]{2,1,0:T(8,128)(2,1)S(1)} %bitcast.120), channel_id=1, source_target_pairs={{0,2},{2,0},{4,6},{6,4},{8,10},{10,8},{12,14},{14,12},{16,18},{18,... | collective-permute-start | bytes 3538952 | tf_op jit(solution)/shard_map/ppermute | solution.py:543
  156.3 14.6 %collective-permute-start.32 = (bf16[512,1152]{1,0:T(8,128)(2,1)S(1)}, bf16[512,1152]{1,0:T(8,128)(2,1)S(1)}, u32[]{:S(2)}, u32[]{:S(2)}) collective-permute-start(bf16[512,1152]{1,0:T(8,128)(2,1)S(1)} %get-tuple-element.181.other), channel_id=1, source_target_pairs={{0,1},{1,0},{2,3},{3,2},{4,5},{5,4},{6,7},{7,6},{8,9},{9,8},{10,11... | collective-permute-start | bytes 3538952 | tf_op jit(solution)/shard_map/ppermute | solution.py:547
  156.4 13.5 %collective-permute-start.34 = (bf16[768,512]{1,0:T(8,128)(2,1)S(1)}, bf16[768,512]{1,0:T(8,128)(2,1)S(1)}, u32[]{:S(2)}, u32[]{:S(2)}) collective-permute-start(bf16[768,512]{1,0:T(8,128)(2,1)S(1)} %get-tuple-element.187.branch_t), channel_id=1, source_target_pairs={{0,1},{1,0},{2,3},{3,2},{4,5},{5,4},{6,7},{7,6},{8,9},{9,8},{10,11... | collective-permute-start | bytes 2359304 | tf_op jit(solution)/shard_map/ppermute | solution.py:547
  156.9 13.0 %collective-permute-start.30 = (f32[16,768]{1,0:T(8,128)S(1)}, f32[16,768]{1,0:T(8,128)S(1)}, u32[]{:S(2)}, u32[]{:S(2)}) collective-permute-start(f32[16,768]{1,0:T(8,128)S(1)} %get-tuple-element.165.sums_in), channel_id=1, source_target_pairs={{0,1},{1,0},{2,3},{3,2},{4,5},{5,4},{6,7},{7,6},{8,9},{9,8},{10,11... | collective-permute-start | bytes 147464 | tf_op jit(solution)/shard_map/ppermute | solution.py:547
  173.7 16.6 %collective-permute-start.37 = (bf16[8,48,896]{2,1,0:T(8,128)(2,1)S(1)}, bf16[8,48,896]{2,1,0:T(8,128)(2,1)S(1)}, u32[]{:S(2)}, u32[]{:S(2)}) collective-permute-start(bf16[8,48,896]{2,1,0:T(8,128)(2,1)S(1)} %bitcast.123), channel_id=1, source_target_pairs={{0,2},{2,0},{4,6},{6,4},{8,10},{10,8},{12,14},{14,12},{16,18},{18,... | collective-permute-start | bytes 2064392 | tf_op jit(solution)/shard_map/ppermute | solution.py:543
  175.0 19.4 %collective-permute-start.41 = (bf16[4,48,1920]{2,1,0:T(8,128)(2,1)S(1)}, bf16[4,48,1920]{2,1,0:T(8,128)(2,1)S(1)}, u32[]{:S(2)}, u32[]{:S(2)}) collective-permute-start(bf16[4,48,1920]{2,1,0:T(8,128)(2,1)S(1)} %get-tuple-element.208), channel_id=1, source_target_pairs={{0,8},{2,10},{4,12},{6,14},{8,0},{10,2},{12,4},{14,6},{16,24},{18,... | collective-permute-start | bytes 2211848 | tf_op jit(solution)/shard_map/ppermute | solution.py:543
  176.5 16.3 %collective-permute-start.36 = (bf16[8,48,768]{2,1,0:T(8,128)(2,1)S(1)}, bf16[8,48,768]{2,1,0:T(8,128)(2,1)S(1)}, u32[]{:S(2)}, u32[]{:S(2)}) collective-permute-start(bf16[8,48,768]{2,1,0:T(8,128)(2,1)S(1)} %bitcast.124), channel_id=1, source_target_pairs={{0,4},{2,6},{4,0},{6,2},{8,12},{10,14},{12,8},{14,10},{16,20},{18,... | collective-permute-start | bytes 1769480 | tf_op jit(solution)/shard_map/ppermute | solution.py:543
  177.5 19.6 %collective-permute-start.38 = (bf16[512,768]{1,0:T(8,128)(2,1)S(1)}, bf16[512,768]{1,0:T(8,128)(2,1)S(1)}, u32[]{:S(2)}, u32[]{:S(2)}) collective-permute-start(bf16[512,768]{1,0:T(8,128)(2,1)S(1)} %input.1.grad_own), channel_id=1, source_target_pairs={{0,1},{1,0},{2,3},{3,2},{4,5},{5,4},{6,7},{7,6},{8,9},{9,8},{10,11... | collective-permute-start | bytes 2359304 | tf_op jit(solution)/shard_map/ppermute | solution.py:547
  177.5 34.2 %collective-permute-start.43 = (bf16[4,48,1536]{2,1,0:T(8,128)(2,1)S(1)}, bf16[4,48,1536]{2,1,0:T(8,128)(2,1)S(1)}, u32[]{:S(2)}, u32[]{:S(2)}) collective-permute-start(bf16[4,48,1536]{2,1,0:T(8,128)(2,1)S(1)} %get-tuple-element.214), channel_id=1, source_target_pairs={{0,4},{2,6},{4,0},{6,2},{8,12},{10,14},{12,8},{14,10},{16,20},{18,... | collective-permute-start | bytes 1769480 | tf_op jit(solution)/shard_map/ppermute | solution.py:543
  190.4 20.6 %collective-permute-start.40 = (bf16[4,48,896]{2,1,0:T(8,128)(2,1)S(1)}, bf16[4,48,896]{2,1,0:T(8,128)(2,1)S(1)}, u32[]{:S(2)}, u32[]{:S(2)}) collective-permute-start(bf16[4,48,896]{2,1,0:T(8,128)(2,1)S(1)} %get-tuple-element.205), channel_id=1, source_target_pairs={{0,4},{2,6},{4,0},{6,2},{8,12},{10,14},{12,8},{14,10},{16,20},{18,... | collective-permute-start | bytes 1032200 | tf_op jit(solution)/shard_map/ppermute | solution.py:543
  192.8 6.8 %collective-permute-start.39 = (bf16[4,48,768]{2,1,0:T(8,128)(2,1)S(1)}, bf16[4,48,768]{2,1,0:T(8,128)(2,1)S(1)}, u32[]{:S(2)}, u32[]{:S(2)}) collective-permute-start(bf16[4,48,768]{2,1,0:T(8,128)(2,1)S(1)} %get-tuple-element.204), channel_id=1, source_target_pairs={{0,2},{2,0},{4,6},{6,4},{8,10},{10,8},{12,14},{14,12},{16,18},{18,... | collective-permute-start | bytes 884744 | tf_op jit(solution)/shard_map/ppermute | solution.py:543
  194.5 18.9 %collective-permute-start.42 = (bf16[2,48,1920]{2,1,0:T(8,128)(2,1)S(1)}, bf16[2,48,1920]{2,1,0:T(8,128)(2,1)S(1)}, u32[]{:S(2)}, u32[]{:S(2)}) collective-permute-start(bf16[2,48,1920]{2,1,0:T(8,128)(2,1)S(1)} %get-tuple-element.211), channel_id=1, source_target_pairs={{0,16},{2,18},{4,20},{6,22},{8,24},{10,26},{12,28},{14,30},{16,0},... | collective-permute-start | bytes 1105928 | tf_op jit(solution)/shard_map/ppermute | solution.py:543
  211.1 17.8 %collective-permute-start.45 = (bf16[2,48,1664]{2,1,0:T(8,128)(2,1)S(1)}, bf16[2,48,1664]{2,1,0:T(8,128)(2,1)S(1)}, u32[]{:S(2)}, u32[]{:S(2)}) collective-permute-start(bf16[2,48,1664]{2,1,0:T(8,128)(2,1)S(1)} %get-tuple-element.220), channel_id=1, source_target_pairs={{0,8},{2,10},{4,12},{6,14},{8,0},{10,2},{12,4},{14,6},{16,24},{18,... | collective-permute-start | bytes 958472 | tf_op jit(solution)/shard_map/ppermute | solution.py:543
  211.8 13.5 %collective-permute-start.44 = (bf16[2,48,1536]{2,1,0:T(8,128)(2,1)S(1)}, bf16[2,48,1536]{2,1,0:T(8,128)(2,1)S(1)}, u32[]{:S(2)}, u32[]{:S(2)}) collective-permute-start(bf16[2,48,1536]{2,1,0:T(8,128)(2,1)S(1)} %get-tuple-element.217), channel_id=1, source_target_pairs={{0,8},{2,10},{4,12},{6,14},{8,0},{10,2},{12,4},{14,6},{16,24},{18,... | collective-permute-start | bytes 884744 | tf_op jit(solution)/shard_map/ppermute | solution.py:543
  213.4 15.6 %collective-permute-start.46 = (bf16[1,48,1920]{2,1,0:T(8,128)(2,1)S(1)}, bf16[1,48,1920]{2,1,0:T(8,128)(2,1)S(1)}, u32[]{:S(2)}, u32[]{:S(2)}) collective-permute-start(bf16[1,48,1920]{2,1,0:T(8,128)(2,1)S(1)} %get-tuple-element.223), channel_id=1, source_target_pairs={{0,2},{2,0},{4,6},{6,4},{8,10},{10,8},{12,14},{14,12},{16,18},{18,... | collective-permute-start | bytes 552968 | tf_op jit(solution)/shard_map/ppermute | solution.py:543
  225.3 11.8 %collective-permute-start.47 = (bf16[1,48,1536]{2,1,0:T(8,128)(2,1)S(1)}, bf16[1,48,1536]{2,1,0:T(8,128)(2,1)S(1)}, u32[]{:S(2)}, u32[]{:S(2)}) collective-permute-start(bf16[1,48,1536]{2,1,0:T(8,128)(2,1)S(1)} %get-tuple-element.225), channel_id=1, source_target_pairs={{0,16},{2,18},{4,20},{6,22},{8,24},{10,26},{12,28},{14,30},{16,0},... | collective-permute-start | bytes 442376 | tf_op jit(solution)/shard_map/ppermute | solution.py:543
  229.0 9.6 %collective-permute-start.49 = (bf16[48,384]{1,0:T(8,128)(2,1)S(1)}, bf16[48,384]{1,0:T(8,128)(2,1)S(1)}, u32[]{:S(2)}, u32[]{:S(2)}) collective-permute-start(bf16[48,384]{1,0:T(8,128)(2,1)S(1)} %slice.21), channel_id=1, source_target_pairs={{0,1},{1,0},{2,3},{3,2},{4,5},{5,4},{6,7},{7,6},{8,9},{9,8},{10,11... | collective-permute-start | bytes 110600 | tf_op jit(solution)/shard_map/ppermute | solution.py:547
  229.1 10.8 %collective-permute-start.48 = (bf16[1,48,1664]{2,1,0:T(8,128)(2,1)S(1)}, bf16[1,48,1664]{2,1,0:T(8,128)(2,1)S(1)}, u32[]{:S(2)}, u32[]{:S(2)}) collective-permute-start(bf16[1,48,1664]{2,1,0:T(8,128)(2,1)S(1)} %get-tuple-element.227), channel_id=1, source_target_pairs={{0,16},{2,18},{4,20},{6,22},{8,24},{10,26},{12,28},{14,30},{16,0},... | collective-permute-start | bytes 479240 | tf_op jit(solution)/shard_map/ppermute | solution.py:543
  (22 other events, 152.6 us)
where the time goes:
time: 242 us
  waiting for transfers between devices  97.2 us (40%)
  Pallas kernels  81 us (33%)
  starting transfers between devices  43.1 us (18%)
  other arithmetic  10 us (4%)
  local copies, waits for them, and re-layouts  9.42 us (4%)
    ppermute x30, waiting for transfers between devices, swap(): return lax.ppermute(array, 'dp', [(i, i ^ mask) for i in range(size)])  93 us
    pallas_call x24, Pallas kernels, call(): pl.pallas_call(body, name=name, in_specs=in_specs, out_specs=[spec for _,...  81 us
    ppermute x30, starting transfers between devices, swap(): return lax.ppermute(array, 'dp', [(i, i ^ mask) for i in range(size)])  39.2 us
    unnamed x74, local copies, waits for them, and re-layouts  6.25 us
    concatenate x12, other arithmetic, join(): return jnp.concatenate([left, right], 0)  5.36 us
  transfers between devices with their start and end apart: 50, of which 22 were waited for; matrix products, arithmetic and copies ran while one was open for 5% of the time, Pallas kernels for 31%

commit v1 on v0

--- a/solution.py
+++ b/solution.py
@@ -27,6 +27,7 @@
     0, 1, 2, 3, 4, 5, 6, 7, 10, 11, 12,
 )
 SHARED, PAIR_ROW, UP_ROW, CLASS_ROW = 10, 10, 11, 12
+NOTES = 16
 
 
 def dot(left, right, dims=NN):
@@ -134,7 +135,7 @@
 
 
 def prepare_kernel(masks_p, masks_q, info, hidden, *refs):
-    outs, (rows_p, rows_q, x, other_x, flip, held, sems) = refs[0:4], refs[4:]
+    outs, (x_rows, x, other_x, flip, held, sems) = refs[0:4], refs[4:]
     me, core = info[0], info[1]
     begin(hidden.at[core], x, sems.at[0])
     begin(hidden.at[1 - core], other_x, sems.at[1])
@@ -144,13 +145,12 @@
         for n, masks in enumerate((masks_p, masks_q)):
             to_blocks(flip, held.at[2 * i + n], masks, me)
             begin(held.at[2 * i + n], outs[2 * i + n], sems.at[2 + 2 * i + n])
-    rows_p[...] = held[0].T
-    rows_q[...] = held[1].T
+    x_rows[...] = held[0].T
     for i in range(4):
         landed(held.at[i], sems.at[2 + i])
 
 
-def attend_kernel(masks_p, masks_q, info, hidden, rows_p, rows_q, *refs):
+def attend_kernel(masks, info, hidden, x_rows, *refs):
     qk, vo = refs[0:4], refs[4:8]
     q, k, v, att_own, att_other, p, first, first_p = refs[8:16]
     normed, root, vec = refs[16:19]
@@ -167,15 +167,15 @@
         loaded(wb, h, sems.at[pl.ds(2, 4)])
         for j in range(BLOCKS):
             piece = wb[h, j * rows : (j + 1) * rows, width:]
-            extra[row_block(me, masks_q[j], rows), :] = piece.astype(F32)
+            extra[row_block(me, masks[j], rows), :] = piece.astype(F32)
         unpack_vectors(extra, vec, h)
     for h in range(2):
         own = slice(h * half, (h + 1) * half)
         loaded(wa, h, sems.at[pl.ds(6, 4)])
-        both = dot(rows_p[...], wa[h])
+        both = dot(x_rows[...], wa[h])
         q[:, own] = (both[:, :half] + vec[QUERY_B : QUERY_B + 1, own]).astype(BF) * (1.0 / math.sqrt(HD))
         k[:, own] = both[:, half:].astype(BF)
-        v[:, own] = (dot(rows_q[...], wb[h, :, 0:half]) + vec[VALUE_B : VALUE_B + 1, own]).astype(BF)
+        v[:, own] = (dot(x_rows[...], wb[h, :, 0:half]) + vec[VALUE_B : VALUE_B + 1, own]).astype(BF)
     keys = lax.broadcasted_iota(jnp.int32, (1, length), 1)
     bias = jnp.where(keys < count, 0.0, -1e30).astype(F32)
     lane = lax.broadcasted_iota(jnp.int32, (1, LANES), 1)
@@ -194,7 +194,7 @@
         att[:, cols] = acc.astype(BF)
     att_own[...] = att[:, :half]
     att_other[...] = att[:, half:]
-    to_rows(row_product([wb[h, :, half:width] for h in range(2)], (att[:, :half], att[:, half:])), wide, masks_q, me)
+    to_rows(row_product([wb[h, :, half:width] for h in range(2)], (att[:, :half], att[:, half:])), wide, masks, me)
     landed(x, sems.at[0])
     own_normed, own_root = normalize(x[...].astype(F32) + wide[...].T + vec[OUT_B : OUT_B + 1, :])
     normed[...] = own_normed
@@ -202,7 +202,7 @@
     low = (own_normed * vec[GAIN_1 : GAIN_1 + 1, :] + vec[SHIFT_1 : SHIFT_1 + 1, :]).astype(BF)
     first[...] = low
     flip[...] = low.T
-    to_blocks(flip, first_p, masks_p, me)
+    to_blocks(flip, first_p, masks, me)
 
 
 def up_kernel(vec, first_p, *refs):
@@ -226,24 +226,30 @@
             slope[:, at : at + chunk] = (cdf + hidden * density).astype(BF)
 
 
-def ramp_kernel(masks, pool_masks, info, class_bias, vec, cotangent, active, other_active, first, *refs):
+def ramp_kernel(masks, pool_masks, back_masks, info, class_bias, vec, cotangent, active, other_active, first, *refs):
     pieces, pool_pieces = refs[0:4], refs[4:8]
-    block, ramp, feed_r, second, grads, w = refs[8:14]
-    cot, right, pool, flip, wide, slim, z, sems = refs[14:]
+    block, ramp, feed_r, feed_back, second, grads = refs[8:14]
+    w, cot, right, pool, flip, wide, slim, z, sems = refs[14:]
     me, core = info[0], info[1]
     count, label = info[2 + core], info[4 + core]
     length, width = first.shape
     half = width // 2
     cut = w.shape[2]
-    load(pieces, w, sems.at[pl.ds(0, 4)])
+    load(pieces, w, sems.at[pl.ds(0, 4)], (0, cut))
     begin(other_active, right, sems.at[8])
     load(pool_pieces, pool, sems.at[pl.ds(4, 4)], (cut, half))
     begin(cotangent.at[core], cot, sems.at[9])
-    loaded(w, 0, sems)
-    part = dot(w[0], active[...], NT)
+    parts = []
+    for i in range(2):
+        span = slice(i * half, (i + 1) * half)
+        landed(w.at[0, pl.ds(i * half, half), :], sems.at[i])
+        parts.append(dot(w[0, span, :], active[...], NT))
     landed(right, sems.at[8])
-    loaded(w, 1, sems)
-    to_rows(part + dot(w[1], right[...], NT), wide, masks, me)
+    for i in range(2):
+        span = slice(i * half, (i + 1) * half)
+        landed(w.at[1, pl.ds(i * half, half), :], sems.at[2 + i])
+        parts[i] = parts[i] + dot(w[1, span, :], right[...], NT)
+    to_rows(jnp.concatenate(parts, 0), wide, masks, me)
     total = first[...].astype(F32) + wide[...].T + vec[DOWN_B : DOWN_B + 1, :]
     gain, shift = vec[GAIN_2 : GAIN_2 + 1, :], vec[SHIFT_2 : SHIFT_2 + 1, :]
     normed, root = normalize(total)
@@ -304,41 +310,44 @@
     second[...] = dsecond
     flip[...] = dsecond.astype(BF).T
     to_blocks(flip, feed_r, masks, me)
-
-
-def hidden_kernel(feed_r, slope, w, delta, other_delta):
+    to_blocks(flip, feed_back, back_masks, me)
+
+
+def hidden_kernel(feed_r, slope, *refs):
+    pieces = refs[0:4]
+    delta, other_delta, w, sems = refs[4:]
     half = delta.shape[1]
+    load(pieces[2:] + pieces[:2], w, sems, (0, half))
     left = feed_r[...].T
     chunk = 512
-    for h, target in ((1, other_delta), (0, delta)):
+    for n, (h, target) in enumerate(((1, other_delta), (0, delta))):
+        loaded(w, n, sems)
         for c in range(half // chunk):
             cols = slice(c * chunk, (c + 1) * chunk)
             at = h * half + c * chunk
-            target[:, cols] = (dot(left, w[h, :, cols]) * slope[:, at : at + chunk].astype(F32)).astype(BF)
-
-
-def down_grad_kernel(masks, info, ramp, ramp_other, left_in, left_other_in, right, right_other_in, *refs):
-    lower, upper, logits, left, left_other, right_other, wide, slim, sems = refs
+            target[:, cols] = (dot(left, w[n, :, cols]) * slope[:, at : at + chunk].astype(F32)).astype(BF)
+
+
+def down_grad_kernel(info, ramp, ramp_other, left_in, left_other_in, right, right_other_in, *refs):
+    lower, upper, logits, left, left_other, right_other, sems = refs
     loads = ((left_in, left), (left_other_in, left_other), (right_other_in, right_other))
     for i, (source, target) in enumerate(loads):
         begin(source, target, sems.at[i])
     width, columns = left.shape[0], right.shape[1]
     half = width // 2
-    own = pl.ds(pl.multiple_of(info[1] * half, LANES), half)
     classes = logits.shape[1]
     pair = [r[3:4, LANES : LANES + classes] for r in (ramp, ramp_other)]
     logits[0:1, :] = jnp.where(info[1] == 0, pair[0], pair[1])
     logits[1:2, :] = jnp.where(info[1] == 0, pair[1], pair[0])
-    none = jnp.zeros((14, width), F32)
-    wide[...] = jnp.concatenate([ramp[0:1, :], ramp_other[0:1, :], none], 0).T
-    to_blocks(wide, slim, masks, info[0])
-    heads = slim[...].astype(BF)
-    pres = jnp.concatenate([ramp[2:3, own], ramp_other[2:3, own], none[:, :half]], 0).astype(BF)
-    for i, target in enumerate((lower, upper)):
-        target[:, columns:] = dot(heads[i * half : (i + 1) * half], pres).astype(BF)
+    heads = jnp.concatenate([ramp[0:1, :], ramp_other[0:1, :], jnp.zeros((NOTES - 2, width), F32)], 0)
+    pres = jnp.concatenate([ramp[2:3, :], ramp_other[2:3, :], jnp.zeros((NOTES - 2, width), F32)], 0)
+    upper[half:, :width] = heads.astype(BF)
+    upper[half:, width:] = pres.astype(BF)
     for i, (_, target) in enumerate(loads):
         landed(target, sems.at[i])
-    pair_product((left, left_other), (right, right_other), lower, upper)
+    for target, span in ((lower, slice(0, half)), (upper, slice(half, width))):
+        total = dot(left[span, :], right[...]) + dot(left_other[span, :], right_other[...])
+        target[0:half, :] = total.astype(BF)
 
 
 def up_grad_kernel(left, left_other, right, right_other_in, *refs):
@@ -350,19 +359,28 @@
     pair_product((left, left_other), (right, right_other), lower, upper)
 
 
-def branch_kernel(masks_p, masks_q, info, vec, sums_in, delta, other_delta, second, normed, root, wu, *refs):
-    vo = refs[0:4]
-    total_out, datt, branch_p, grads = refs[4:8]
-    wo, right, flip, rows_q, wide, sems = refs[8:]
+def branch_kernel(masks_p, masks_q, info, vec, sums_in, delta, other_delta, second, normed, root, *refs):
+    up, vo = refs[0:4], refs[4:8]
+    total_out, datt, branch_p, grads = refs[8:12]
+    wu, wo, right, flip, rows_q, wide, sems = refs[12:]
     me = info[0]
     width = normed.shape[1]
     half = width // 2
+    load(up, wu, sems.at[pl.ds(5, 4)], (0, delta.shape[1]))
     begin(other_delta, right, sems.at[4])
     load(vo, wo, sems.at[pl.ds(0, 4)], (half, half))
     gain = vec[GAIN_1 : GAIN_1 + 1, :]
-    part = dot(wu[0], delta[...], NT)
+    parts = []
+    for i in range(2):
+        span = slice(i * half, (i + 1) * half)
+        landed(wu.at[0, pl.ds(i * half, half), :], sems.at[5 + i])
+        parts.append(dot(wu[0, span, :], delta[...], NT))
     landed(right, sems.at[4])
-    to_rows(part + dot(wu[1], right[...], NT), wide, masks_p, me)
+    for i in range(2):
+        span = slice(i * half, (i + 1) * half)
+        landed(wu.at[1, pl.ds(i * half, half), :], sems.at[7 + i])
+        parts[i] = parts[i] + dot(wu[1, span, :], right[...], NT)
+    to_rows(jnp.concatenate(parts, 0), wide, masks_p, me)
     dfirst = second[...] + wide[...].T
     own_normed = normed[...]
     total = norm_backward(dfirst, own_normed, root[:, 0:1], gain)
@@ -382,8 +400,8 @@
 
 
 def back_kernel(q, k, v, att_own, att_other, datt, p, *refs):
-    own_out, other_out = refs[0:2]
-    att, dq, dk, dv = refs[2:]
+    qk_own, v_own, qk_other, v_other = refs[0:4]
+    att, dq, dk, dv = refs[4:]
     length, width = q.shape
     half = width // 2
     att[:, :half] = att_own[...]
@@ -414,9 +432,11 @@
         dq[:, cols] = (dq_sum * (1.0 / math.sqrt(HD))).astype(BF)
         dk[:, cols] = jnp.concatenate(dk_parts, 0).T.astype(BF)
         dv[:, cols] = jnp.concatenate(dv_parts, 0).T.astype(BF)
-    for h, out in ((1, other_out), (0, own_out)):
-        for i, source in enumerate((dq, dk, dv)):
-            out[:, i * half : (i + 1) * half] = source[:, h * half : (h + 1) * half]
+    for h, (qk, values) in enumerate(((qk_own, v_own), (qk_other, v_other))):
+        own = slice(h * half, (h + 1) * half)
+        qk[:, :half] = dq[:, own]
+        qk[:, half:] = dk[:, own]
+        values[...] = dv[:, own]
 
 
 def out_grad_kernel(branch_t, other_branch_t, att, other_att, grad):
@@ -424,7 +444,8 @@
 
 
 def input_grad_kernel(
-    masks_p, info, sums_in, sums_other, up_sums, x_p, x_q, other_p, other_q, delta, other_delta, out_grad, *refs
+    masks_p, info, sums_in, sums_other, up_sums, x_p, x_q, other_p, other_q, qk, qk_in, values, values_in, out_grad,
+    *refs
 ):
     qk_pieces, vo_pieces = refs[0:2], refs[2:4]
     extra = refs[4]
@@ -432,17 +453,18 @@
     width = x_p.shape[0]
     half = width // 2
     rows = width // BLOCKS
-    columns = column_sum(delta[...].astype(F32)) + column_sum(other_delta[...].astype(F32))
-    pack_vectors(sums_in[...] + sums_other[...], columns[:, :half], columns[:, width:], up_sums[...], extra)
+    query_sum = column_sum(qk[:, :half].astype(F32)) + column_sum(qk_in[:, :half].astype(F32))
+    value_sum = column_sum(values[...].astype(F32)) + column_sum(values_in[...].astype(F32))
+    pack_vectors(sums_in[...] + sums_other[...], query_sum, value_sum, up_sums[...], extra)
     for i, target in enumerate(vo_pieces):
         span = slice(i * half, (i + 1) * half)
-        total = dot(x_p[span, :], delta[:, width:]) + dot(other_p[span, :], other_delta[:, width:])
+        total = dot(x_p[span, :], values[...]) + dot(other_p[span, :], values_in[...])
         target[:, 0:half] = total.astype(BF)
         target[:, half:width] = out_grad[span, :]
         for j in range(BLOCKS // 2):
             at = row_block(me, masks_p[i * (BLOCKS // 2) + j], rows)
             target[j * rows : (j + 1) * rows, width:] = extra[at, :].astype(BF)
-    pair_product((x_q, other_q), (delta.at[:, pl.ds(0, width)], other_delta.at[:, pl.ds(0, width)]), *qk_pieces)
+    pair_product((x_q, other_q), (qk, qk_in), *qk_pieces)
 
 
 def hop_kernel(*refs):
@@ -454,6 +476,23 @@
         sent[:, :, cols] = own[half:] + arrived[half:]
         kept[:, :, cols] = own[:half] + arrived[:half]
         at += width
+
+
+def noted_hop_kernel(count, notes, own, arrived, sent, kept):
+    cut = sent.shape[0] - NOTES
+    sent[0:cut, :] = own[cut:, :] + arrived[cut : 2 * cut, :]
+    kept[...] = own[0:cut, :] + arrived[0:cut, :]
+    low, high = notes[0:NOTES, :].astype(F32), arrived[2 * cut :, :].astype(F32)
+    rows = lax.broadcasted_iota(jnp.int32, (NOTES, 1), 0)
+    sent[cut:, :] = jnp.where(rows < count, low, jnp.where(rows < 2 * count, pltpu.roll(high, count, 0), 0.0)).astype(BF)
+
+
+def ramp_grad_kernel(info, notes, arrived, out, flip):
+    rows, width = out.shape
+    both = jnp.concatenate([notes[...], arrived[...]], 0).astype(F32)
+    flip[...] = both[:, :width].T
+    own = flip[pl.ds(pl.multiple_of(info[0] * rows, 16), rows), :].astype(BF)
+    out[...] = dot(own, both[:, width:].astype(BF))
 
 
 def finish_kernel(kept, arrived, input_out, out_out, pair_out, up_out, class_bias_out, class_out, *vectors):
@@ -489,7 +528,7 @@
         landed(held.at[i], sems.at[4 + i])
 
 
-def input_kernel(masks_p, masks_q, info, own, other, total, *refs):
+def input_kernel(masks_p, masks_q, info, qk_own, v_own, qk_other, v_other, total, *refs):
     qk, vo = refs[0:4], refs[4:8]
     out, wa, wv, wide, wide_v, sems = refs[8:]
     me = info[0]
@@ -499,10 +538,10 @@
     load(qk, wa, sems.at[pl.ds(4, 4)])
     for h in range(2):
         loaded(wv, h, sems.at[pl.ds(0, 4)])
-    to_rows(row_product(wv, (own[:, width:], other[:, width:])), wide_v, masks_q, me)
+    to_rows(row_product(wv, (v_own[...], v_other[...])), wide_v, masks_q, me)
     for h in range(2):
         loaded(wa, h, sems.at[pl.ds(4, 4)])
-    to_rows(row_product(wa, (own[:, :width], other[:, :width])), wide, masks_p, me)
+    to_rows(row_product(wa, (qk_own[...], qk_other[...])), wide, masks_p, me)
     out[...] = (total[...] + (wide[...] + wide_v[...]).T).astype(BF)
 
 
@@ -527,7 +566,7 @@
     bits = [1 << k for k in range(size.bit_length() - 1)]
     high = bits[2:][::-1]
     x_last, y_last = high + [2, 1], high + [1, 2]
-    return (x_last, y_last, x_last, [1] + high + [2]), (y_last, x_last, x_last, [1] + high + [2])
+    return (x_last, x_last, x_last, [1] + high + [2]), (y_last, x_last, x_last, [1] + high + [2])
 
 
 def block_mask(index, order):
@@ -662,13 +701,13 @@
 
     row = shape(length, width)
     flat = shape(width, length)
-    x_p, x_q, other_p, other_q, rows_p, rows_q = call(
-        functools.partial(prepare_kernel, a_masks, b_masks),
+    x_p, x_q, other_p, other_q, x_rows = call(
+        functools.partial(prepare_kernel, back_masks[1], back_masks[0]),
         "prepare",
         0,
         8,
         [SCALARS, HBM],
-        in_hbm(flat, flat, flat, flat) + in_vmem(row, row),
+        in_hbm(flat, flat, flat, flat) + in_vmem(row),
         [of(row), of(row), of(flat), ((4, width, length), BF)],
         6,
         (info, inputs),
@@ -677,8 +716,8 @@
     pool_half = lax.dynamic_slice_in_dim(pool_weight, core * half, half, 1)
     a_shard = jnp.concatenate([input_weight[0], input_weight[1]], 1)
     vo_shard = jnp.concatenate([input_weight[2], out_weight.T], 1)
-    u_shard = jnp.concatenate([up_weight, pool_half], 1)
-    d_shard = down_weight.T
+    u_shard = up_weight
+    d_shard = jnp.concatenate([down_weight.T, pool_half], 1)
     shared = jnp.concatenate(
         [
             jnp.stack(
@@ -709,20 +748,20 @@
         a2_in, b2_in = swap(a2, z0), swap(b2, z0)
         u1 = swap(after(u0, a2, b2), z1)
         a4, b4 = join(a2, a2_in), join(b2, b2_in)
-        a4_in, b4_in = swap(a4, 2), swap(b4, 1)
+        a4_in, b4_in = swap(a4, 2), swap(b4, 2)
         u2 = after(join(u0, u1), a4, b4)
+        u2_in = swap(u2, z0)
+        a8, b8 = join(a4, a4_in), join(b4, b4_in)
+        a8_in, b8_in = swap(a8, 1), swap(b8, 1)
+        u4 = after(join(u2, u2_in), a8, b8)
         d2 = after(join(d0, d1), a4, b4)
-        u2_in, d2_in = swap(u2, z0), swap(d2, z1)
-        u4 = join(u2, u2_in)
-        u4_in = swap(u4, 2)
-        a8, b8 = join(a4, a4_in), join(b4, b4_in)
-        a8_in, b8_in = swap(a8, 1), swap(b8, 2)
+        u4_in, d2_in = swap(u4, 2), swap(d2, z1)
+        d4 = after(join(d2, d2_in), u4, a8_in, x_rows)
+        d4_in = swap(d4, z0)
         a8_other, b8_other = swap_core(a8), swap_core(b8)
-        d4 = after(join(d2, d2_in), a8, b8)
-        d4_in = swap(d4, z0)
-        u8 = after(join(u4, u4_in), a8_in, b8, rows_q)
+        u8 = after(join(u4, u4_in), a8_in, b8_in, d4)
         u8_in = swap(u8, 1)
-        d8 = after(join(d4, d4_in), b8_in, u8)
+        d8 = after(join(d4, d4_in), u8)
         d8_in = swap(d8, 2)
         info = after(info, u8, d8)
         qk = flat_rows(a8, a8_in, a8_other, swap_core(a8_in))
@@ -770,69 +809,68 @@
         return shape(2, width, columns)
 
     q, k, v, att, att_other, p, first, first_p, normed, root, vec = call(
-        functools.partial(attend_kernel, a_masks, b_masks),
+        functools.partial(attend_kernel, a_masks),
         "attend",
         0,
         18,
-        [SCALARS, HBM, VMEM, VMEM] + [HBM] * 8,
+        [SCALARS, HBM, VMEM] + [HBM] * 8,
         in_vmem(row, row, row, slim, slim, probs, row, flat, norm, roots, vectors),
         [of(row), of(blocks_of(width)), of(blocks_of(part)), of(row), of(flat), ((width, length), F32)]
         + [((width, LANES), F32)],
         10,
-        (info, inputs, rows_p, rows_q, *qk, *vo),
+        (info, inputs, x_rows, *qk, *vo),
     )
     (up_lo, up_hi), (down_lo, down_hi) = pieces
-    up_hi, down_hi = after(up_hi, first), after(down_hi, first)
-    up = with_other(up_lo, up_hi)
-    down = with_other(down_lo, down_hi)
+    up = with_other(up_lo, after(up_hi, first))
     first_in, att_in = swap_core(first_p), swap_core(att_other)
-    act, act_other, slope, up_matrix = call(
+    act, act_other, slope = call(
         up_kernel,
         "up",
         0,
-        4,
+        8,
         [VMEM, VMEM] + [HBM] * 4,
-        in_vmem(halved, halved, wide, blocks_of(hidden_half)),
-        [],
+        in_vmem(halved, halved, wide),
+        [of(blocks_of(hidden_half))],
         4,
         (vec, first_p, *up),
     )
     act_in = swap_core(act_other)
-    block_out, ramp, feed, second, sums_two, down_matrix = call(
-        functools.partial(ramp_kernel, d_masks, u_masks),
+    down = with_other(down_lo, after(down_hi, act))
+    block_out, ramp, feed, feed_back, second, sums_two = call(
+        functools.partial(ramp_kernel, d_masks, d_masks, back_masks[3]),
         "ramp",
         15,
-        14,
+        18,
         [SCALARS, SCALARS, VMEM, HBM, VMEM, HBM, VMEM] + [HBM] * 8,
-        in_vmem(row, eight, flat, norm, eight, blocks_of(hidden_half)),
-        [of(row), of(halved), of(blocks_of(half)), of(flat), ((width, length), F32), ((width, 2 * LANES), F32)]
+        in_vmem(row, eight, flat, flat, norm, eight),
+        [of(blocks_of(hidden_half)), of(row), of(halved), of(blocks_of(half)), of(flat), ((width, length), F32), ((width, 2 * LANES), F32)]
         + [of(eight)],
         10,
-        (info, class_bias.astype(F32), vec, cotangents, act, act_other, first, *down, *up),
-    )
-    feed_in, ramp_in = swap_core(feed), swap_core(ramp)
+        (info, class_bias.astype(F32), vec, cotangents, act, act_other, first, *down, *down),
+    )
+    feed_in, ramp_in = swap_core(feed_back), swap_core(ramp)
     delta, delta_other = call(
         hidden_kernel,
         "hidden",
         400,
-        5,
-        [VMEM] * 3,
+        9,
+        [VMEM] * 2 + [HBM] * 4,
         in_vmem(halved, halved),
-        [],
-        0,
-        (after(feed, act_in, first_in, att_in), slope, down_matrix),
+        [of(blocks_of(hidden_half))],
+        4,
+        (after(feed, act_in, first_in, att_in), slope, *down),
     )
     delta_in = swap_core(delta_other)
     *down_grad, logits_out = call(
-        functools.partial(down_grad_kernel, back_masks[3]),
+        down_grad_kernel,
         "down_grad",
         400,
         6,
         [SCALARS, VMEM, VMEM, HBM, HBM, VMEM, HBM],
-        in_vmem(*grad(hidden_half + half), shape(2, classes, dtype=F32)),
-        [of(flat), of(flat), of(halved), ((width, 16), F32), ((width, 16), F32)],
+        in_vmem(shape(half, hidden_half), shape(half + NOTES, hidden_half), shape(2, classes, dtype=F32)),
+        [of(flat), of(flat), of(halved)],
         3,
-        (after(info, delta), ramp, ramp_in, feed, feed_in, act, act_in),
+        (after(info, delta), ramp, ramp_in, feed_back, feed_in, act, act_in),
     )
 
     def first_hop(pieces, order):
@@ -858,8 +896,25 @@
         sent, kept = add((after(kept, start), arrived))
         return kept, swap(sent, mask)
 
-    down_grad = by_block(down_grad)
-    down_arrived = first_hop(down_grad, back_d)
+    down_arrived = swap(down_grad[1], back_d[-1]) if direct else None
+
+    def noted_hop(kept, notes, arrived, k, start):
+        if not direct:
+            return kept, notes, None
+        cut = kept.shape[0] // 2
+        sent, kept = call(
+            functools.partial(noted_hop_kernel, 2 << (2 - k)),
+            "noted_hop",
+            0,
+            4,
+            [VMEM] * 3,
+            in_vmem(shape(cut + NOTES, hidden_half), shape(cut, hidden_half)),
+            [],
+            0,
+            (notes, after(kept, start), arrived),
+        )
+        return kept, sent[cut:], swap(sent, back_d[k])
+
     *up_grad, up_sums = call(
         up_grad_kernel,
         "up_grad",
@@ -878,38 +933,37 @@
         functools.partial(branch_kernel, u_masks, b_masks),
         "branch",
         0,
-        11,
-        [SCALARS] + [VMEM] * 3 + [HBM] + [VMEM] * 4 + [HBM] * 4,
+        16,
+        [SCALARS] + [VMEM] * 3 + [HBM] + [VMEM] * 3 + [HBM] * 8,
         in_vmem(norm, row, flat, vectors),
-        [of(blocks_of(half)), of(halved), of(flat), of(flat), ((width, length), F32)],
-        5,
-        (after(info, up_grad[0]), vec, sums_two, delta, delta_other, second, normed, root, up_matrix, *vo),
+        [of(blocks_of(hidden_half)), of(blocks_of(half)), of(halved), of(flat), of(flat), ((width, length), F32)],
+        9,
+        (after(info, up_grad[0]), vec, sums_two, delta, delta_other, second, normed, root, *up, *vo),
     )
     branch_in, sums_in = swap_core(branch), swap_core(sums_one)
-    dqkv, dqkv_other = call(
+    dqk, dv, dqk_other, dv_other = call(
         back_kernel,
         "back",
         0,
         10,
         [VMEM] * 7,
-        in_vmem(thirds, thirds),
+        in_vmem(row, slim, row, slim),
         [of(row)] * 4,
         0,
         (q, k, v, att, att_other, after(datt, block_in), p),
     )
-    dqkv_in = swap_core(dqkv_other)
+    dqk_in, dv_in = swap_core(dqk_other), swap_core(dv_other)
     (input_delta,) = call(
         functools.partial(input_kernel, a_masks, b_masks),
         "input",
         0,
         9,
-        [SCALARS] + [VMEM] * 3 + [HBM] * 8,
+        [SCALARS] + [VMEM] * 5 + [HBM] * 8,
         in_vmem(row),
         [of(blocks_of(width)), of(blocks_of(half)), ((width, length), F32), ((width, length), F32)],
         8,
-        (info, dqkv, dqkv_other, total, *qk, *vo),
-    )
-    up_kept, up_arrived = next_hop(up_grad[0], up_arrived, back_u[2], input_delta)
+        (info, dqk, dv, dqk_other, dv_other, total, *qk, *vo),
+    )
     (out_grad,) = call(
         out_grad_kernel,
         "out_grad",
@@ -919,27 +973,28 @@
         in_vmem(shape(width, half)),
         [],
         0,
-        (after(branch, dqkv, sums_in, up_kept), branch_in, att, att_in),
-    )
+        (after(branch, dqk, sums_in, input_delta), branch_in, att, att_in),
+    )
+    up_sent, up_kept = add((after(up_grad[0], out_grad), up_arrived)) if direct else (None, up_grad[0])
     input_grads = call(
         functools.partial(input_grad_kernel, back_masks[1]),
         "input_grad",
         0,
         4,
-        [SCALARS] + [VMEM] * 10,
+        [SCALARS] + [VMEM] * 12,
         in_vmem(*grad(width), *grad(part)),
         [((width, LANES), F32)],
         0,
-        (info, sums_one, sums_in, up_sums, x_p, x_q, other_p, other_q, dqkv, dqkv_in, out_grad),
+        (after(info, up_kept), sums_one, sums_in, up_sums, x_p, x_q, other_p, other_q, dqk, dqk_in, dv, dv_in, out_grad),
     )
     qk_grad, vo_grad = by_block(input_grads[:2]), by_block(input_grads[2:])
     qk_arrived, vo_arrived = first_hop(qk_grad, back_a), first_hop(vo_grad, back_b)
     input_delta_in = swap_core(input_delta)
-    down_kept, down_arrived = next_hop(down_grad[0], down_arrived, back_d[2], qk_grad[0])
-    up_kept, up_arrived = next_hop(up_kept, up_arrived, back_u[1], down_kept)
-    qk_kept, qk_arrived = next_hop(qk_grad[0], qk_arrived, back_a[2], down_kept)
+    down_kept, notes, down_arrived = noted_hop(down_grad[0], down_grad[1][half:], down_arrived, 2, qk_grad[0])
     vo_kept, vo_arrived = next_hop(vo_grad[0], vo_arrived, back_b[2], down_kept)
-    down_kept, down_arrived = next_hop(down_kept, down_arrived, back_d[1], vo_kept)
+    qk_kept, qk_arrived = next_hop(qk_grad[0], qk_arrived, back_a[2], vo_kept)
+    up_arrived = swap(after(up_sent, qk_kept), back_u[2]) if direct else None
+    down_kept, notes, down_arrived = noted_hop(down_kept, notes, down_arrived, 1, qk_kept)
     blocks_out, input_grad = call(
         arrange_kernel,
         "arrange",
@@ -949,30 +1004,41 @@
         in_hbm(*[shape(2, length, width)] * 2),
         [((4, length, width), BF)],
         8,
-        (after(info, qk_kept, vo_kept), block_out, block_in, input_delta, input_delta_in),
+        (after(info, qk_kept), block_out, block_in, input_delta, input_delta_in),
     )
     if direct:
         sent, kept = add((after(qk_kept, blocks_out), qk_arrived), (vo_kept, vo_arrived))
         arrived = swap(sent, back_a[1])
-        down_kept, down_arrived = next_hop(down_kept, down_arrived, back_d[0], kept)
+        up_kept, up_arrived = next_hop(up_kept, up_arrived, back_u[1], kept)
+        down_kept, notes, down_arrived = noted_hop(down_kept, notes, down_arrived, 0, up_kept)
+        sent, kept = add((after(kept, down_kept), arrived))
+        arrived = swap(sent, back_a[0])
         up_kept, up_arrived = next_hop(up_kept, up_arrived, back_u[0], kept)
-        sent, kept = add((after(kept, down_kept, up_kept), arrived))
-        arrived = swap(sent, back_a[0])
         down_kept, up_kept = after(down_kept, kept), after(up_kept, kept)
-        down_share, up_share = (down_kept + down_arrived)[0], (up_kept + up_arrived)[0]
+        down_share, up_share = down_kept + down_arrived[:rows], (up_kept + up_arrived)[0]
+        (pool_grad,) = call(
+            ramp_grad_kernel,
+            "ramp_grad",
+            0,
+            2,
+            [SCALARS, VMEM, VMEM],
+            in_vmem(shape(rows, width, dtype=F32)),
+            [((width, 2 * NOTES), F32)],
+            0,
+            (info, notes, after(down_arrived[rows:], kept)),
+        )
         kept = after(kept, down_share, up_share)
     else:
 
         def spread(pieces, order):
             return scatter_blocks(out_of_order(join(*pieces).reshape(size, rows, -1), order, me), order)
 
-        down_share, up_share = spread(down_grad, back_d), spread(up_grad, back_u)
+        down_halves = by_block([down_grad[0], down_grad[1][:half]])
+        down_share, up_share = spread(down_halves, back_d), spread(up_grad, back_u)
+        notes = lax.all_gather(down_grad[1][half : half + 2], "dp", axis=0, tiled=True)
+        own_heads = lax.dynamic_slice_in_dim(notes[:, :width], me * rows, rows, 1)
+        pool_grad = dot(own_heads, notes[:, width:], TN)
         qk_share = spread(qk_grad, back_a)
-    down_share, pool_share = down_share[:, :hidden_half], down_share[:, hidden_half:]
-    pool_shares = pool_share, swap_core(pool_share)
-    pool_grad = jnp.where(
-        core == 0, jnp.concatenate(pool_shares, 1), jnp.concatenate(pool_shares[::-1], 1)
-    ).astype(F32)
     if direct:
         input_share, out_share, pair_share, up_bias_share, class_bias_grad, class_grad, *vector_grads = call(
             finish_kernel,

time: 242 us -> 228 us (0.942); the launches traced: 242 us -> 224 us
  Pallas kernels: 81 us -> 72.7 us
  starting transfers between devices: 43.1 us -> 36.1 us
    pallas_call x24 -> x25, Pallas kernels: 81 us -> 72.7 us  [call(): pl.pallas_call(body, name=name, in_specs=in_specs, out_specs=[spec for _,...]
    ppermute x30, starting transfers between devices: 39.2 us -> 31.5 us  [swap(): return lax.ppermute(array, 'dp', [(i, i ^ mask) for i in range(size)])]
    ppermute x20, waiting for transfers between devices: 4.23 us -> 7.73 us  [swap_core(): return lax.ppermute(array, 'tensor', [(0, 1), (1, 0)])]
    ppermute x30, waiting for transfers between devices: 93 us -> 90.1 us  [swap(): return lax.ppermute(array, 'dp', [(i, i ^ mask) for i in range(size)])]
    unnamed x74 -> x70, local copies, waits for them, and re-layouts: 6.25 us -> 4 us
  transfers between devices with their start and end apart: 50 -> 50, of which waited for: 22 -> 21; matrix products, arithmetic and copies ran while one was open for 5% -> 5% of each run, Pallas kernels for 31% -> 30%
where the time goes in v1:
time: 228 us; the launch traced here: 224 us
  waiting for transfers between devices  97.9 us (43%)
  Pallas kernels  72.7 us (32%)
  starting transfers between devices  36.1 us (16%)
  other arithmetic  8.54 us (4%)
  local copies, waits for them, and re-layouts  7.19 us (3%)
    ppermute x30, waiting for transfers between devices, swap(): return lax.ppermute(array, 'dp', [(i, i ^ mask) for i in range(size)])  90.1 us
    pallas_call x25, Pallas kernels, call(): pl.pallas_call(body, name=name, in_specs=in_specs, out_specs=[spec for _,...  72.7 us
    ppermute x30, starting transfers between devices, swap(): return lax.ppermute(array, 'dp', [(i, i ^ mask) for i in range(size)])  31.5 us
    ppermute x20, waiting for transfers between devices, swap_core(): return lax.ppermute(array, 'tensor', [(0, 1), (1, 0)])  7.73 us
    concatenate x12, other arithmetic, join(): return jnp.concatenate([left, right], 0)  4.61 us
  transfers between devices with their start and end apart: 50, of which 21 were waited for; matrix products, arithmetic and copies ran while one was open for 5% of the time, Pallas kernels for 30%

profile of v1, /device:TPU:0, one launch (start us, length us, event | category | flops | bytes accessed | tf_op | source)
XLA Modules:
  0.0 224.0 jit_solution(5289399014263670632)
XLA Ops:
  0.7 0.9 slice_bitcast_fusion
  1.6 4.1 %collective-permute-start = (bf16[1,48,768]{2,1,0:T(8,128)(2,1)S(1)}, bf16[1,48,768]{2,1,0:T(8,128)(2,1)S(1)}, u32[]{:S(2)}, u32[]{:S(2)}) collective-permute-start(bf16[1,48,768]{2,1,0:T(8,128)(2,1)S(1)} %fusion.6), channel_id=1, source_target_pairs={{0,16},{2,18},{4,20},{6,22},{8,24},{10,26},{12,28},{14,30},{16,0},... | collective-permute-start | bytes 221192 | tf_op jit(solution)/shard_map/ppermute | solution.py:582
  5.7 0.7 reshape.151
  6.4 1.6 concatenate.61
  8.6 0.8 maximum_bitcast_fusion
  9.6 1.9 collective-permute-start.3
  11.5 4.3 %collective-permute-done.1 = bf16[1,48,896]{2,1,0:T(8,128)(2,1)S(1)} collective-permute-done((bf16[1,48,896]{2,1,0:T(8,128)(2,1)S(1)}, bf16[1,48,896]{2,1,0:T(8,128)(2,1)S(1)}, u32[]{:S(2)}, u32[]{:S(2)}) %collective-permute-start.1) | collective-permute-done | bytes 86048 | tf_op jit(solution)/shard_map/ppermute | solution.py:582
  15.9 0.9 fusion.7
  16.8 1.9 collective-permute-start.11
  18.7 2.0 collective-permute-start.4
  20.7 1.6 collective-permute-start.6
  22.6 3.0 %collective-permute-done.4 = bf16[2,48,896]{2,1,0:T(8,128)(2,1)S(1)} collective-permute-done((bf16[2,48,896]{2,1,0:T(8,128)(2,1)S(1)}, bf16[2,48,896]{2,1,0:T(8,128)(2,1)S(1)}, u32[]{:S(2)}, u32[]{:S(2)}) %collective-permute-start.4) | collective-permute-done | bytes 172064 | tf_op jit(solution)/shard_map/ppermute | solution.py:582
  26.2 0.8 pad_maximum_fusion.6
  27.0 1.5 collective-permute-start.7
  28.5 2.2 collective-permute-start.12
  30.8 1.5 collective-permute-start.9
  32.3 5.1 %collective-permute-done.5 = bf16[2,48,1536]{2,1,0:T(8,128)(2,1)S(1)} collective-permute-done((bf16[2,48,1536]{2,1,0:T(8,128)(2,1)S(1)}, bf16[2,48,1536]{2,1,0:T(8,128)(2,1)S(1)}, u32[]{:S(2)}, u32[]{:S(2)}) %collective-permute-start.5) | collective-permute-done | bytes 294944 | tf_op jit(solution)/shard_map/ppermute | solution.py:582
  37.4 0.9 pad_maximum_fusion.4
  38.4 1.7 collective-permute-start.8
  40.7 1.9 prepare.1
  42.7 4.2 %collective-permute-done.12 = bf16[2,48,1920]{2,1,0:T(8,128)(2,1)} collective-permute-done((bf16[2,48,1920]{2,1,0:T(8,128)(2,1)}, bf16[2,48,1920]{2,1,0:T(8,128)(2,1)}, u32[]{:S(2)}, u32[]{:S(2)}) %collective-permute-start.12) | collective-permute-done | bytes 368672 | tf_op jit(solution)/shard_map/ppermute | solution.py:582
  46.9 1.2 pad_maximum_fusion.2
  48.2 4.4 %collective-permute-done.8 = bf16[4,48,1536]{2,1,0:T(8,128)(2,1)} collective-permute-done((bf16[4,48,1536]{2,1,0:T(8,128)(2,1)}, bf16[4,48,1536]{2,1,0:T(8,128)(2,1)}, u32[]{:S(2)}, u32[]{:S(2)}) %collective-permute-start.8) | collective-permute-done | bytes 589856 | tf_op jit(solution)/shard_map/ppermute | solution.py:582
  52.6 1.3 pad_maximum_fusion.1
  53.9 4.4 %collective-permute-done.10 = bf16[8,48,896]{2,1,0:T(8,128)(2,1)S(1)} collective-permute-done((bf16[8,48,896]{2,1,0:T(8,128)(2,1)S(1)}, bf16[8,48,896]{2,1,0:T(8,128)(2,1)S(1)}, u32[]{:S(2)}, u32[]{:S(2)}) %collective-permute-start.10) | collective-permute-done | bytes 688160 | tf_op jit(solution)/shard_map/ppermute | solution.py:582
  58.3 2.3 %collective-permute-start.18 = (bf16[8,48,1536]{2,1,0:T(8,128)(2,1)S(1)}, bf16[8,48,1536]{2,1,0:T(8,128)(2,1)S(1)}, u32[]{:S(2)}, u32[]{:S(2)}) collective-permute-start(bf16[8,48,1536]{2,1,0:T(8,128)(2,1)S(1)} %pad_maximum_fusion.1), channel_id=1, source_target_pairs={{0,2},{2,0},{4,6},{6,4},{8,10},{10,8},{12,14},{14,12},{16,18},{18,... | collective-permute-start | bytes 3538952 | tf_op jit(solution)/shard_map/ppermute | solution.py:582
  61.1 3.8 %collective-permute-done.13 = bf16[4,48,1920]{2,1,0:T(8,128)(2,1)S(1)} collective-permute-done((bf16[4,48,1920]{2,1,0:T(8,128)(2,1)S(1)}, bf16[4,48,1920]{2,1,0:T(8,128)(2,1)S(1)}, u32[]{:S(2)}, u32[]{:S(2)}) %collective-permute-start.13) | collective-permute-done | bytes 737312 | tf_op jit(solution)/shard_map/ppermute | solution.py:582
  65.9 1.2 collective-permute-done.15
  67.1 13.4 %attend.1 = (bf16[512,768]{1,0:T(8,128)(2,1)S(1)}, bf16[512,768]{1,0:T(8,128)(2,1)S(1)}, bf16[512,768]{1,0:T(8,128)(2,1)S(1)}, bf16[512,384]{1,0:T(8,128)(2,1)S(...) custom-call(s32[6]{0:T(128)S(1)} %pad_add_fusion.info, ...), custom_call_target="tpu_custom_call" | custom-call | bytes 1024 | tf_op jit(solution)/shard_map/attend/pallas_call | solution.py:553
  80.6 3.2 %collective-permute-done.18 = bf16[8,48,1536]{2,1,0:T(8,128)(2,1)S(1)} collective-permute-done((bf16[8,48,1536]{2,1,0:T(8,128)(2,1)S(1)}, bf16[8,48,1536]{2,1,0:T(8,128)(2,1)S(1)}, u32[]{:S(2)}, u32[]{:S(2)}) %collective-permute-start.18) | collective-permute-done | bytes 1179680 | tf_op jit(solution)/shard_map/ppermute | solution.py:582
  84.4 2.3 %collective-permute-done.20 = bf16[8,48,1536]{2,1,0:T(8,128)(2,1)S(1)} collective-permute-done((bf16[8,48,1536]{2,1,0:T(8,128)(2,1)S(1)}, bf16[8,48,1536]{2,1,0:T(8,128)(2,1)S(1)}, u32[]{:S(2)}, u32[]{:S(2)}) %collective-permute-start.20) | collective-permute-done | bytes 1179680 | tf_op jit(solution)/shard_map/ppermute | solution.py:586
  86.7 6.1 %up.1 = (bf16[512,1536]{1,0:T(8,128)(2,1)S(1)}, bf16[512,1536]{1,0:T(8,128)(2,1)S(1)}, bf16[512,3072]{1,0:T(8,128)(2,1)S(1)}) custom-call(f32[16,768]{1,0:T(8,128)S(1)} %get-tuple-element.145.vec, bf16[768,512]{1,0:T(8,128)(2,1)S(1)} %get-tuple-element.160.first_p.left, bf16[384,1536]{1,0:T(8,128)(2,1)S(1)} %bitcast.80, bf16[384,1536]{1,0:T(8,128)(2,1)S(1)} %bitcast.95, ...), custom_call_target="tpu_custom_call" | custom-call | bytes 1024 | tf_op jit(solution)/shard_map/up/pallas_call | solution.py:553
  92.9 7.0 %collective-permute-done.21 = bf16[8,48,1920]{2,1,0:T(8,128)(2,1)S(1)} collective-permute-done((bf16[8,48,1920]{2,1,0:T(8,128)(2,1)S(1)}, bf16[8,48,1920]{2,1,0:T(8,128)(2,1)S(1)}, u32[]{:S(2)}, u32[]{:S(2)}) %collective-permute-start.21) | collective-permute-done | bytes 1474592 | tf_op jit(solution)/shard_map/ppermute | solution.py:582
  100.9 2.2 collective-permute-done.23
  103.1 9.1 %ramp.1 = (bf16[512,768]{1,0:T(8,128)(2,1)S(1)}, f32[8,768]{1,0:T(8,128)}, bf16[768,512]{1,0:T(8,128)(2,1)S(1)}, bf16[768,512]{1,0:T(8,128)(2,1)}, f32[512,768]{1,0:T(8,128)S(1)}, /*index=5*/f32[8,768]{1,0:T(8,128)S(1)}) custom-call(s32[6]{0:T(128)S(1)} %pad_add_fusion.info, f32[3]{0:T(128)S(1)} %convert_element_type.20.class_bias, ...), custom_call_target="tpu_custom_call" | custom-call | flops 17250000896 | bytes 1024 | tf_op jit(solution)/shard_map/ramp/pallas_call | solution.py:553
  112.9 1.2 copy-done.28
  114.1 3.9 %hidden.1 = (bf16[512,1536]{1,0:T(8,128)(2,1)S(1)}, bf16[512,1536]{1,0:T(8,128)(2,1)}) custom-call(bf16[768,512]{1,0:T(8,128)(2,1)S(1)} %get-tuple-element.153.feed_r, bf16[512,3072]{1,0:T(8,128)(2,1)S(1)} %get-tuple-element.154.slope, bf16[384,1920]{1,0:T(8,128)(2,1)S(1)} %bitcast.107, bf16[384,1920]{1,0:T(8,128)(2,1)S(1)} %bitcast.114, ...), custom_call_target="tpu_custom_call" | custom-call | flops 460000002048 | bytes 1024 | tf_op jit(solution)/shard_map/hidden/pallas_call | solution.py:553
  118.2 4.8 %down_grad.1 = (bf16[384,1536]{1,0:T(8,128)(2,1)S(1)}, bf16[400,1536]{1,0:T(8,128)(2,1)S(1)}, f32[2,3]{1,0:T(2,128)}) custom-call(s32[6]{0:T(128)S(1)} %pad_add_fusion.info, f32[8,768]{1,0:T(8,128)} %get-tuple-element.157.ramp, f32[8,768]{1,0:T(8,128)} %collective-permute-done.27.ramp_other, bf16[768,512]{1,0:T(8,128)(2,1)} %get-tuple-element.158.left_in, ...), custom_call_target="tpu_custom_call" | custom-call | flops 460000002048 | bytes 1024 | tf_op jit(solution)/shard_map/down_grad/pallas_call | solution.py:553
  123.1 4.3 %up_grad.1 = (bf16[384,1536]{1,0:T(8,128)(2,1)S(1)}, bf16[384,1536]{1,0:T(8,128)(2,1)S(1)}, f32[1,1536]{1,0:T(1,128)S(1)}) custom-call(bf16[768,512]{1,0:T(8,128)(2,1)S(1)} %get-tuple-element.160.first_p.left, bf16[768,512]{1,0:T(8,128)(2,1)S(1)} %copy-done.18, bf16[512,1536]{1,0:T(8,128)(2,1)S(1)} %get-tuple-element.155.right.delta, ...), custom_call_target="tpu_custom_call" | custom-call | bytes 1024 | tf_op jit(solution)/shard_map/up_grad/pallas_call | solution.py:553
  127.9 1.1 collective-permute-start.36
  129.0 1.3 copy-done.12
  130.3 8.5 %branch.1 = (f32[512,768]{1,0:T(8,128)S(1)}, bf16[512,768]{1,0:T(8,128)(2,1)S(1)}, bf16[768,512]{1,0:T(8,128)(2,1)S(1)}, f32[16,768]{1,0:T(8,128)S(1)}) custom-call(s32[6]{0:T(128)S(1)} %copy-done.24, f32[16,768]{1,0:T(8,128)S(1)} %get-tuple-element.145.vec, f32[8,768]{1,0:T(8,128)S(1)} %get-tuple-element.164.sums_in, ...), custom_call_target="tpu_custom_call" | custom-call | bytes 1024 | tf_op jit(solution)/shard_map/branch/pallas_call | solution.py:553
  138.9 6.9 %back.1 = (bf16[512,768]{1,0:T(8,128)(2,1)S(1)}, bf16[512,384]{1,0:T(8,128)(2,1)S(1)}, bf16[512,768]{1,0:T(8,128)(2,1)S(1)}, bf16[512,384]{1,0:T(8,128)(2,1)S(1)}) custom-call(bf16[512,768]{1,0:T(8,128)(2,1)S(1)} %get-tuple-element.169.q, bf16[512,768]{1,0:T(8,128)(2,1)S(1)} %get-tuple-element.170.k, bf16[512,768]{1,0:T(8,128)(2,1)S(1)} %get-tuple-element.171.v, ...), custom_call_target="tpu_custom_call" | custom-call | bytes 1024 | tf_op jit(solution)/shard_map/back/pallas_call | solution.py:553
  146.5 1.9 collective-permute-done.31.sums_other
  148.7 4.2 %input.1.grad_own = bf16[512,768]{1,0:T(8,128)(2,1)S(1)} custom-call(s32[6]{0:T(128)S(1)} %copy-done.24, bf16[512,768]{1,0:T(8,128)(2,1)S(1)} %get-tuple-element.179.qk_own.qk, bf16[512,384]{1,0:T(8,128)(2,1)S(1)} %get-tuple-element.181.v_own.values, bf16[512,768]{1,0:T(8,128)(2,1)S(1)} %get-tuple-element.182.qk_other, ...), custom_call_target="tpu_custom_call" | custom-call | bytes 1024 | tf_op jit(solution)/shard_map/input/pallas_call | solution.py:553
  153.0 1.0 out_grad.1
  154.0 1.9 collective-permute-done.33.refs_1_
  156.1 2.9 %input_grad.1 = (bf16[384,768]{1,0:T(8,128)(2,1)S(1)}, bf16[384,768]{1,0:T(8,128)(2,1)S(1)}, bf16[384,896]{1,0:T(8,128)(2,1)S(1)}, bf16[384,896]{1,0:T(8,128)(2,1)S(1)}) custom-call(s32[6]{0:T(128)S(1)} %copy-done.24, f32[16,768]{1,0:T(8,128)S(1)} %get-tuple-element.180.sums_in, f32[16,768]{1,0:T(8,128)S(1)} %collective-permute-done.31.sums_other, ...), custom_call_target="tpu_custom_call" | custom-call | bytes 1024 | tf_op jit(solution)/shard_map/input_grad/pallas_call | solution.py:553
  159.3 0.8 collective-permute-start.38
  160.6 15.0 %collective-permute-done.37.refs_1_ = bf16[8,48,896]{2,1,0:T(8,128)(2,1)S(1)} collective-permute-done((bf16[8,48,896]{2,1,0:T(8,128)(2,1)S(1)}, bf16[8,48,896]{2,1,0:T(8,128)(2,1)S(1)}, u32[]{:S(2)}, u32[]{:S(2)}) %collective-permute-start.37) | collective-permute-done | bytes 688160 | tf_op jit(solution)/shard_map/ppermute | solution.py:582
  176.4 1.5 collective-permute-start.41
  178.7 2.5 %arrange.1 = (bf16[2,512,768]{2,1,0:T(8,128)(2,1)}, bf16[2,512,768]{2,1,0:T(8,128)(2,1)}) custom-call(s32[6]{0:T(128)S(1)} %copy-done.24, bf16[512,768]{1,0:T(8,128)(2,1)S(1)} %get-tuple-element.176.block_own, bf16[512,768]{1,0:T(8,128)(2,1)S(1)} %collective-permute-done.30.block_other, bf16[512,768]{1,0:T(8,128)(2,1)S(1)} %input.1.grad_own, ...), custom_call_target="tpu_custom_call" | custom-call | bytes 1024 | tf_op jit(solution)/shard_map/arrange/pallas_call | solution.py:553
  181.2 3.4 %collective-permute-done.40.refs_1_ = bf16[4,48,768]{2,1,0:T(8,128)(2,1)S(1)} collective-permute-done((bf16[4,48,768]{2,1,0:T(8,128)(2,1)S(1)}, bf16[4,48,768]{2,1,0:T(8,128)(2,1)S(1)}, u32[]{:S(2)}, u32[]{:S(2)}) %collective-permute-start.40) | collective-permute-done | bytes 294944 | tf_op jit(solution)/shard_map/ppermute | solution.py:582
  184.6 12.2 %collective-permute-done.41.refs_3_ = bf16[4,48,896]{2,1,0:T(8,128)(2,1)S(1)} collective-permute-done((bf16[4,48,896]{2,1,0:T(8,128)(2,1)S(1)}, bf16[4,48,896]{2,1,0:T(8,128)(2,1)S(1)}, u32[]{:S(2)}, u32[]{:S(2)}) %collective-permute-start.41) | collective-permute-done | bytes 344096 | tf_op jit(solution)/shard_map/ppermute | solution.py:582
  197.4 1.8 collective-permute-start.47
  199.2 1.1 collective-permute-start.46
  200.4 8.4 %collective-permute-done.45.refs_1_ = bf16[2,48,1664]{2,1,0:T(8,128)(2,1)S(1)} collective-permute-done((bf16[2,48,1664]{2,1,0:T(8,128)(2,1)S(1)}, bf16[2,48,1664]{2,1,0:T(8,128)(2,1)S(1)}, u32[]{:S(2)}, u32[]{:S(2)}) %collective-permute-start.45) | collective-permute-done | bytes 319520 | tf_op jit(solution)/shard_map/ppermute | solution.py:582
  208.9 3.0 %collective-permute-done.47.refs_1_ = bf16[2,48,1536]{2,1,0:T(8,128)(2,1)S(1)} collective-permute-done((bf16[2,48,1536]{2,1,0:T(8,128)(2,1)S(1)}, bf16[2,48,1536]{2,1,0:T(8,128)(2,1)S(1)}, u32[]{:S(2)}, u32[]{:S(2)}) %collective-permute-start.47) | collective-permute-done | bytes 294944 | tf_op jit(solution)/shard_map/ppermute | solution.py:582
  212.0 0.7 convert_bitcast_fusion
  212.8 1.5 ramp_grad.1
  214.3 6.5 %collective-permute-done.48 = bf16[1,48,1536]{2,1,0:T(8,128)(2,1)S(1)} collective-permute-done((bf16[1,48,1536]{2,1,0:T(8,128)(2,1)S(1)}, bf16[1,48,1536]{2,1,0:T(8,128)(2,1)S(1)}, u32[]{:S(2)}, u32[]{:S(2)}) %collective-permute-start.48) | collective-permute-done | bytes 147488 | tf_op jit(solution)/shard_map/ppermute | solution.py:582
  220.8 0.7 fusion.8
  221.5 0.8 finish.1
  223.0 0.7 copy.42
  (161 shorter events, 12.2 us)
Async XLA Ops:
  0.7 21.9 %copy-start.30 = (bf16[48,1536]{1,0:T(8,128)(2,1)S(1)}, bf16[48,1536]{1,0:T(8,128)(2,1)}, u32[]{:S(2)}) copy-start(bf16[48,1536]{1,0:T(8,128)(2,1)} %param.30) | copy-start | bytes 442372
  1.6 8.0 %collective-permute-start = (bf16[1,48,768]{2,1,0:T(8,128)(2,1)S(1)}, bf16[1,48,768]{2,1,0:T(8,128)(2,1)S(1)}, u32[]{:S(2)}, u32[]{:S(2)}) collective-permute-start(bf16[1,48,768]{2,1,0:T(8,128)(2,1)S(1)} %fusion.6), channel_id=1, source_target_pairs={{0,16},{2,18},{4,20},{6,22},{8,24},{10,26},{12,28},{14,30},{16,0},... | collective-permute-start | bytes 221192 | tf_op jit(solution)/shard_map/ppermute | solution.py:582
  9.4 6.3 %collective-permute-start.1 = (bf16[1,48,896]{2,1,0:T(8,128)(2,1)S(1)}, bf16[1,48,896]{2,1,0:T(8,128)(2,1)S(1)}, u32[]{:S(2)}, u32[]{:S(2)}) collective-permute-start(bf16[1,48,896]{2,1,0:T(8,128)(2,1)S(1)} %maximum_bitcast_fusion), channel_id=1, source_target_pairs={{0,16},{2,18},{4,20},{6,22},{8,24},{10,26},{12,28},{14,30},{16,0},... | collective-permute-start | bytes 258056 | tf_op jit(solution)/shard_map/ppermute | solution.py:582
  9.6 11.1 %collective-permute-start.3 = (bf16[2,48,768]{2,1,0:T(8,128)(2,1)S(1)}, bf16[2,48,768]{2,1,0:T(8,128)(2,1)S(1)}, u32[]{:S(2)}, u32[]{:S(2)}) collective-permute-start(bf16[2,48,768]{2,1,0:T(8,128)(2,1)S(1)} %pad_maximum_fusion.12), channel_id=1, source_target_pairs={{0,8},{2,10},{4,12},{6,14},{8,0},{10,2},{12,4},{14,6},{16,24},{18,... | collective-permute-start | bytes 442376 | tf_op jit(solution)/shard_map/ppermute | solution.py:582
  15.8 6.8 %collective-permute-start.2 = (bf16[1,48,1536]{2,1,0:T(8,128)(2,1)}, bf16[1,48,1536]{2,1,0:T(8,128)(2,1)S(1)}, u32[]{:S(2)}, u32[]{:S(2)}) collective-permute-start(bf16[1,48,1536]{2,1,0:T(8,128)(2,1)} %bitcast.125), channel_id=1, source_target_pairs={{0,16},{2,18},{4,20},{6,22},{8,24},{10,26},{12,28},{14,30},{16,0},... | collective-permute-start | bytes 442376 | tf_op jit(solution)/shard_map/ppermute | solution.py:582
  16.8 9.4 %collective-permute-start.11 = (bf16[1,48,1920]{2,1,0:T(8,128)(2,1)S(1)}, bf16[1,48,1920]{2,1,0:T(8,128)(2,1)S(1)}, u32[]{:S(2)}, u32[]{:S(2)}) collective-permute-start(bf16[1,48,1920]{2,1,0:T(8,128)(2,1)S(1)} %fusion.7), channel_id=1, source_target_pairs={{0,2},{2,0},{4,6},{6,4},{8,10},{10,8},{12,14},{14,12},{16,18},{18,... | collective-permute-start | bytes 552968 | tf_op jit(solution)/shard_map/ppermute | solution.py:582
  18.7 6.9 %collective-permute-start.4 = (bf16[2,48,896]{2,1,0:T(8,128)(2,1)S(1)}, bf16[2,48,896]{2,1,0:T(8,128)(2,1)S(1)}, u32[]{:S(2)}, u32[]{:S(2)}) collective-permute-start(bf16[2,48,896]{2,1,0:T(8,128)(2,1)S(1)} %pad_maximum_fusion.11), channel_id=1, source_target_pairs={{0,8},{2,10},{4,12},{6,14},{8,0},{10,2},{12,4},{14,6},{16,24},{18,... | collective-permute-start | bytes 516104 | tf_op jit(solution)/shard_map/ppermute | solution.py:582
  20.7 10.0 %collective-permute-start.6 = (bf16[4,48,768]{2,1,0:T(8,128)(2,1)S(1)}, bf16[4,48,768]{2,1,0:T(8,128)(2,1)S(1)}, u32[]{:S(2)}, u32[]{:S(2)}) collective-permute-start(bf16[4,48,768]{2,1,0:T(8,128)(2,1)S(1)} %pad_maximum_fusion.9), channel_id=1, source_target_pairs={{0,4},{2,6},{4,0},{6,2},{8,12},{10,14},{12,8},{14,10},{16,20},{18,... | collective-permute-start | bytes 884744 | tf_op jit(solution)/shard_map/ppermute | solution.py:582
  25.6 11.8 %collective-permute-start.5 = (bf16[2,48,1536]{2,1,0:T(8,128)(2,1)S(1)}, bf16[2,48,1536]{2,1,0:T(8,128)(2,1)S(1)}, u32[]{:S(2)}, u32[]{:S(2)}) collective-permute-start(bf16[2,48,1536]{2,1,0:T(8,128)(2,1)S(1)} %pad_maximum_fusion.8), channel_id=1, source_target_pairs={{0,8},{2,10},{4,12},{6,14},{8,0},{10,2},{12,4},{14,6},{16,24},{18,... | collective-permute-start | bytes 884744 | tf_op jit(solution)/shard_map/ppermute | solution.py:582
  27.0 11.3 %collective-permute-start.7 = (bf16[4,48,896]{2,1,0:T(8,128)(2,1)S(1)}, bf16[4,48,896]{2,1,0:T(8,128)(2,1)S(1)}, u32[]{:S(2)}, u32[]{:S(2)}) collective-permute-start(bf16[4,48,896]{2,1,0:T(8,128)(2,1)S(1)} %pad_maximum_fusion.7), channel_id=1, source_target_pairs={{0,4},{2,6},{4,0},{6,2},{8,12},{10,14},{12,8},{14,10},{16,20},{18,... | collective-permute-start | bytes 1032200 | tf_op jit(solution)/shard_map/ppermute | solution.py:582
  28.5 18.4 %collective-permute-start.12 = (bf16[2,48,1920]{2,1,0:T(8,128)(2,1)}, bf16[2,48,1920]{2,1,0:T(8,128)(2,1)}, u32[]{:S(2)}, u32[]{:S(2)}) collective-permute-start(bf16[2,48,1920]{2,1,0:T(8,128)(2,1)} %pad_maximum_fusion.6), channel_id=1, source_target_pairs={{0,16},{2,18},{4,20},{6,22},{8,24},{10,26},{12,28},{14,30},{16,0},... | collective-permute-start | bytes 1105928 | tf_op jit(solution)/shard_map/ppermute | solution.py:582
  30.8 9.9 %copy-start.31 = (s32[2,1]{0,1:T(1,128)S(1)}, s32[2,1]{0,1:T(1,128)}, u32[]{:S(2)}) copy-start(s32[2,1]{0,1:T(1,128)} %param.22) | copy-start | bytes 28
  30.8 9.8 %copy-start.32 = (s32[2,1]{0,1:T(1,128)S(1)}, s32[2,1]{0,1:T(1,128)}, u32[]{:S(2)}) copy-start(s32[2,1]{0,1:T(1,128)} %param.21) | copy-start | bytes 28
  30.8 9.9 %copy-start.2 = (bf16[2,1,512,768]{3,2,1,0:T(8,128)(2,1)S(1)}, bf16[2,1,512,768]{3,2,1,0:T(8,128)(2,1)}, u32[]{:S(2)}) copy-start(bf16[2,1,512,768]{3,2,1,0:T(8,128)(2,1)} %param.20) | copy-start | bytes 4718596
  30.8 17.2 %collective-permute-start.9 = (bf16[8,48,768]{2,1,0:T(8,128)(2,1)S(1)}, bf16[8,48,768]{2,1,0:T(8,128)(2,1)}, u32[]{:S(2)}, u32[]{:S(2)}) collective-permute-start(bf16[8,48,768]{2,1,0:T(8,128)(2,1)S(1)} %pad_maximum_fusion.5), channel_id=1, source_target_pairs={{0,2},{2,0},{4,6},{6,4},{8,10},{10,8},{12,14},{14,12},{16,18},{18,... | collective-permute-start | bytes 1769480 | tf_op jit(solution)/shard_map/ppermute | solution.py:582
  38.4 14.2 %collective-permute-start.8 = (bf16[4,48,1536]{2,1,0:T(8,128)(2,1)}, bf16[4,48,1536]{2,1,0:T(8,128)(2,1)}, u32[]{:S(2)}, u32[]{:S(2)}) collective-permute-start(bf16[4,48,1536]{2,1,0:T(8,128)(2,1)} %pad_maximum_fusion.4), channel_id=1, source_target_pairs={{0,4},{2,6},{4,0},{6,2},{8,12},{10,14},{12,8},{14,10},{16,20},{18,... | collective-permute-start | bytes 1769480 | tf_op jit(solution)/shard_map/ppermute | solution.py:582
  40.0 18.2 %collective-permute-start.10 = (bf16[8,48,896]{2,1,0:T(8,128)(2,1)S(1)}, bf16[8,48,896]{2,1,0:T(8,128)(2,1)S(1)}, u32[]{:S(2)}, u32[]{:S(2)}) collective-permute-start(bf16[8,48,896]{2,1,0:T(8,128)(2,1)S(1)} %pad_maximum_fusion.3), channel_id=1, source_target_pairs={{0,2},{2,0},{4,6},{6,4},{8,10},{10,8},{12,14},{14,12},{16,18},{18,... | collective-permute-start | bytes 2064392 | tf_op jit(solution)/shard_map/ppermute | solution.py:582
  40.7 77.4 %copy-start.23 = (s32[6]{0:T(128)}, s32[6]{0:T(128)S(1)}, u32[]{:S(2)}) copy-start(s32[6]{0:T(128)S(1)} %pad_add_fusion.info) | copy-start | bytes 76
  48.1 16.8 %collective-permute-start.13 = (bf16[4,48,1920]{2,1,0:T(8,128)(2,1)S(1)}, bf16[4,48,1920]{2,1,0:T(8,128)(2,1)S(1)}, u32[]{:S(2)}, u32[]{:S(2)}) collective-permute-start(bf16[4,48,1920]{2,1,0:T(8,128)(2,1)S(1)} %pad_maximum_fusion.2), channel_id=1, source_target_pairs={{0,8},{2,10},{4,12},{6,14},{8,0},{10,2},{12,4},{14,6},{16,24},{18,... | collective-permute-start | bytes 2211848 | tf_op jit(solution)/shard_map/ppermute | solution.py:582
  58.3 25.6 %collective-permute-start.18 = (bf16[8,48,1536]{2,1,0:T(8,128)(2,1)S(1)}, bf16[8,48,1536]{2,1,0:T(8,128)(2,1)S(1)}, u32[]{:S(2)}, u32[]{:S(2)}) collective-permute-start(bf16[8,48,1536]{2,1,0:T(8,128)(2,1)S(1)} %pad_maximum_fusion.1), channel_id=1, source_target_pairs={{0,2},{2,0},{4,6},{6,4},{8,10},{10,8},{12,14},{14,12},{16,18},{18,... | collective-permute-start | bytes 3538952 | tf_op jit(solution)/shard_map/ppermute | solution.py:582
  60.6 4.5 %collective-permute-start.14 = (bf16[8,48,768]{2,1,0:T(8,128)(2,1)S(1)}, bf16[8,48,768]{2,1,0:T(8,128)(2,1)S(1)}, u32[]{:S(2)}, u32[]{:S(2)}) collective-permute-start(bf16[8,48,768]{2,1,0:T(8,128)(2,1)S(1)} %pad_maximum_fusion.5), channel_id=1, source_target_pairs={{0,1},{1,0},{2,3},{3,2},{4,5},{5,4},{6,7},{7,6},{8,9},{9,8},{10,11... | collective-permute-start | bytes 1769480 | tf_op jit(solution)/shard_map/ppermute | solution.py:586
  60.6 5.1 %collective-permute-start.16 = (bf16[8,48,896]{2,1,0:T(8,128)(2,1)S(1)}, bf16[8,48,896]{2,1,0:T(8,128)(2,1)S(1)}, u32[]{:S(2)}, u32[]{:S(2)}) collective-permute-start(bf16[8,48,896]{2,1,0:T(8,128)(2,1)S(1)} %pad_maximum_fusion.3), channel_id=1, source_target_pairs={{0,1},{1,0},{2,3},{3,2},{4,5},{5,4},{6,7},{7,6},{8,9},{9,8},{10,11... | collective-permute-start | bytes 2064392 | tf_op jit(solution)/shard_map/ppermute | solution.py:586
  61.1 6.1 %collective-permute-start.17 = (bf16[8,48,896]{2,1,0:T(8,128)(2,1)S(1)}, bf16[8,48,896]{2,1,0:T(8,128)(2,1)S(1)}, u32[]{:S(2)}, u32[]{:S(2)}) collective-permute-start(bf16[8,48,896]{2,1,0:T(8,128)(2,1)S(1)} %collective-permute-done.10), channel_id=1, source_target_pairs={{0,1},{1,0},{2,3},{3,2},{4,5},{5,4},{6,7},{7,6},{8,9},{9,8},{10,11... | collective-permute-start | bytes 2064392 | tf_op jit(solution)/shard_map/ppermute | solution.py:586
  64.9 2.2 collective-permute-start.15
  65.1 15.5 %copy-start.13 = (bf16[8,48,768]{2,1,0:T(8,128)(2,1)}, bf16[8,48,768]{2,1,0:T(8,128)(2,1)S(1)}, u32[]{:S(2)}) copy-start(bf16[8,48,768]{2,1,0:T(8,128)(2,1)S(1)} %collective-permute-done.14) | copy-start | bytes 1769476
  65.1 34.8 %collective-permute-start.21 = (bf16[8,48,1920]{2,1,0:T(8,128)(2,1)S(1)}, bf16[8,48,1920]{2,1,0:T(8,128)(2,1)S(1)}, u32[]{:S(2)}, u32[]{:S(2)}) collective-permute-start(bf16[8,48,1920]{2,1,0:T(8,128)(2,1)S(1)} %pad_maximum_fusion), channel_id=1, source_target_pairs={{0,4},{2,6},{4,0},{6,2},{8,12},{10,14},{12,8},{14,10},{16,20},{18,... | collective-permute-start | bytes 4423688 | tf_op jit(solution)/shard_map/ppermute | solution.py:582
  65.7 14.9 %copy-start.3 = (bf16[8,48,896]{2,1,0:T(8,128)(2,1)}, bf16[8,48,896]{2,1,0:T(8,128)(2,1)S(1)}, u32[]{:S(2)}) copy-start(bf16[8,48,896]{2,1,0:T(8,128)(2,1)S(1)} %collective-permute-done.16) | copy-start | bytes 2064388
  65.7 18.7 %collective-permute-start.19 = (bf16[8,48,1536]{2,1,0:T(8,128)(2,1)S(1)}, bf16[8,48,1536]{2,1,0:T(8,128)(2,1)S(1)}, u32[]{:S(2)}, u32[]{:S(2)}) collective-permute-start(bf16[8,48,1536]{2,1,0:T(8,128)(2,1)S(1)} %pad_maximum_fusion.1), channel_id=1, source_target_pairs={{0,1},{1,0},{2,3},{3,2},{4,5},{5,4},{6,7},{7,6},{8,9},{9,8},{10,11... | collective-permute-start | bytes 3538952 | tf_op jit(solution)/shard_map/ppermute | solution.py:586
  67.1 13.5 %copy-start.15 = (bf16[8,48,768]{2,1,0:T(8,128)(2,1)}, bf16[8,48,768]{2,1,0:T(8,128)(2,1)S(1)}, u32[]{:S(2)}) copy-start(bf16[8,48,768]{2,1,0:T(8,128)(2,1)S(1)} %collective-permute-done.15) | copy-start | bytes 1769476
  67.1 13.5 %copy-start.5 = (bf16[8,48,896]{2,1,0:T(8,128)(2,1)}, bf16[8,48,896]{2,1,0:T(8,128)(2,1)S(1)}, u32[]{:S(2)}) copy-start(bf16[8,48,896]{2,1,0:T(8,128)(2,1)S(1)} %collective-permute-done.17) | copy-start | bytes 2064388
  80.6 19.8 %copy-start.19 = (bf16[512,384]{1,0:T(8,128)(2,1)}, bf16[512,384]{1,0:T(8,128)(2,1)S(1)}, u32[]{:S(2)}) copy-start(bf16[512,384]{1,0:T(8,128)(2,1)S(1)} %get-tuple-element.152.att_other) | copy-start | bytes 1179652
  83.9 2.8 %collective-permute-start.20 = (bf16[8,48,1536]{2,1,0:T(8,128)(2,1)S(1)}, bf16[8,48,1536]{2,1,0:T(8,128)(2,1)S(1)}, u32[]{:S(2)}, u32[]{:S(2)}) collective-permute-start(bf16[8,48,1536]{2,1,0:T(8,128)(2,1)S(1)} %collective-permute-done.18), channel_id=1, source_target_pairs={{0,1},{1,0},{2,3},{3,2},{4,5},{5,4},{6,7},{7,6},{8,9},{9,8},{10,11... | collective-permute-start | bytes 3538952 | tf_op jit(solution)/shard_map/ppermute | solution.py:586
  83.9 17.0 %collective-permute-start.22 = (bf16[8,48,1920]{2,1,0:T(8,128)(2,1)S(1)}, bf16[8,48,1920]{2,1,0:T(8,128)(2,1)S(1)}, u32[]{:S(2)}, u32[]{:S(2)}) collective-permute-start(bf16[8,48,1920]{2,1,0:T(8,128)(2,1)S(1)} %pad_maximum_fusion), channel_id=1, source_target_pairs={{0,1},{1,0},{2,3},{3,2},{4,5},{5,4},{6,7},{7,6},{8,9},{9,8},{10,11... | collective-permute-start | bytes 4423688 | tf_op jit(solution)/shard_map/ppermute | solution.py:586
  86.7 13.2 %copy-start.33 = (bf16[3]{0:T(256)(128)(2,1)S(1)}, bf16[3]{0:T(256)(128)(2,1)}, u32[]{:S(2)}) copy-start(bf16[3]{0:T(256)(128)(2,1)} %param.39) | copy-start | bytes 22
  86.7 16.4 %copy-start.25 = (bf16[2,1,512,768]{3,2,1,0:T(8,128)(2,1)S(1)}, bf16[2,1,512,768]{3,2,1,0:T(8,128)(2,1)}, u32[]{:S(2)}) copy-start(bf16[2,1,512,768]{3,2,1,0:T(8,128)(2,1)} %param.23) | copy-start | bytes 4718596
  92.9 19.4 %copy-start.26 = (bf16[512,1536]{1,0:T(8,128)(2,1)}, bf16[512,1536]{1,0:T(8,128)(2,1)S(1)}, u32[]{:S(2)}) copy-start(bf16[512,1536]{1,0:T(8,128)(2,1)S(1)} %get-tuple-element.148.active.right) | copy-start | bytes 4718596
  99.8 3.3 %collective-permute-start.23 = (bf16[8,48,1920]{2,1,0:T(8,128)(2,1)S(1)}, bf16[8,48,1920]{2,1,0:T(8,128)(2,1)S(1)}, u32[]{:S(2)}, u32[]{:S(2)}) collective-permute-start(bf16[8,48,1920]{2,1,0:T(8,128)(2,1)S(1)} %collective-permute-done.21), channel_id=1, source_target_pairs={{0,1},{1,0},{2,3},{3,2},{4,5},{5,4},{6,7},{7,6},{8,9},{9,8},{10,11... | collective-permute-start | bytes 4423688 | tf_op jit(solution)/shard_map/ppermute | solution.py:586
  99.9 13.0 %collective-permute-start.25 = (bf16[768,512]{1,0:T(8,128)(2,1)S(1)}, bf16[768,512]{1,0:T(8,128)(2,1)S(1)}, u32[]{:S(2)}, u32[]{:S(2)}) collective-permute-start(bf16[768,512]{1,0:T(8,128)(2,1)S(1)} %get-tuple-element.160.first_p.left), channel_id=1, source_target_pairs={{0,1},{1,0},{2,3},{3,2},{4,5},{5,4},{6,7},{7,6},{8,9},{9,8},{10,11... | collective-permute-start | bytes 2359304 | tf_op jit(solution)/shard_map/ppermute | solution.py:586
  100.4 12.5 %collective-permute-start.26 = (bf16[512,384]{1,0:T(8,128)(2,1)S(1)}, bf16[512,384]{1,0:T(8,128)(2,1)S(1)}, u32[]{:S(2)}, u32[]{:S(2)}) collective-permute-start(bf16[512,384]{1,0:T(8,128)(2,1)S(1)} %get-tuple-element.152.att_other), channel_id=1, source_target_pairs={{0,1},{1,0},{2,3},{3,2},{4,5},{5,4},{6,7},{7,6},{8,9},{9,8},{10,11... | collective-permute-start | bytes 1179656 | tf_op jit(solution)/shard_map/ppermute | solution.py:586
  100.4 12.4 %collective-permute-start.24 = (bf16[512,1536]{1,0:T(8,128)(2,1)S(1)}, bf16[512,1536]{1,0:T(8,128)(2,1)S(1)}, u32[]{:S(2)}, u32[]{:S(2)}) collective-permute-start(bf16[512,1536]{1,0:T(8,128)(2,1)S(1)} %get-tuple-element.149.other_active), channel_id=1, source_target_pairs={{0,1},{1,0},{2,3},{3,2},{4,5},{5,4},{6,7},{7,6},{8,9},{9,8},{10,11... | collective-permute-start | bytes 4718600 | tf_op jit(solution)/shard_map/ppermute | solution.py:586
  112.3 5.9 %collective-permute-start.27 = (f32[8,768]{1,0:T(8,128)}, f32[8,768]{1,0:T(8,128)}, u32[]{:S(2)}, u32[]{:S(2)}) collective-permute-start(f32[8,768]{1,0:T(8,128)} %get-tuple-element.157.ramp), channel_id=1, source_target_pairs={{0,1},{1,0},{2,3},{3,2},{4,5},{5,4},{6,7},{7,6},{8,9},{9,8},{10,11... | collective-permute-start | bytes 73736 | tf_op jit(solution)/shard_map/ppermute | solution.py:586
  112.5 5.7 %collective-permute-start.28 = (bf16[768,512]{1,0:T(8,128)(2,1)}, bf16[768,512]{1,0:T(8,128)(2,1)}, u32[]{:S(2)}, u32[]{:S(2)}) collective-permute-start(bf16[768,512]{1,0:T(8,128)(2,1)} %get-tuple-element.158.left_in), channel_id=1, source_target_pairs={{0,1},{1,0},{2,3},{3,2},{4,5},{5,4},{6,7},{7,6},{8,9},{9,8},{10,11... | collective-permute-start | bytes 2359304 | tf_op jit(solution)/shard_map/ppermute | solution.py:586
  118.0 5.1 %collective-permute-start.29 = (bf16[512,1536]{1,0:T(8,128)(2,1)}, bf16[512,1536]{1,0:T(8,128)(2,1)}, u32[]{:S(2)}, u32[]{:S(2)}) collective-permute-start(bf16[512,1536]{1,0:T(8,128)(2,1)} %get-tuple-element.161.other_delta), channel_id=1, source_target_pairs={{0,1},{1,0},{2,3},{3,2},{4,5},{5,4},{6,7},{7,6},{8,9},{9,8},{10,11... | collective-permute-start | bytes 4718600 | tf_op jit(solution)/shard_map/ppermute | solution.py:586
  127.5 11.4 %collective-permute-start.30 = (bf16[512,768]{1,0:T(8,128)(2,1)S(1)}, bf16[512,768]{1,0:T(8,128)(2,1)S(1)}, u32[]{:S(2)}, u32[]{:S(2)}) collective-permute-start(bf16[512,768]{1,0:T(8,128)(2,1)S(1)} %get-tuple-element.176.block_own), channel_id=1, source_target_pairs={{0,1},{1,0},{2,3},{3,2},{4,5},{5,4},{6,7},{7,6},{8,9},{9,8},{10,11... | collective-permute-start | bytes 2359304 | tf_op jit(solution)/shard_map/ppermute | solution.py:586
  127.9 28.0 %collective-permute-start.33 = (bf16[8,48,1536]{2,1,0:T(8,128)(2,1)S(1)}, bf16[8,48,1536]{2,1,0:T(8,128)(2,1)S(1)}, u32[]{:S(2)}, u32[]{:S(2)}) collective-permute-start(bf16[8,48,1536]{2,1,0:T(8,128)(2,1)S(1)} %bitcast.121), channel_id=1, source_target_pairs={{0,2},{2,0},{4,6},{6,4},{8,10},{10,8},{12,14},{14,12},{16,18},{18,... | collective-permute-start | bytes 3538952 | tf_op jit(solution)/shard_map/ppermute | solution.py:582
  127.9 32.2 %collective-permute-start.36 = (bf16[400,1536]{1,0:T(8,128)(2,1)S(1)}, bf16[400,1536]{1,0:T(8,128)(2,1)S(1)}, u32[]{:S(2)}, u32[]{:S(2)}) collective-permute-start(bf16[400,1536]{1,0:T(8,128)(2,1)S(1)} %get-tuple-element.196), channel_id=1, source_target_pairs={{0,4},{2,6},{4,0},{6,2},{8,12},{10,14},{12,8},{14,10},{16,20},{18,... | collective-permute-start | bytes 3686408 | tf_op jit(solution)/shard_map/ppermute | solution.py:582
  138.8 14.2 %collective-permute-start.32 = (bf16[768,512]{1,0:T(8,128)(2,1)S(1)}, bf16[768,512]{1,0:T(8,128)(2,1)S(1)}, u32[]{:S(2)}, u32[]{:S(2)}) collective-permute-start(bf16[768,512]{1,0:T(8,128)(2,1)S(1)} %get-tuple-element.185.branch_t), channel_id=1, source_target_pairs={{0,1},{1,0},{2,3},{3,2},{4,5},{5,4},{6,7},{7,6},{8,9},{9,8},{10,11... | collective-permute-start | bytes 2359304 | tf_op jit(solution)/shard_map/ppermute | solution.py:586
  145.8 10.2 %collective-permute-start.34 = (bf16[512,768]{1,0:T(8,128)(2,1)S(1)}, bf16[512,768]{1,0:T(8,128)(2,1)S(1)}, u32[]{:S(2)}, u32[]{:S(2)}) collective-permute-start(bf16[512,768]{1,0:T(8,128)(2,1)S(1)} %get-tuple-element.182.qk_other), channel_id=1, source_target_pairs={{0,1},{1,0},{2,3},{3,2},{4,5},{5,4},{6,7},{7,6},{8,9},{9,8},{10,11... | collective-permute-start | bytes 2359304 | tf_op jit(solution)/shard_map/ppermute | solution.py:586
  146.4 2.0 collective-permute-start.31
  148.4 7.7 %collective-permute-start.35 = (bf16[512,384]{1,0:T(8,128)(2,1)S(1)}, bf16[512,384]{1,0:T(8,128)(2,1)S(1)}, u32[]{:S(2)}, u32[]{:S(2)}) collective-permute-start(bf16[512,384]{1,0:T(8,128)(2,1)S(1)} %get-tuple-element.183.v_other), channel_id=1, source_target_pairs={{0,1},{1,0},{2,3},{3,2},{4,5},{5,4},{6,7},{7,6},{8,9},{9,8},{10,11... | collective-permute-start | bytes 1179656 | tf_op jit(solution)/shard_map/ppermute | solution.py:586
  158.9 16.7 %collective-permute-start.37 = (bf16[8,48,896]{2,1,0:T(8,128)(2,1)S(1)}, bf16[8,48,896]{2,1,0:T(8,128)(2,1)S(1)}, u32[]{:S(2)}, u32[]{:S(2)}) collective-permute-start(bf16[8,48,896]{2,1,0:T(8,128)(2,1)S(1)} %bitcast.122), channel_id=1, source_target_pairs={{0,2},{2,0},{4,6},{6,4},{8,10},{10,8},{12,14},{14,12},{16,18},{18,... | collective-permute-start | bytes 2064392 | tf_op jit(solution)/shard_map/ppermute | solution.py:582
  159.3 16.5 %collective-permute-start.38 = (bf16[8,48,768]{2,1,0:T(8,128)(2,1)S(1)}, bf16[8,48,768]{2,1,0:T(8,128)(2,1)S(1)}, u32[]{:S(2)}, u32[]{:S(2)}) collective-permute-start(bf16[8,48,768]{2,1,0:T(8,128)(2,1)S(1)} %bitcast.123), channel_id=1, source_target_pairs={{0,4},{2,6},{4,0},{6,2},{8,12},{10,14},{12,8},{14,10},{16,20},{18,... | collective-permute-start | bytes 1769480 | tf_op jit(solution)/shard_map/ppermute | solution.py:582
  160.3 18.3 %collective-permute-start.42 = (bf16[208,1536]{1,0:T(8,128)(2,1)S(1)}, bf16[208,1536]{1,0:T(8,128)(2,1)S(1)}, u32[]{:S(2)}, u32[]{:S(2)}) collective-permute-start(bf16[208,1536]{1,0:T(8,128)(2,1)S(1)} %get-tuple-element.213), channel_id=1, source_target_pairs={{0,8},{2,10},{4,12},{6,14},{8,0},{10,2},{12,4},{14,6},{16,24},{18,... | collective-permute-start | bytes 1916936 | tf_op jit(solution)/shard_map/ppermute | solution.py:582
  160.6 18.1 %collective-permute-start.39 = (bf16[512,768]{1,0:T(8,128)(2,1)S(1)}, bf16[512,768]{1,0:T(8,128)(2,1)S(1)}, u32[]{:S(2)}, u32[]{:S(2)}) collective-permute-start(bf16[512,768]{1,0:T(8,128)(2,1)S(1)} %input.1.grad_own), channel_id=1, source_target_pairs={{0,1},{1,0},{2,3},{3,2},{4,5},{5,4},{6,7},{7,6},{8,9},{9,8},{10,11... | collective-permute-start | bytes 2359304 | tf_op jit(solution)/shard_map/ppermute | solution.py:586
  175.8 21.5 %collective-permute-start.43 = (bf16[4,48,1536]{2,1,0:T(8,128)(2,1)S(1)}, bf16[4,48,1536]{2,1,0:T(8,128)(2,1)S(1)}, u32[]{:S(2)}, u32[]{:S(2)}) collective-permute-start(bf16[4,48,1536]{2,1,0:T(8,128)(2,1)S(1)} %get-tuple-element.219), channel_id=1, source_target_pairs={{0,4},{2,6},{4,0},{6,2},{8,12},{10,14},{12,8},{14,10},{16,20},{18,... | collective-permute-start | bytes 1769480 | tf_op jit(solution)/shard_map/ppermute | solution.py:582
  176.4 20.5 %collective-permute-start.41 = (bf16[4,48,896]{2,1,0:T(8,128)(2,1)S(1)}, bf16[4,48,896]{2,1,0:T(8,128)(2,1)S(1)}, u32[]{:S(2)}, u32[]{:S(2)}) collective-permute-start(bf16[4,48,896]{2,1,0:T(8,128)(2,1)S(1)} %get-tuple-element.211), channel_id=1, source_target_pairs={{0,4},{2,6},{4,0},{6,2},{8,12},{10,14},{12,8},{14,10},{16,20},{18,... | collective-permute-start | bytes 1032200 | tf_op jit(solution)/shard_map/ppermute | solution.py:582
  177.9 6.7 %collective-permute-start.40 = (bf16[4,48,768]{2,1,0:T(8,128)(2,1)S(1)}, bf16[4,48,768]{2,1,0:T(8,128)(2,1)S(1)}, u32[]{:S(2)}, u32[]{:S(2)}) collective-permute-start(bf16[4,48,768]{2,1,0:T(8,128)(2,1)S(1)} %get-tuple-element.210), channel_id=1, source_target_pairs={{0,2},{2,0},{4,6},{6,4},{8,10},{10,8},{12,14},{14,12},{16,18},{18,... | collective-permute-start | bytes 884744 | tf_op jit(solution)/shard_map/ppermute | solution.py:582
  178.6 20.6 %collective-permute-start.44 = (bf16[112,1536]{1,0:T(8,128)(2,1)S(1)}, bf16[112,1536]{1,0:T(8,128)(2,1)S(1)}, u32[]{:S(2)}, u32[]{:S(2)}) collective-permute-start(bf16[112,1536]{1,0:T(8,128)(2,1)S(1)} %get-tuple-element.215), channel_id=1, source_target_pairs={{0,16},{2,18},{4,20},{6,22},{8,24},{10,26},{12,28},{14,30},{16,0},... | collective-permute-start | bytes 1032200 | tf_op jit(solution)/shard_map/ppermute | solution.py:582
  196.9 11.8 %collective-permute-start.45 = (bf16[2,48,1664]{2,1,0:T(8,128)(2,1)S(1)}, bf16[2,48,1664]{2,1,0:T(8,128)(2,1)S(1)}, u32[]{:S(2)}, u32[]{:S(2)}) collective-permute-start(bf16[2,48,1664]{2,1,0:T(8,128)(2,1)S(1)} %get-tuple-element.224), channel_id=1, source_target_pairs={{0,8},{2,10},{4,12},{6,14},{8,0},{10,2},{12,4},{14,6},{16,24},{18,... | collective-permute-start | bytes 958472 | tf_op jit(solution)/shard_map/ppermute | solution.py:582
  197.4 14.5 %collective-permute-start.47 = (bf16[2,48,1536]{2,1,0:T(8,128)(2,1)S(1)}, bf16[2,48,1536]{2,1,0:T(8,128)(2,1)S(1)}, u32[]{:S(2)}, u32[]{:S(2)}) collective-permute-start(bf16[2,48,1536]{2,1,0:T(8,128)(2,1)S(1)} %get-tuple-element.229), channel_id=1, source_target_pairs={{0,8},{2,10},{4,12},{6,14},{8,0},{10,2},{12,4},{14,6},{16,24},{18,... | collective-permute-start | bytes 884744 | tf_op jit(solution)/shard_map/ppermute | solution.py:582
  199.2 12.8 %collective-permute-start.46 = (bf16[64,1536]{1,0:T(8,128)(2,1)S(1)}, bf16[64,1536]{1,0:T(8,128)(2,1)S(1)}, u32[]{:S(2)}, u32[]{:S(2)}) collective-permute-start(bf16[64,1536]{1,0:T(8,128)(2,1)S(1)} %get-tuple-element.227), channel_id=1, source_target_pairs={{0,2},{2,0},{4,6},{6,4},{8,10},{10,8},{12,14},{14,12},{16,18},{18,... | collective-permute-start | bytes 589832 | tf_op jit(solution)/shard_map/ppermute | solution.py:582
  208.8 15.0 %copy-start.1 = (bf16[48,768]{1,0:T(8,128)(2,1)S(1)}, bf16[48,768]{1,0:T(8,128)(2,1)}, u32[]{:S(2)}) copy-start(bf16[48,768]{1,0:T(8,128)(2,1)} %param.36) | copy-start | bytes 221188
  208.8 12.7 %collective-permute-start.49 = (bf16[1,48,1664]{2,1,0:T(8,128)(2,1)S(1)}, bf16[1,48,1664]{2,1,0:T(8,128)(2,1)S(1)}, u32[]{:S(2)}, u32[]{:S(2)}) collective-permute-start(bf16[1,48,1664]{2,1,0:T(8,128)(2,1)S(1)} %get-tuple-element.234), channel_id=1, source_target_pairs={{0,16},{2,18},{4,20},{6,22},{8,24},{10,26},{12,28},{14,30},{16,0},... | collective-permute-start | bytes 479240 | tf_op jit(solution)/shard_map/ppermute | solution.py:582
  212.0 8.8 %collective-permute-start.48 = (bf16[1,48,1536]{2,1,0:T(8,128)(2,1)S(1)}, bf16[1,48,1536]{2,1,0:T(8,128)(2,1)S(1)}, u32[]{:S(2)}, u32[]{:S(2)}) collective-permute-start(bf16[1,48,1536]{2,1,0:T(8,128)(2,1)S(1)} %get-tuple-element.232), channel_id=1, source_target_pairs={{0,16},{2,18},{4,20},{6,22},{8,24},{10,26},{12,28},{14,30},{16,0},... | collective-permute-start | bytes 442376 | tf_op jit(solution)/shard_map/ppermute | solution.py:582
  (20 other events, 120.5 us)

commit v2 on v1

--- a/solution.py
+++ b/solution.py
@@ -113,10 +113,9 @@
         if h == 0:
             vec[0:SHARED, b * rows : (b + 1) * rows] = own[0:SHARED, 0:rows]
         at = h * width // 2 + b * part
-        vec[QUERY_B : QUERY_B + 1, at : at + part] = own[PAIR_ROW : PAIR_ROW + 1, 0:part]
-        vec[VALUE_B : VALUE_B + 1, at : at + part] = own[PAIR_ROW : PAIR_ROW + 1, part:rows]
+        vec[QUERY_B : VALUE_B + 1, at : at + part] = own[SHARED : SHARED + 2, 0:part]
         row, at = UP_B + 2 * h + b // (BLOCKS // 2), b % (BLOCKS // 2) * 2 * rows
-        vec[row : row + 1, at : at + 2 * rows] = own[UP_ROW : UP_ROW + 1, 0 : 2 * rows]
+        vec[row : row + 1, at : at + 2 * rows] = own[SHARED + 2 : SHARED + 3, 0 : 2 * rows]
 
 
 def pack_vectors(sums, query, value, up, extra):
@@ -500,7 +499,7 @@
     rows, half = input_out.shape[1:]
     for i in range(3):
         input_out[i] = share[:, i * half : (i + 1) * half]
-    out_out[...] = share[:, 3 * half : 4 * half].T
+    out_out[...] = share[:, 3 * half : 4 * half]
     extra = share[:, 4 * half :]
     for i, target in enumerate(vectors):
         target[...] = extra[i : i + 1, 0:rows]
@@ -508,7 +507,7 @@
     pair_out[1:2, :] = extra[PAIR_ROW : PAIR_ROW + 1, rows // 2 : rows]
     up_out[...] = extra[UP_ROW : UP_ROW + 1, 0 : 2 * rows]
     class_bias_out[...] = extra[CLASS_ROW : CLASS_ROW + 1, 0 : class_bias_out.shape[1]]
-    class_out[...] = extra[:, 0:rows].T[:, len(vectors) : SHARED]
+    class_out[...] = extra[len(vectors) : SHARED, 0:rows]
 
 
 def arrange_kernel(info, block_own, block_other, grad_own, grad_other, block_out, grad_out, held, sems):
@@ -738,9 +737,9 @@
 
     if direct:
         extra = extra_columns(
-            shared[None], input_bias.reshape(1, 1, rows), up_bias.reshape(1, 1, 2 * rows), rows
+            shared[None], input_bias[None], up_bias.reshape(1, 1, 2 * rows), rows
         )
-        b_shard = jnp.concatenate([vo_shard, after(extra, a_shard, d_shard)[0]], 1)
+        b_shard = jnp.concatenate([vo_shard, after(extra, a_shard)[0]], 1)
         a0, b0, u0, d0 = a_shard[None], b_shard[None], u_shard[None], d_shard[None]
         z1, z0 = order_a[0], order_a[1]
         a1, b1, d1 = swap(a0, z1), swap(b0, z1), swap(d0, 1)
@@ -780,7 +779,7 @@
         pair = whole(input_bias, order_a).transpose(1, 0, 2).reshape(2, BLOCKS, block // 2)
         extra = extra_columns(
             shared.transpose(1, 0, 2),
-            pair.transpose(1, 0, 2).reshape(BLOCKS, 1, block),
+            pair.transpose(1, 0, 2),
             whole(up_bias, order_a).reshape(BLOCKS, 1, 2 * block),
             block,
         )
@@ -1048,17 +1047,18 @@
             [VMEM] * 2,
             in_vmem(
                 shape(3, rows, half, dtype=F32),
-                shape(half, rows, dtype=F32),
+                shape(rows, half, dtype=F32),
                 shape(2, rows // 2, dtype=F32),
                 shape(1, 2 * rows, dtype=F32),
                 shape(1, classes, dtype=F32),
-                shape(rows, classes, dtype=F32),
+                shape(classes, rows, dtype=F32),
                 *[shape(1, rows, dtype=F32)] * 7,
             ),
             [],
             0,
             (kept, arrived),
         )
+        out_share, class_grad = out_share.T, class_grad.T
         up_bias_share, class_bias_grad = up_bias_share.reshape(-1), class_bias_grad.reshape(-1)
         vector_grads = [array.reshape(-1) for array in vector_grads]
     else:

time: 228 us -> 226 us (level)
  transfers between devices with their start and end apart: 50 -> 50, of which waited for: 21 -> 22; matrix products, arithmetic and copies ran while one was open for 5% -> 5% of each run, Pallas kernels for 30% -> 30%
where the time goes in v2:
time: 226 us; the launch traced here: 222 us
  waiting for transfers between devices  98.1 us (43%)
  Pallas kernels  72.7 us (32%)
  starting transfers between devices  35.7 us (16%)
  other arithmetic  8.56 us (4%)
  local copies, waits for them, and re-layouts  5.05 us (2%)
    ppermute x30, waiting for transfers between devices, swap(): return lax.ppermute(array, 'dp', [(i, i ^ mask) for i in range(size)])  90.3 us
    pallas_call x25, Pallas kernels, call(): pl.pallas_call(body, name=name, in_specs=in_specs, out_specs=[spec for _,...  72.7 us
    ppermute x30, starting transfers between devices, swap(): return lax.ppermute(array, 'dp', [(i, i ^ mask) for i in range(size)])  31.2 us
    ppermute x20, waiting for transfers between devices, swap_core(): return lax.ppermute(array, 'tensor', [(0, 1), (1, 0)])  7.73 us
    concatenate x12, other arithmetic, join(): return jnp.concatenate([left, right], 0)  4.61 us
    ppermute x20, starting transfers between devices, swap_core(): return lax.ppermute(array, 'tensor', [(0, 1), (1, 0)])  4.54 us
  transfers between devices with their start and end apart: 50, of which 22 were waited for; matrix products, arithmetic and copies ran while one was open for 5% of the time, Pallas kernels for 30%

profile of v2, /device:TPU:0, one launch (start us, length us, event | category | flops | bytes accessed | tf_op | source)
XLA Modules:
  0.0 221.6 jit_solution(18302174818970891375)
XLA Ops:
  0.7 0.9 slice_bitcast_fusion
  1.6 4.1 %collective-permute-start = (bf16[1,48,768]{2,1,0:T(8,128)(2,1)S(1)}, bf16[1,48,768]{2,1,0:T(8,128)(2,1)S(1)}, u32[]{:S(2)}, u32[]{:S(2)}) collective-permute-start(bf16[1,48,768]{2,1,0:T(8,128)(2,1)S(1)} %fusion.6), channel_id=1, source_target_pairs={{0,16},{2,18},{4,20},{6,22},{8,24},{10,26},{12,28},{14,30},{16,0},... | collective-permute-start | bytes 221192 | tf_op jit(solution)/shard_map/ppermute | solution.py:581
  5.7 1.6 concatenate.61
  7.2 0.7 fusion.5
  7.9 0.8 maximum_bitcast_fusion.1
  8.8 0.8 collective-permute-done
  9.6 1.2 collective-permute-start.3
  10.8 4.4 %collective-permute-done.1 = bf16[1,48,896]{2,1,0:T(8,128)(2,1)S(1)} collective-permute-done((bf16[1,48,896]{2,1,0:T(8,128)(2,1)S(1)}, bf16[1,48,896]{2,1,0:T(8,128)(2,1)S(1)}, u32[]{:S(2)}, u32[]{:S(2)}) %collective-permute-start.1) | collective-permute-done | bytes 86048 | tf_op jit(solution)/shard_map/ppermute | solution.py:581
  15.3 0.9 maximum_bitcast_fusion
  16.2 1.8 collective-permute-start.11
  18.0 2.0 collective-permute-start.4
  20.0 1.6 collective-permute-start.6
  22.2 2.6 %collective-permute-done.4 = bf16[2,48,896]{2,1,0:T(8,128)(2,1)S(1)} collective-permute-done((bf16[2,48,896]{2,1,0:T(8,128)(2,1)S(1)}, bf16[2,48,896]{2,1,0:T(8,128)(2,1)S(1)}, u32[]{:S(2)}, u32[]{:S(2)}) %collective-permute-start.4) | collective-permute-done | bytes 172064 | tf_op jit(solution)/shard_map/ppermute | solution.py:581
  25.5 0.8 pad_maximum_fusion.6
  26.3 1.5 collective-permute-start.7
  27.8 2.2 collective-permute-start.12
  30.1 1.5 collective-permute-start.9
  31.6 5.0 %collective-permute-done.5 = bf16[2,48,1536]{2,1,0:T(8,128)(2,1)S(1)} collective-permute-done((bf16[2,48,1536]{2,1,0:T(8,128)(2,1)S(1)}, bf16[2,48,1536]{2,1,0:T(8,128)(2,1)S(1)}, u32[]{:S(2)}, u32[]{:S(2)}) %collective-permute-start.5) | collective-permute-done | bytes 294944 | tf_op jit(solution)/shard_map/ppermute | solution.py:581
  36.6 0.9 pad_maximum_fusion.4
  37.5 1.8 collective-permute-start.8
  39.8 1.9 prepare.1
  41.8 4.3 %collective-permute-done.12 = bf16[2,48,1920]{2,1,0:T(8,128)(2,1)} collective-permute-done((bf16[2,48,1920]{2,1,0:T(8,128)(2,1)}, bf16[2,48,1920]{2,1,0:T(8,128)(2,1)}, u32[]{:S(2)}, u32[]{:S(2)}) %collective-permute-start.12) | collective-permute-done | bytes 368672 | tf_op jit(solution)/shard_map/ppermute | solution.py:581
  46.1 1.2 pad_maximum_fusion.2
  47.3 4.4 %collective-permute-done.8 = bf16[4,48,1536]{2,1,0:T(8,128)(2,1)} collective-permute-done((bf16[4,48,1536]{2,1,0:T(8,128)(2,1)}, bf16[4,48,1536]{2,1,0:T(8,128)(2,1)}, u32[]{:S(2)}, u32[]{:S(2)}) %collective-permute-start.8) | collective-permute-done | bytes 589856 | tf_op jit(solution)/shard_map/ppermute | solution.py:581
  51.7 1.3 pad_maximum_fusion.1
  53.0 4.5 %collective-permute-done.10 = bf16[8,48,896]{2,1,0:T(8,128)(2,1)S(1)} collective-permute-done((bf16[8,48,896]{2,1,0:T(8,128)(2,1)S(1)}, bf16[8,48,896]{2,1,0:T(8,128)(2,1)S(1)}, u32[]{:S(2)}, u32[]{:S(2)}) %collective-permute-start.10) | collective-permute-done | bytes 688160 | tf_op jit(solution)/shard_map/ppermute | solution.py:581
  57.5 2.3 %collective-permute-start.18 = (bf16[8,48,1536]{2,1,0:T(8,128)(2,1)S(1)}, bf16[8,48,1536]{2,1,0:T(8,128)(2,1)S(1)}, u32[]{:S(2)}, u32[]{:S(2)}) collective-permute-start(bf16[8,48,1536]{2,1,0:T(8,128)(2,1)S(1)} %pad_maximum_fusion.1), channel_id=1, source_target_pairs={{0,2},{2,0},{4,6},{6,4},{8,10},{10,8},{12,14},{14,12},{16,18},{18,... | collective-permute-start | bytes 3538952 | tf_op jit(solution)/shard_map/ppermute | solution.py:581
  60.4 3.6 %collective-permute-done.13 = bf16[4,48,1920]{2,1,0:T(8,128)(2,1)S(1)} collective-permute-done((bf16[4,48,1920]{2,1,0:T(8,128)(2,1)S(1)}, bf16[4,48,1920]{2,1,0:T(8,128)(2,1)S(1)}, u32[]{:S(2)}, u32[]{:S(2)}) %collective-permute-start.13) | collective-permute-done | bytes 737312 | tf_op jit(solution)/shard_map/ppermute | solution.py:581
  65.0 1.2 collective-permute-done.15
  66.2 13.4 %attend.1 = (bf16[512,768]{1,0:T(8,128)(2,1)S(1)}, bf16[512,768]{1,0:T(8,128)(2,1)S(1)}, bf16[512,768]{1,0:T(8,128)(2,1)S(1)}, bf16[512,384]{1,0:T(8,128)(2,1)S(...) custom-call(s32[6]{0:T(128)S(1)} %pad_add_fusion.info, ...), custom_call_target="tpu_custom_call" | custom-call | bytes 1024 | tf_op jit(solution)/shard_map/attend/pallas_call | solution.py:552
  79.7 3.3 %collective-permute-done.18 = bf16[8,48,1536]{2,1,0:T(8,128)(2,1)S(1)} collective-permute-done((bf16[8,48,1536]{2,1,0:T(8,128)(2,1)S(1)}, bf16[8,48,1536]{2,1,0:T(8,128)(2,1)S(1)}, u32[]{:S(2)}, u32[]{:S(2)}) %collective-permute-start.18) | collective-permute-done | bytes 1179680 | tf_op jit(solution)/shard_map/ppermute | solution.py:581
  83.5 2.3 %collective-permute-done.20 = bf16[8,48,1536]{2,1,0:T(8,128)(2,1)S(1)} collective-permute-done((bf16[8,48,1536]{2,1,0:T(8,128)(2,1)S(1)}, bf16[8,48,1536]{2,1,0:T(8,128)(2,1)S(1)}, u32[]{:S(2)}, u32[]{:S(2)}) %collective-permute-start.20) | collective-permute-done | bytes 1179680 | tf_op jit(solution)/shard_map/ppermute | solution.py:585
  85.8 6.1 %up.1 = (bf16[512,1536]{1,0:T(8,128)(2,1)S(1)}, bf16[512,1536]{1,0:T(8,128)(2,1)S(1)}, bf16[512,3072]{1,0:T(8,128)(2,1)S(1)}) custom-call(f32[16,768]{1,0:T(8,128)S(1)} %get-tuple-element.145.vec, bf16[768,512]{1,0:T(8,128)(2,1)S(1)} %get-tuple-element.160.first_p.left, bf16[384,1536]{1,0:T(8,128)(2,1)S(1)} %bitcast.83, bf16[384,1536]{1,0:T(8,128)(2,1)S(1)} %bitcast.98, ...), custom_call_target="tpu_custom_call" | custom-call | bytes 1024 | tf_op jit(solution)/shard_map/up/pallas_call | solution.py:552
  92.0 6.9 %collective-permute-done.21 = bf16[8,48,1920]{2,1,0:T(8,128)(2,1)S(1)} collective-permute-done((bf16[8,48,1920]{2,1,0:T(8,128)(2,1)S(1)}, bf16[8,48,1920]{2,1,0:T(8,128)(2,1)S(1)}, u32[]{:S(2)}, u32[]{:S(2)}) %collective-permute-start.21) | collective-permute-done | bytes 1474592 | tf_op jit(solution)/shard_map/ppermute | solution.py:581
  100.0 2.2 %collective-permute-done.23 = bf16[8,48,1920]{2,1,0:T(8,128)(2,1)S(1)} collective-permute-done((bf16[8,48,1920]{2,1,0:T(8,128)(2,1)S(1)}, bf16[8,48,1920]{2,1,0:T(8,128)(2,1)S(1)}, u32[]{:S(2)}, u32[]{:S(2)}) %collective-permute-start.23) | collective-permute-done | bytes 1474592 | tf_op jit(solution)/shard_map/ppermute | solution.py:585
  102.2 9.1 %ramp.1 = (bf16[512,768]{1,0:T(8,128)(2,1)S(1)}, f32[8,768]{1,0:T(8,128)}, bf16[768,512]{1,0:T(8,128)(2,1)S(1)}, bf16[768,512]{1,0:T(8,128)(2,1)}, f32[512,768]{1,0:T(8,128)S(1)}, /*index=5*/f32[8,768]{1,0:T(8,128)S(1)}) custom-call(s32[6]{0:T(128)S(1)} %pad_add_fusion.info, f32[3]{0:T(128)S(1)} %convert_element_type.20.class_bias, ...), custom_call_target="tpu_custom_call" | custom-call | flops 17250000896 | bytes 1024 | tf_op jit(solution)/shard_map/ramp/pallas_call | solution.py:552
  111.9 1.2 copy-done.28
  113.1 3.9 %hidden.1 = (bf16[512,1536]{1,0:T(8,128)(2,1)S(1)}, bf16[512,1536]{1,0:T(8,128)(2,1)}) custom-call(bf16[768,512]{1,0:T(8,128)(2,1)S(1)} %get-tuple-element.153.feed_r, bf16[512,3072]{1,0:T(8,128)(2,1)S(1)} %get-tuple-element.154.slope, bf16[384,1920]{1,0:T(8,128)(2,1)S(1)} %bitcast.110, bf16[384,1920]{1,0:T(8,128)(2,1)S(1)} %bitcast.117, ...), custom_call_target="tpu_custom_call" | custom-call | flops 460000002048 | bytes 1024 | tf_op jit(solution)/shard_map/hidden/pallas_call | solution.py:552
  117.3 4.8 %down_grad.1 = (bf16[384,1536]{1,0:T(8,128)(2,1)S(1)}, bf16[400,1536]{1,0:T(8,128)(2,1)S(1)}, f32[2,3]{1,0:T(2,128)}) custom-call(s32[6]{0:T(128)S(1)} %pad_add_fusion.info, f32[8,768]{1,0:T(8,128)} %get-tuple-element.157.ramp, f32[8,768]{1,0:T(8,128)} %collective-permute-done.27.ramp_other, bf16[768,512]{1,0:T(8,128)(2,1)} %get-tuple-element.158.left_in, ...), custom_call_target="tpu_custom_call" | custom-call | flops 460000002048 | bytes 1024 | tf_op jit(solution)/shard_map/down_grad/pallas_call | solution.py:552
  122.2 4.3 %up_grad.1 = (bf16[384,1536]{1,0:T(8,128)(2,1)S(1)}, bf16[384,1536]{1,0:T(8,128)(2,1)S(1)}, f32[1,1536]{1,0:T(1,128)S(1)}) custom-call(bf16[768,512]{1,0:T(8,128)(2,1)S(1)} %get-tuple-element.160.first_p.left, bf16[768,512]{1,0:T(8,128)(2,1)S(1)} %copy-done.18, bf16[512,1536]{1,0:T(8,128)(2,1)S(1)} %get-tuple-element.155.right.delta, ...), custom_call_target="tpu_custom_call" | custom-call | bytes 1024 | tf_op jit(solution)/shard_map/up_grad/pallas_call | solution.py:552
  127.0 1.4 collective-permute-start.36
  128.4 1.3 copy-done.12
  129.7 8.5 %branch.1 = (f32[512,768]{1,0:T(8,128)S(1)}, bf16[512,768]{1,0:T(8,128)(2,1)S(1)}, bf16[768,512]{1,0:T(8,128)(2,1)S(1)}, f32[16,768]{1,0:T(8,128)S(1)}) custom-call(s32[6]{0:T(128)S(1)} %copy-done.24, f32[16,768]{1,0:T(8,128)S(1)} %get-tuple-element.145.vec, f32[8,768]{1,0:T(8,128)S(1)} %get-tuple-element.164.sums_in, ...), custom_call_target="tpu_custom_call" | custom-call | bytes 1024 | tf_op jit(solution)/shard_map/branch/pallas_call | solution.py:552
  138.3 6.9 %back.1 = (bf16[512,768]{1,0:T(8,128)(2,1)S(1)}, bf16[512,384]{1,0:T(8,128)(2,1)S(1)}, bf16[512,768]{1,0:T(8,128)(2,1)S(1)}, bf16[512,384]{1,0:T(8,128)(2,1)S(1)}) custom-call(bf16[512,768]{1,0:T(8,128)(2,1)S(1)} %get-tuple-element.169.q, bf16[512,768]{1,0:T(8,128)(2,1)S(1)} %get-tuple-element.170.k, bf16[512,768]{1,0:T(8,128)(2,1)S(1)} %get-tuple-element.171.v, ...), custom_call_target="tpu_custom_call" | custom-call | bytes 1024 | tf_op jit(solution)/shard_map/back/pallas_call | solution.py:552
  145.8 1.9 collective-permute-done.31.sums_other
  148.1 4.2 %input.1.grad_own = bf16[512,768]{1,0:T(8,128)(2,1)S(1)} custom-call(s32[6]{0:T(128)S(1)} %copy-done.24, bf16[512,768]{1,0:T(8,128)(2,1)S(1)} %get-tuple-element.179.qk_own.qk, bf16[512,384]{1,0:T(8,128)(2,1)S(1)} %get-tuple-element.181.v_own.values, bf16[512,768]{1,0:T(8,128)(2,1)S(1)} %get-tuple-element.182.qk_other, ...), custom_call_target="tpu_custom_call" | custom-call | bytes 1024 | tf_op jit(solution)/shard_map/input/pallas_call | solution.py:552
  152.4 1.0 out_grad.1
  153.4 1.6 collective-permute-done.33.refs_1_
  155.1 2.9 %input_grad.1 = (bf16[384,768]{1,0:T(8,128)(2,1)S(1)}, bf16[384,768]{1,0:T(8,128)(2,1)S(1)}, bf16[384,896]{1,0:T(8,128)(2,1)S(1)}, bf16[384,896]{1,0:T(8,128)(2,1)S(1)}) custom-call(s32[6]{0:T(128)S(1)} %copy-done.24, f32[16,768]{1,0:T(8,128)S(1)} %get-tuple-element.180.sums_in, f32[16,768]{1,0:T(8,128)S(1)} %collective-permute-done.31.sums_other, ...), custom_call_target="tpu_custom_call" | custom-call | bytes 1024 | tf_op jit(solution)/shard_map/input_grad/pallas_call | solution.py:552
  158.4 1.1 collective-permute-start.38
  160.0 14.7 %collective-permute-done.37.refs_1_ = bf16[8,48,896]{2,1,0:T(8,128)(2,1)S(1)} collective-permute-done((bf16[8,48,896]{2,1,0:T(8,128)(2,1)S(1)}, bf16[8,48,896]{2,1,0:T(8,128)(2,1)S(1)}, u32[]{:S(2)}, u32[]{:S(2)}) %collective-permute-start.37) | collective-permute-done | bytes 688160 | tf_op jit(solution)/shard_map/ppermute | solution.py:581
  175.5 1.5 collective-permute-start.41
  177.9 2.5 %arrange.1 = (bf16[2,512,768]{2,1,0:T(8,128)(2,1)}, bf16[2,512,768]{2,1,0:T(8,128)(2,1)}) custom-call(s32[6]{0:T(128)S(1)} %copy-done.24, bf16[512,768]{1,0:T(8,128)(2,1)S(1)} %get-tuple-element.176.block_own, bf16[512,768]{1,0:T(8,128)(2,1)S(1)} %collective-permute-done.30.block_other, bf16[512,768]{1,0:T(8,128)(2,1)S(1)} %input.1.grad_own, ...), custom_call_target="tpu_custom_call" | custom-call | bytes 1024 | tf_op jit(solution)/shard_map/arrange/pallas_call | solution.py:552
  180.4 3.3 %collective-permute-done.40.refs_1_ = bf16[4,48,768]{2,1,0:T(8,128)(2,1)S(1)} collective-permute-done((bf16[4,48,768]{2,1,0:T(8,128)(2,1)S(1)}, bf16[4,48,768]{2,1,0:T(8,128)(2,1)S(1)}, u32[]{:S(2)}, u32[]{:S(2)}) %collective-permute-start.40) | collective-permute-done | bytes 294944 | tf_op jit(solution)/shard_map/ppermute | solution.py:581
  183.7 12.2 %collective-permute-done.41.refs_3_ = bf16[4,48,896]{2,1,0:T(8,128)(2,1)S(1)} collective-permute-done((bf16[4,48,896]{2,1,0:T(8,128)(2,1)S(1)}, bf16[4,48,896]{2,1,0:T(8,128)(2,1)S(1)}, u32[]{:S(2)}, u32[]{:S(2)}) %collective-permute-start.41) | collective-permute-done | bytes 344096 | tf_op jit(solution)/shard_map/ppermute | solution.py:581
  196.5 1.8 collective-permute-start.47
  198.3 1.0 collective-permute-start.46
  199.3 8.5 %collective-permute-done.45.refs_1_ = bf16[2,48,1664]{2,1,0:T(8,128)(2,1)S(1)} collective-permute-done((bf16[2,48,1664]{2,1,0:T(8,128)(2,1)S(1)}, bf16[2,48,1664]{2,1,0:T(8,128)(2,1)S(1)}, u32[]{:S(2)}, u32[]{:S(2)}) %collective-permute-start.45) | collective-permute-done | bytes 319520 | tf_op jit(solution)/shard_map/ppermute | solution.py:581
  208.0 3.0 %collective-permute-done.47.refs_1_ = bf16[2,48,1536]{2,1,0:T(8,128)(2,1)S(1)} collective-permute-done((bf16[2,48,1536]{2,1,0:T(8,128)(2,1)S(1)}, bf16[2,48,1536]{2,1,0:T(8,128)(2,1)S(1)}, u32[]{:S(2)}, u32[]{:S(2)}) %collective-permute-start.47) | collective-permute-done | bytes 294944 | tf_op jit(solution)/shard_map/ppermute | solution.py:581
  211.1 0.7 convert_bitcast_fusion
  211.9 1.5 ramp_grad.1
  213.4 6.5 %collective-permute-done.48 = bf16[1,48,1536]{2,1,0:T(8,128)(2,1)S(1)} collective-permute-done((bf16[1,48,1536]{2,1,0:T(8,128)(2,1)S(1)}, bf16[1,48,1536]{2,1,0:T(8,128)(2,1)S(1)}, u32[]{:S(2)}, u32[]{:S(2)}) %collective-permute-start.48) | collective-permute-done | bytes 147488 | tf_op jit(solution)/shard_map/ppermute | solution.py:581
  219.9 0.7 fusion.7
  220.6 0.8 finish.1
  (158 shorter events, 11.1 us)
Async XLA Ops:
  0.7 21.5 %copy-start.30 = (bf16[48,1536]{1,0:T(8,128)(2,1)S(1)}, bf16[48,1536]{1,0:T(8,128)(2,1)}, u32[]{:S(2)}) copy-start(bf16[48,1536]{1,0:T(8,128)(2,1)} %param.30) | copy-start | bytes 442372
  1.6 8.0 %collective-permute-start = (bf16[1,48,768]{2,1,0:T(8,128)(2,1)S(1)}, bf16[1,48,768]{2,1,0:T(8,128)(2,1)S(1)}, u32[]{:S(2)}, u32[]{:S(2)}) collective-permute-start(bf16[1,48,768]{2,1,0:T(8,128)(2,1)S(1)} %fusion.6), channel_id=1, source_target_pairs={{0,16},{2,18},{4,20},{6,22},{8,24},{10,26},{12,28},{14,30},{16,0},... | collective-permute-start | bytes 221192 | tf_op jit(solution)/shard_map/ppermute | solution.py:581
  8.7 6.5 %collective-permute-start.1 = (bf16[1,48,896]{2,1,0:T(8,128)(2,1)S(1)}, bf16[1,48,896]{2,1,0:T(8,128)(2,1)S(1)}, u32[]{:S(2)}, u32[]{:S(2)}) collective-permute-start(bf16[1,48,896]{2,1,0:T(8,128)(2,1)S(1)} %maximum_bitcast_fusion.1), channel_id=1, source_target_pairs={{0,16},{2,18},{4,20},{6,22},{8,24},{10,26},{12,28},{14,30},{16,0},... | collective-permute-start | bytes 258056 | tf_op jit(solution)/shard_map/ppermute | solution.py:581
  9.6 10.4 %collective-permute-start.3 = (bf16[2,48,768]{2,1,0:T(8,128)(2,1)S(1)}, bf16[2,48,768]{2,1,0:T(8,128)(2,1)S(1)}, u32[]{:S(2)}, u32[]{:S(2)}) collective-permute-start(bf16[2,48,768]{2,1,0:T(8,128)(2,1)S(1)} %pad_maximum_fusion.11), channel_id=1, source_target_pairs={{0,8},{2,10},{4,12},{6,14},{8,0},{10,2},{12,4},{14,6},{16,24},{18,... | collective-permute-start | bytes 442376 | tf_op jit(solution)/shard_map/ppermute | solution.py:581
  15.2 7.0 %collective-permute-start.2 = (bf16[1,48,1536]{2,1,0:T(8,128)(2,1)}, bf16[1,48,1536]{2,1,0:T(8,128)(2,1)S(1)}, u32[]{:S(2)}, u32[]{:S(2)}) collective-permute-start(bf16[1,48,1536]{2,1,0:T(8,128)(2,1)} %bitcast.128), channel_id=1, source_target_pairs={{0,16},{2,18},{4,20},{6,22},{8,24},{10,26},{12,28},{14,30},{16,0},... | collective-permute-start | bytes 442376 | tf_op jit(solution)/shard_map/ppermute | solution.py:581
  16.2 9.3 %collective-permute-start.11 = (bf16[1,48,1920]{2,1,0:T(8,128)(2,1)S(1)}, bf16[1,48,1920]{2,1,0:T(8,128)(2,1)S(1)}, u32[]{:S(2)}, u32[]{:S(2)}) collective-permute-start(bf16[1,48,1920]{2,1,0:T(8,128)(2,1)S(1)} %maximum_bitcast_fusion), channel_id=1, source_target_pairs={{0,2},{2,0},{4,6},{6,4},{8,10},{10,8},{12,14},{14,12},{16,18},{18,... | collective-permute-start | bytes 552968 | tf_op jit(solution)/shard_map/ppermute | solution.py:581
  18.0 6.9 %collective-permute-start.4 = (bf16[2,48,896]{2,1,0:T(8,128)(2,1)S(1)}, bf16[2,48,896]{2,1,0:T(8,128)(2,1)S(1)}, u32[]{:S(2)}, u32[]{:S(2)}) collective-permute-start(bf16[2,48,896]{2,1,0:T(8,128)(2,1)S(1)} %pad_maximum_fusion.10), channel_id=1, source_target_pairs={{0,8},{2,10},{4,12},{6,14},{8,0},{10,2},{12,4},{14,6},{16,24},{18,... | collective-permute-start | bytes 516104 | tf_op jit(solution)/shard_map/ppermute | solution.py:581
  20.0 10.0 %collective-permute-start.6 = (bf16[4,48,768]{2,1,0:T(8,128)(2,1)S(1)}, bf16[4,48,768]{2,1,0:T(8,128)(2,1)S(1)}, u32[]{:S(2)}, u32[]{:S(2)}) collective-permute-start(bf16[4,48,768]{2,1,0:T(8,128)(2,1)S(1)} %pad_maximum_fusion.9), channel_id=1, source_target_pairs={{0,4},{2,6},{4,0},{6,2},{8,12},{10,14},{12,8},{14,10},{16,20},{18,... | collective-permute-start | bytes 884744 | tf_op jit(solution)/shard_map/ppermute | solution.py:581
  24.9 11.6 %collective-permute-start.5 = (bf16[2,48,1536]{2,1,0:T(8,128)(2,1)S(1)}, bf16[2,48,1536]{2,1,0:T(8,128)(2,1)S(1)}, u32[]{:S(2)}, u32[]{:S(2)}) collective-permute-start(bf16[2,48,1536]{2,1,0:T(8,128)(2,1)S(1)} %pad_maximum_fusion.8), channel_id=1, source_target_pairs={{0,8},{2,10},{4,12},{6,14},{8,0},{10,2},{12,4},{14,6},{16,24},{18,... | collective-permute-start | bytes 884744 | tf_op jit(solution)/shard_map/ppermute | solution.py:581
  26.3 11.2 %collective-permute-start.7 = (bf16[4,48,896]{2,1,0:T(8,128)(2,1)S(1)}, bf16[4,48,896]{2,1,0:T(8,128)(2,1)S(1)}, u32[]{:S(2)}, u32[]{:S(2)}) collective-permute-start(bf16[4,48,896]{2,1,0:T(8,128)(2,1)S(1)} %pad_maximum_fusion.7), channel_id=1, source_target_pairs={{0,4},{2,6},{4,0},{6,2},{8,12},{10,14},{12,8},{14,10},{16,20},{18,... | collective-permute-start | bytes 1032200 | tf_op jit(solution)/shard_map/ppermute | solution.py:581
  27.8 18.2 %collective-permute-start.12 = (bf16[2,48,1920]{2,1,0:T(8,128)(2,1)}, bf16[2,48,1920]{2,1,0:T(8,128)(2,1)}, u32[]{:S(2)}, u32[]{:S(2)}) collective-permute-start(bf16[2,48,1920]{2,1,0:T(8,128)(2,1)} %pad_maximum_fusion.6), channel_id=1, source_target_pairs={{0,16},{2,18},{4,20},{6,22},{8,24},{10,26},{12,28},{14,30},{16,0},... | collective-permute-start | bytes 1105928 | tf_op jit(solution)/shard_map/ppermute | solution.py:581
  30.1 9.8 %copy-start.2 = (bf16[2,1,512,768]{3,2,1,0:T(8,128)(2,1)S(1)}, bf16[2,1,512,768]{3,2,1,0:T(8,128)(2,1)}, u32[]{:S(2)}) copy-start(bf16[2,1,512,768]{3,2,1,0:T(8,128)(2,1)} %param.20) | copy-start | bytes 4718596
  30.1 17.2 %collective-permute-start.9 = (bf16[8,48,768]{2,1,0:T(8,128)(2,1)S(1)}, bf16[8,48,768]{2,1,0:T(8,128)(2,1)}, u32[]{:S(2)}, u32[]{:S(2)}) collective-permute-start(bf16[8,48,768]{2,1,0:T(8,128)(2,1)S(1)} %pad_maximum_fusion.5), channel_id=1, source_target_pairs={{0,2},{2,0},{4,6},{6,4},{8,10},{10,8},{12,14},{14,12},{16,18},{18,... | collective-permute-start | bytes 1769480 | tf_op jit(solution)/shard_map/ppermute | solution.py:581
  37.5 14.1 %collective-permute-start.8 = (bf16[4,48,1536]{2,1,0:T(8,128)(2,1)}, bf16[4,48,1536]{2,1,0:T(8,128)(2,1)}, u32[]{:S(2)}, u32[]{:S(2)}) collective-permute-start(bf16[4,48,1536]{2,1,0:T(8,128)(2,1)} %pad_maximum_fusion.4), channel_id=1, source_target_pairs={{0,4},{2,6},{4,0},{6,2},{8,12},{10,14},{12,8},{14,10},{16,20},{18,... | collective-permute-start | bytes 1769480 | tf_op jit(solution)/shard_map/ppermute | solution.py:581
  39.3 18.2 %collective-permute-start.10 = (bf16[8,48,896]{2,1,0:T(8,128)(2,1)S(1)}, bf16[8,48,896]{2,1,0:T(8,128)(2,1)S(1)}, u32[]{:S(2)}, u32[]{:S(2)}) collective-permute-start(bf16[8,48,896]{2,1,0:T(8,128)(2,1)S(1)} %pad_maximum_fusion.3), channel_id=1, source_target_pairs={{0,2},{2,0},{4,6},{6,4},{8,10},{10,8},{12,14},{14,12},{16,18},{18,... | collective-permute-start | bytes 2064392 | tf_op jit(solution)/shard_map/ppermute | solution.py:581
  39.8 77.4 %copy-start.23 = (s32[6]{0:T(128)}, s32[6]{0:T(128)S(1)}, u32[]{:S(2)}) copy-start(s32[6]{0:T(128)S(1)} %pad_add_fusion.info) | copy-start | bytes 76
  47.2 16.7 %collective-permute-start.13 = (bf16[4,48,1920]{2,1,0:T(8,128)(2,1)S(1)}, bf16[4,48,1920]{2,1,0:T(8,128)(2,1)S(1)}, u32[]{:S(2)}, u32[]{:S(2)}) collective-permute-start(bf16[4,48,1920]{2,1,0:T(8,128)(2,1)S(1)} %pad_maximum_fusion.2), channel_id=1, source_target_pairs={{0,8},{2,10},{4,12},{6,14},{8,0},{10,2},{12,4},{14,6},{16,24},{18,... | collective-permute-start | bytes 2211848 | tf_op jit(solution)/shard_map/ppermute | solution.py:581
  57.5 25.4 %collective-permute-start.18 = (bf16[8,48,1536]{2,1,0:T(8,128)(2,1)S(1)}, bf16[8,48,1536]{2,1,0:T(8,128)(2,1)S(1)}, u32[]{:S(2)}, u32[]{:S(2)}) collective-permute-start(bf16[8,48,1536]{2,1,0:T(8,128)(2,1)S(1)} %pad_maximum_fusion.1), channel_id=1, source_target_pairs={{0,2},{2,0},{4,6},{6,4},{8,10},{10,8},{12,14},{14,12},{16,18},{18,... | collective-permute-start | bytes 3538952 | tf_op jit(solution)/shard_map/ppermute | solution.py:581
  59.9 4.3 %collective-permute-start.14 = (bf16[8,48,768]{2,1,0:T(8,128)(2,1)S(1)}, bf16[8,48,768]{2,1,0:T(8,128)(2,1)S(1)}, u32[]{:S(2)}, u32[]{:S(2)}) collective-permute-start(bf16[8,48,768]{2,1,0:T(8,128)(2,1)S(1)} %pad_maximum_fusion.5), channel_id=1, source_target_pairs={{0,1},{1,0},{2,3},{3,2},{4,5},{5,4},{6,7},{7,6},{8,9},{9,8},{10,11... | collective-permute-start | bytes 1769480 | tf_op jit(solution)/shard_map/ppermute | solution.py:585
  59.9 4.9 %collective-permute-start.16 = (bf16[8,48,896]{2,1,0:T(8,128)(2,1)S(1)}, bf16[8,48,896]{2,1,0:T(8,128)(2,1)S(1)}, u32[]{:S(2)}, u32[]{:S(2)}) collective-permute-start(bf16[8,48,896]{2,1,0:T(8,128)(2,1)S(1)} %pad_maximum_fusion.3), channel_id=1, source_target_pairs={{0,1},{1,0},{2,3},{3,2},{4,5},{5,4},{6,7},{7,6},{8,9},{9,8},{10,11... | collective-permute-start | bytes 2064392 | tf_op jit(solution)/shard_map/ppermute | solution.py:585
  60.4 5.8 %collective-permute-start.17 = (bf16[8,48,896]{2,1,0:T(8,128)(2,1)S(1)}, bf16[8,48,896]{2,1,0:T(8,128)(2,1)S(1)}, u32[]{:S(2)}, u32[]{:S(2)}) collective-permute-start(bf16[8,48,896]{2,1,0:T(8,128)(2,1)S(1)} %collective-permute-done.10), channel_id=1, source_target_pairs={{0,1},{1,0},{2,3},{3,2},{4,5},{5,4},{6,7},{7,6},{8,9},{9,8},{10,11... | collective-permute-start | bytes 2064392 | tf_op jit(solution)/shard_map/ppermute | solution.py:585
  64.0 2.2 collective-permute-start.15
  64.2 15.5 %copy-start.13 = (bf16[8,48,768]{2,1,0:T(8,128)(2,1)}, bf16[8,48,768]{2,1,0:T(8,128)(2,1)S(1)}, u32[]{:S(2)}) copy-start(bf16[8,48,768]{2,1,0:T(8,128)(2,1)S(1)} %collective-permute-done.14) | copy-start | bytes 1769476
  64.2 34.8 %collective-permute-start.21 = (bf16[8,48,1920]{2,1,0:T(8,128)(2,1)S(1)}, bf16[8,48,1920]{2,1,0:T(8,128)(2,1)S(1)}, u32[]{:S(2)}, u32[]{:S(2)}) collective-permute-start(bf16[8,48,1920]{2,1,0:T(8,128)(2,1)S(1)} %pad_maximum_fusion), channel_id=1, source_target_pairs={{0,4},{2,6},{4,0},{6,2},{8,12},{10,14},{12,8},{14,10},{16,20},{18,... | collective-permute-start | bytes 4423688 | tf_op jit(solution)/shard_map/ppermute | solution.py:581
  64.8 14.9 %copy-start.3 = (bf16[8,48,896]{2,1,0:T(8,128)(2,1)}, bf16[8,48,896]{2,1,0:T(8,128)(2,1)S(1)}, u32[]{:S(2)}) copy-start(bf16[8,48,896]{2,1,0:T(8,128)(2,1)S(1)} %collective-permute-done.16) | copy-start | bytes 2064388
  64.8 18.7 %collective-permute-start.19 = (bf16[8,48,1536]{2,1,0:T(8,128)(2,1)S(1)}, bf16[8,48,1536]{2,1,0:T(8,128)(2,1)S(1)}, u32[]{:S(2)}, u32[]{:S(2)}) collective-permute-start(bf16[8,48,1536]{2,1,0:T(8,128)(2,1)S(1)} %pad_maximum_fusion.1), channel_id=1, source_target_pairs={{0,1},{1,0},{2,3},{3,2},{4,5},{5,4},{6,7},{7,6},{8,9},{9,8},{10,11... | collective-permute-start | bytes 3538952 | tf_op jit(solution)/shard_map/ppermute | solution.py:585
  66.2 13.5 %copy-start.15 = (bf16[8,48,768]{2,1,0:T(8,128)(2,1)}, bf16[8,48,768]{2,1,0:T(8,128)(2,1)S(1)}, u32[]{:S(2)}) copy-start(bf16[8,48,768]{2,1,0:T(8,128)(2,1)S(1)} %collective-permute-done.15) | copy-start | bytes 1769476
  66.2 13.5 %copy-start.5 = (bf16[8,48,896]{2,1,0:T(8,128)(2,1)}, bf16[8,48,896]{2,1,0:T(8,128)(2,1)S(1)}, u32[]{:S(2)}) copy-start(bf16[8,48,896]{2,1,0:T(8,128)(2,1)S(1)} %collective-permute-done.17) | copy-start | bytes 2064388
  79.7 19.8 %copy-start.19 = (bf16[512,384]{1,0:T(8,128)(2,1)}, bf16[512,384]{1,0:T(8,128)(2,1)S(1)}, u32[]{:S(2)}) copy-start(bf16[512,384]{1,0:T(8,128)(2,1)S(1)} %get-tuple-element.152.att_other) | copy-start | bytes 1179652
  83.0 2.8 %collective-permute-start.20 = (bf16[8,48,1536]{2,1,0:T(8,128)(2,1)S(1)}, bf16[8,48,1536]{2,1,0:T(8,128)(2,1)S(1)}, u32[]{:S(2)}, u32[]{:S(2)}) collective-permute-start(bf16[8,48,1536]{2,1,0:T(8,128)(2,1)S(1)} %collective-permute-done.18), channel_id=1, source_target_pairs={{0,1},{1,0},{2,3},{3,2},{4,5},{5,4},{6,7},{7,6},{8,9},{9,8},{10,11... | collective-permute-start | bytes 3538952 | tf_op jit(solution)/shard_map/ppermute | solution.py:585
  83.0 17.0 %collective-permute-start.22 = (bf16[8,48,1920]{2,1,0:T(8,128)(2,1)S(1)}, bf16[8,48,1920]{2,1,0:T(8,128)(2,1)S(1)}, u32[]{:S(2)}, u32[]{:S(2)}) collective-permute-start(bf16[8,48,1920]{2,1,0:T(8,128)(2,1)S(1)} %pad_maximum_fusion), channel_id=1, source_target_pairs={{0,1},{1,0},{2,3},{3,2},{4,5},{5,4},{6,7},{7,6},{8,9},{9,8},{10,11... | collective-permute-start | bytes 4423688 | tf_op jit(solution)/shard_map/ppermute | solution.py:585
  85.8 13.1 %copy-start.33 = (bf16[3]{0:T(256)(128)(2,1)S(1)}, bf16[3]{0:T(256)(128)(2,1)}, u32[]{:S(2)}) copy-start(bf16[3]{0:T(256)(128)(2,1)} %param.39) | copy-start | bytes 22
  85.8 16.4 %copy-start.25 = (bf16[2,1,512,768]{3,2,1,0:T(8,128)(2,1)S(1)}, bf16[2,1,512,768]{3,2,1,0:T(8,128)(2,1)}, u32[]{:S(2)}) copy-start(bf16[2,1,512,768]{3,2,1,0:T(8,128)(2,1)} %param.23) | copy-start | bytes 4718596
  92.0 19.3 %copy-start.26 = (bf16[512,1536]{1,0:T(8,128)(2,1)}, bf16[512,1536]{1,0:T(8,128)(2,1)S(1)}, u32[]{:S(2)}) copy-start(bf16[512,1536]{1,0:T(8,128)(2,1)S(1)} %get-tuple-element.148.active.right) | copy-start | bytes 4718596
  98.9 3.3 %collective-permute-start.23 = (bf16[8,48,1920]{2,1,0:T(8,128)(2,1)S(1)}, bf16[8,48,1920]{2,1,0:T(8,128)(2,1)S(1)}, u32[]{:S(2)}, u32[]{:S(2)}) collective-permute-start(bf16[8,48,1920]{2,1,0:T(8,128)(2,1)S(1)} %collective-permute-done.21), channel_id=1, source_target_pairs={{0,1},{1,0},{2,3},{3,2},{4,5},{5,4},{6,7},{7,6},{8,9},{9,8},{10,11... | collective-permute-start | bytes 4423688 | tf_op jit(solution)/shard_map/ppermute | solution.py:585
  98.9 13.0 %collective-permute-start.25 = (bf16[768,512]{1,0:T(8,128)(2,1)S(1)}, bf16[768,512]{1,0:T(8,128)(2,1)S(1)}, u32[]{:S(2)}, u32[]{:S(2)}) collective-permute-start(bf16[768,512]{1,0:T(8,128)(2,1)S(1)} %get-tuple-element.160.first_p.left), channel_id=1, source_target_pairs={{0,1},{1,0},{2,3},{3,2},{4,5},{5,4},{6,7},{7,6},{8,9},{9,8},{10,11... | collective-permute-start | bytes 2359304 | tf_op jit(solution)/shard_map/ppermute | solution.py:585
  99.4 12.5 %collective-permute-start.26 = (bf16[512,384]{1,0:T(8,128)(2,1)S(1)}, bf16[512,384]{1,0:T(8,128)(2,1)S(1)}, u32[]{:S(2)}, u32[]{:S(2)}) collective-permute-start(bf16[512,384]{1,0:T(8,128)(2,1)S(1)} %get-tuple-element.152.att_other), channel_id=1, source_target_pairs={{0,1},{1,0},{2,3},{3,2},{4,5},{5,4},{6,7},{7,6},{8,9},{9,8},{10,11... | collective-permute-start | bytes 1179656 | tf_op jit(solution)/shard_map/ppermute | solution.py:585
  99.5 12.4 %collective-permute-start.24 = (bf16[512,1536]{1,0:T(8,128)(2,1)S(1)}, bf16[512,1536]{1,0:T(8,128)(2,1)S(1)}, u32[]{:S(2)}, u32[]{:S(2)}) collective-permute-start(bf16[512,1536]{1,0:T(8,128)(2,1)S(1)} %get-tuple-element.149.other_active), channel_id=1, source_target_pairs={{0,1},{1,0},{2,3},{3,2},{4,5},{5,4},{6,7},{7,6},{8,9},{9,8},{10,11... | collective-permute-start | bytes 4718600 | tf_op jit(solution)/shard_map/ppermute | solution.py:585
  111.3 5.9 %collective-permute-start.27 = (f32[8,768]{1,0:T(8,128)}, f32[8,768]{1,0:T(8,128)}, u32[]{:S(2)}, u32[]{:S(2)}) collective-permute-start(f32[8,768]{1,0:T(8,128)} %get-tuple-element.157.ramp), channel_id=1, source_target_pairs={{0,1},{1,0},{2,3},{3,2},{4,5},{5,4},{6,7},{7,6},{8,9},{9,8},{10,11... | collective-permute-start | bytes 73736 | tf_op jit(solution)/shard_map/ppermute | solution.py:585
  111.5 5.7 %collective-permute-start.28 = (bf16[768,512]{1,0:T(8,128)(2,1)}, bf16[768,512]{1,0:T(8,128)(2,1)}, u32[]{:S(2)}, u32[]{:S(2)}) collective-permute-start(bf16[768,512]{1,0:T(8,128)(2,1)} %get-tuple-element.158.left_in), channel_id=1, source_target_pairs={{0,1},{1,0},{2,3},{3,2},{4,5},{5,4},{6,7},{7,6},{8,9},{9,8},{10,11... | collective-permute-start | bytes 2359304 | tf_op jit(solution)/shard_map/ppermute | solution.py:585
  117.0 5.1 %collective-permute-start.29 = (bf16[512,1536]{1,0:T(8,128)(2,1)}, bf16[512,1536]{1,0:T(8,128)(2,1)}, u32[]{:S(2)}, u32[]{:S(2)}) collective-permute-start(bf16[512,1536]{1,0:T(8,128)(2,1)} %get-tuple-element.161.other_delta), channel_id=1, source_target_pairs={{0,1},{1,0},{2,3},{3,2},{4,5},{5,4},{6,7},{7,6},{8,9},{9,8},{10,11... | collective-permute-start | bytes 4718600 | tf_op jit(solution)/shard_map/ppermute | solution.py:585
  126.5 11.7 %collective-permute-start.30 = (bf16[512,768]{1,0:T(8,128)(2,1)S(1)}, bf16[512,768]{1,0:T(8,128)(2,1)S(1)}, u32[]{:S(2)}, u32[]{:S(2)}) collective-permute-start(bf16[512,768]{1,0:T(8,128)(2,1)S(1)} %get-tuple-element.176.block_own), channel_id=1, source_target_pairs={{0,1},{1,0},{2,3},{3,2},{4,5},{5,4},{6,7},{7,6},{8,9},{9,8},{10,11... | collective-permute-start | bytes 2359304 | tf_op jit(solution)/shard_map/ppermute | solution.py:585
  127.0 28.0 %collective-permute-start.33 = (bf16[8,48,1536]{2,1,0:T(8,128)(2,1)S(1)}, bf16[8,48,1536]{2,1,0:T(8,128)(2,1)S(1)}, u32[]{:S(2)}, u32[]{:S(2)}) collective-permute-start(bf16[8,48,1536]{2,1,0:T(8,128)(2,1)S(1)} %bitcast.124), channel_id=1, source_target_pairs={{0,2},{2,0},{4,6},{6,4},{8,10},{10,8},{12,14},{14,12},{16,18},{18,... | collective-permute-start | bytes 3538952 | tf_op jit(solution)/shard_map/ppermute | solution.py:581
  127.0 32.5 %collective-permute-start.36 = (bf16[400,1536]{1,0:T(8,128)(2,1)S(1)}, bf16[400,1536]{1,0:T(8,128)(2,1)S(1)}, u32[]{:S(2)}, u32[]{:S(2)}) collective-permute-start(bf16[400,1536]{1,0:T(8,128)(2,1)S(1)} %get-tuple-element.196), channel_id=1, source_target_pairs={{0,4},{2,6},{4,0},{6,2},{8,12},{10,14},{12,8},{14,10},{16,20},{18,... | collective-permute-start | bytes 3686408 | tf_op jit(solution)/shard_map/ppermute | solution.py:581
  138.2 14.2 %collective-permute-start.32 = (bf16[768,512]{1,0:T(8,128)(2,1)S(1)}, bf16[768,512]{1,0:T(8,128)(2,1)S(1)}, u32[]{:S(2)}, u32[]{:S(2)}) collective-permute-start(bf16[768,512]{1,0:T(8,128)(2,1)S(1)} %get-tuple-element.185.branch_t), channel_id=1, source_target_pairs={{0,1},{1,0},{2,3},{3,2},{4,5},{5,4},{6,7},{7,6},{8,9},{9,8},{10,11... | collective-permute-start | bytes 2359304 | tf_op jit(solution)/shard_map/ppermute | solution.py:585
  138.3 9.8 %copy-start.14 = (bf16[8,48,768]{2,1,0:T(8,128)(2,1)S(1)}, bf16[8,48,768]{2,1,0:T(8,128)(2,1)}, u32[]{:S(2)}) copy-start(bf16[8,48,768]{2,1,0:T(8,128)(2,1)} %copy-done.13) | copy-start | bytes 1769476
  138.3 9.8 %copy-start.16 = (bf16[8,48,768]{2,1,0:T(8,128)(2,1)S(1)}, bf16[8,48,768]{2,1,0:T(8,128)(2,1)}, u32[]{:S(2)}) copy-start(bf16[8,48,768]{2,1,0:T(8,128)(2,1)} %copy-done.15) | copy-start | bytes 1769476
  145.2 9.9 %collective-permute-start.34 = (bf16[512,768]{1,0:T(8,128)(2,1)S(1)}, bf16[512,768]{1,0:T(8,128)(2,1)S(1)}, u32[]{:S(2)}, u32[]{:S(2)}) collective-permute-start(bf16[512,768]{1,0:T(8,128)(2,1)S(1)} %get-tuple-element.182.qk_other), channel_id=1, source_target_pairs={{0,1},{1,0},{2,3},{3,2},{4,5},{5,4},{6,7},{7,6},{8,9},{9,8},{10,11... | collective-permute-start | bytes 2359304 | tf_op jit(solution)/shard_map/ppermute | solution.py:585
  145.7 2.0 collective-permute-start.31
  147.7 7.4 %collective-permute-start.35 = (bf16[512,384]{1,0:T(8,128)(2,1)S(1)}, bf16[512,384]{1,0:T(8,128)(2,1)S(1)}, u32[]{:S(2)}, u32[]{:S(2)}) collective-permute-start(bf16[512,384]{1,0:T(8,128)(2,1)S(1)} %get-tuple-element.183.v_other), channel_id=1, source_target_pairs={{0,1},{1,0},{2,3},{3,2},{4,5},{5,4},{6,7},{7,6},{8,9},{9,8},{10,11... | collective-permute-start | bytes 1179656 | tf_op jit(solution)/shard_map/ppermute | solution.py:585
  158.0 16.7 %collective-permute-start.37 = (bf16[8,48,896]{2,1,0:T(8,128)(2,1)S(1)}, bf16[8,48,896]{2,1,0:T(8,128)(2,1)S(1)}, u32[]{:S(2)}, u32[]{:S(2)}) collective-permute-start(bf16[8,48,896]{2,1,0:T(8,128)(2,1)S(1)} %bitcast.125), channel_id=1, source_target_pairs={{0,2},{2,0},{4,6},{6,4},{8,10},{10,8},{12,14},{14,12},{16,18},{18,... | collective-permute-start | bytes 2064392 | tf_op jit(solution)/shard_map/ppermute | solution.py:581
  158.4 16.5 %collective-permute-start.38 = (bf16[8,48,768]{2,1,0:T(8,128)(2,1)S(1)}, bf16[8,48,768]{2,1,0:T(8,128)(2,1)S(1)}, u32[]{:S(2)}, u32[]{:S(2)}) collective-permute-start(bf16[8,48,768]{2,1,0:T(8,128)(2,1)S(1)} %bitcast.126), channel_id=1, source_target_pairs={{0,4},{2,6},{4,0},{6,2},{8,12},{10,14},{12,8},{14,10},{16,20},{18,... | collective-permute-start | bytes 1769480 | tf_op jit(solution)/shard_map/ppermute | solution.py:581
  159.6 18.0 %collective-permute-start.42 = (bf16[208,1536]{1,0:T(8,128)(2,1)S(1)}, bf16[208,1536]{1,0:T(8,128)(2,1)S(1)}, u32[]{:S(2)}, u32[]{:S(2)}) collective-permute-start(bf16[208,1536]{1,0:T(8,128)(2,1)S(1)} %get-tuple-element.213), channel_id=1, source_target_pairs={{0,8},{2,10},{4,12},{6,14},{8,0},{10,2},{12,4},{14,6},{16,24},{18,... | collective-permute-start | bytes 1916936 | tf_op jit(solution)/shard_map/ppermute | solution.py:581
  160.0 17.9 %collective-permute-start.39 = (bf16[512,768]{1,0:T(8,128)(2,1)S(1)}, bf16[512,768]{1,0:T(8,128)(2,1)S(1)}, u32[]{:S(2)}, u32[]{:S(2)}) collective-permute-start(bf16[512,768]{1,0:T(8,128)(2,1)S(1)} %input.1.grad_own), channel_id=1, source_target_pairs={{0,1},{1,0},{2,3},{3,2},{4,5},{5,4},{6,7},{7,6},{8,9},{9,8},{10,11... | collective-permute-start | bytes 2359304 | tf_op jit(solution)/shard_map/ppermute | solution.py:585
  174.9 21.5 %collective-permute-start.43 = (bf16[4,48,1536]{2,1,0:T(8,128)(2,1)S(1)}, bf16[4,48,1536]{2,1,0:T(8,128)(2,1)S(1)}, u32[]{:S(2)}, u32[]{:S(2)}) collective-permute-start(bf16[4,48,1536]{2,1,0:T(8,128)(2,1)S(1)} %get-tuple-element.219), channel_id=1, source_target_pairs={{0,4},{2,6},{4,0},{6,2},{8,12},{10,14},{12,8},{14,10},{16,20},{18,... | collective-permute-start | bytes 1769480 | tf_op jit(solution)/shard_map/ppermute | solution.py:581
  175.5 20.5 %collective-permute-start.41 = (bf16[4,48,896]{2,1,0:T(8,128)(2,1)S(1)}, bf16[4,48,896]{2,1,0:T(8,128)(2,1)S(1)}, u32[]{:S(2)}, u32[]{:S(2)}) collective-permute-start(bf16[4,48,896]{2,1,0:T(8,128)(2,1)S(1)} %get-tuple-element.211), channel_id=1, source_target_pairs={{0,4},{2,6},{4,0},{6,2},{8,12},{10,14},{12,8},{14,10},{16,20},{18,... | collective-permute-start | bytes 1032200 | tf_op jit(solution)/shard_map/ppermute | solution.py:581
  177.0 6.7 %collective-permute-start.40 = (bf16[4,48,768]{2,1,0:T(8,128)(2,1)S(1)}, bf16[4,48,768]{2,1,0:T(8,128)(2,1)S(1)}, u32[]{:S(2)}, u32[]{:S(2)}) collective-permute-start(bf16[4,48,768]{2,1,0:T(8,128)(2,1)S(1)} %get-tuple-element.210), channel_id=1, source_target_pairs={{0,2},{2,0},{4,6},{6,4},{8,10},{10,8},{12,14},{14,12},{16,18},{18,... | collective-permute-start | bytes 884744 | tf_op jit(solution)/shard_map/ppermute | solution.py:581
  177.7 20.6 %collective-permute-start.44 = (bf16[112,1536]{1,0:T(8,128)(2,1)S(1)}, bf16[112,1536]{1,0:T(8,128)(2,1)S(1)}, u32[]{:S(2)}, u32[]{:S(2)}) collective-permute-start(bf16[112,1536]{1,0:T(8,128)(2,1)S(1)} %get-tuple-element.215), channel_id=1, source_target_pairs={{0,16},{2,18},{4,20},{6,22},{8,24},{10,26},{12,28},{14,30},{16,0},... | collective-permute-start | bytes 1032200 | tf_op jit(solution)/shard_map/ppermute | solution.py:581
  196.0 11.8 %collective-permute-start.45 = (bf16[2,48,1664]{2,1,0:T(8,128)(2,1)S(1)}, bf16[2,48,1664]{2,1,0:T(8,128)(2,1)S(1)}, u32[]{:S(2)}, u32[]{:S(2)}) collective-permute-start(bf16[2,48,1664]{2,1,0:T(8,128)(2,1)S(1)} %get-tuple-element.224), channel_id=1, source_target_pairs={{0,8},{2,10},{4,12},{6,14},{8,0},{10,2},{12,4},{14,6},{16,24},{18,... | collective-permute-start | bytes 958472 | tf_op jit(solution)/shard_map/ppermute | solution.py:581
  196.5 14.5 %collective-permute-start.47 = (bf16[2,48,1536]{2,1,0:T(8,128)(2,1)S(1)}, bf16[2,48,1536]{2,1,0:T(8,128)(2,1)S(1)}, u32[]{:S(2)}, u32[]{:S(2)}) collective-permute-start(bf16[2,48,1536]{2,1,0:T(8,128)(2,1)S(1)} %get-tuple-element.229), channel_id=1, source_target_pairs={{0,8},{2,10},{4,12},{6,14},{8,0},{10,2},{12,4},{14,6},{16,24},{18,... | collective-permute-start | bytes 884744 | tf_op jit(solution)/shard_map/ppermute | solution.py:581
  198.3 12.8 %collective-permute-start.46 = (bf16[64,1536]{1,0:T(8,128)(2,1)S(1)}, bf16[64,1536]{1,0:T(8,128)(2,1)S(1)}, u32[]{:S(2)}, u32[]{:S(2)}) collective-permute-start(bf16[64,1536]{1,0:T(8,128)(2,1)S(1)} %get-tuple-element.227), channel_id=1, source_target_pairs={{0,2},{2,0},{4,6},{6,4},{8,10},{10,8},{12,14},{14,12},{16,18},{18,... | collective-permute-start | bytes 589832 | tf_op jit(solution)/shard_map/ppermute | solution.py:581
  199.3 22.1 %copy-start.1 = (bf16[48,768]{1,0:T(8,128)(2,1)S(1)}, bf16[48,768]{1,0:T(8,128)(2,1)}, u32[]{:S(2)}) copy-start(bf16[48,768]{1,0:T(8,128)(2,1)} %param.36) | copy-start | bytes 221188
  207.9 12.7 %collective-permute-start.49 = (bf16[1,48,1664]{2,1,0:T(8,128)(2,1)S(1)}, bf16[1,48,1664]{2,1,0:T(8,128)(2,1)S(1)}, u32[]{:S(2)}, u32[]{:S(2)}) collective-permute-start(bf16[1,48,1664]{2,1,0:T(8,128)(2,1)S(1)} %get-tuple-element.234), channel_id=1, source_target_pairs={{0,16},{2,18},{4,20},{6,22},{8,24},{10,26},{12,28},{14,30},{16,0},... | collective-permute-start | bytes 479240 | tf_op jit(solution)/shard_map/ppermute | solution.py:581
  211.1 8.8 %collective-permute-start.48 = (bf16[1,48,1536]{2,1,0:T(8,128)(2,1)S(1)}, bf16[1,48,1536]{2,1,0:T(8,128)(2,1)S(1)}, u32[]{:S(2)}, u32[]{:S(2)}) collective-permute-start(bf16[1,48,1536]{2,1,0:T(8,128)(2,1)S(1)} %get-tuple-element.232), channel_id=1, source_target_pairs={{0,16},{2,18},{4,20},{6,22},{8,24},{10,26},{12,28},{14,30},{16,0},... | collective-permute-start | bytes 442376 | tf_op jit(solution)/shard_map/ppermute | solution.py:581
  (20 other events, 121.0 us)

commit v3 on v2

--- a/solution.py
+++ b/solution.py
@@ -149,11 +149,11 @@
         landed(held.at[i], sems.at[2 + i])
 
 
-def attend_kernel(masks, info, hidden, x_rows, *refs):
+def attend_kernel(masks, back_masks, info, hidden, x_rows, *refs):
     qk, vo = refs[0:4], refs[4:8]
-    q, k, v, att_own, att_other, p, first, first_p = refs[8:16]
-    normed, root, vec = refs[16:19]
-    x, wa, wb, att, flip, wide, extra, sems = refs[19:]
+    q, k, v, att_own, att_other, p, first, first_p, first_back = refs[8:17]
+    normed, root, vec = refs[17:20]
+    x, wa, wb, att, flip, wide, extra, sems = refs[20:]
     me, core = info[0], info[1]
     count = info[2 + core]
     length, width = x.shape
@@ -202,6 +202,7 @@
     first[...] = low
     flip[...] = low.T
     to_blocks(flip, first_p, masks, me)
+    to_blocks(flip, first_back, back_masks, me)
 
 
 def up_kernel(vec, first_p, *refs):
@@ -312,19 +313,16 @@
     to_blocks(flip, feed_back, back_masks, me)
 
 
-def hidden_kernel(feed_r, slope, *refs):
-    pieces = refs[0:4]
-    delta, other_delta, w, sems = refs[4:]
-    half = delta.shape[1]
-    load(pieces[2:] + pieces[:2], w, sems, (0, half))
+def hidden_kernel(h, feed_r, slope, lower, upper, target, w, sems):
+    half = target.shape[1]
+    load((lower, upper), w, sems, (0, half))
     left = feed_r[...].T
     chunk = 512
-    for n, (h, target) in enumerate(((1, other_delta), (0, delta))):
-        loaded(w, n, sems)
-        for c in range(half // chunk):
-            cols = slice(c * chunk, (c + 1) * chunk)
-            at = h * half + c * chunk
-            target[:, cols] = (dot(left, w[n, :, cols]) * slope[:, at : at + chunk].astype(F32)).astype(BF)
+    loaded(w, 0, sems)
+    for c in range(half // chunk):
+        cols = slice(c * chunk, (c + 1) * chunk)
+        at = h * half + c * chunk
+        target[:, cols] = (dot(left, w[0, :, cols]) * slope[:, at : at + chunk].astype(F32)).astype(BF)
 
 
 def down_grad_kernel(info, ramp, ramp_other, left_in, left_other_in, right, right_other_in, *refs):
@@ -565,7 +563,7 @@
     bits = [1 << k for k in range(size.bit_length() - 1)]
     high = bits[2:][::-1]
     x_last, y_last = high + [2, 1], high + [1, 2]
-    return (x_last, x_last, x_last, [1] + high + [2]), (y_last, x_last, x_last, [1] + high + [2])
+    return (x_last, x_last, x_last, [1] + high + [2]), (y_last, x_last, [2] + high + [1], [1] + high + [2])
 
 
 def block_mask(index, order):
@@ -807,13 +805,13 @@
     def blocks_of(columns):
         return shape(2, width, columns)
 
-    q, k, v, att, att_other, p, first, first_p, normed, root, vec = call(
-        functools.partial(attend_kernel, a_masks),
+    q, k, v, att, att_other, p, first, first_p, first_back, normed, root, vec = call(
+        functools.partial(attend_kernel, a_masks, back_masks[2]),
         "attend",
         0,
         18,
         [SCALARS, HBM, VMEM] + [HBM] * 8,
-        in_vmem(row, row, row, slim, slim, probs, row, flat, norm, roots, vectors),
+        in_vmem(row, row, row, slim, slim, probs, row, flat, flat, norm, roots, vectors),
         [of(row), of(blocks_of(width)), of(blocks_of(part)), of(row), of(flat), ((width, length), F32)]
         + [((width, LANES), F32)],
         10,
@@ -821,7 +819,7 @@
     )
     (up_lo, up_hi), (down_lo, down_hi) = pieces
     up = with_other(up_lo, after(up_hi, first))
-    first_in, att_in = swap_core(first_p), swap_core(att_other)
+    first_in, att_in = swap_core(first_back), swap_core(att_other)
     act, act_other, slope = call(
         up_kernel,
         "up",
@@ -848,29 +846,24 @@
         (info, class_bias.astype(F32), vec, cotangents, act, act_other, first, *down, *down),
     )
     feed_in, ramp_in = swap_core(feed_back), swap_core(ramp)
-    delta, delta_other = call(
-        hidden_kernel,
-        "hidden",
-        400,
-        9,
-        [VMEM] * 2 + [HBM] * 4,
-        in_vmem(halved, halved),
-        [of(blocks_of(hidden_half))],
-        4,
-        (after(feed, act_in, first_in, att_in), slope, *down),
-    )
+
+    def hidden(h, feed):
+        (made,) = call(
+            functools.partial(hidden_kernel, h),
+            "hidden",
+            400,
+            6,
+            [VMEM] * 2 + [HBM] * 2,
+            in_vmem(halved),
+            [((1, width, hidden_half), BF)],
+            2,
+            (feed, slope, *down[2 * h : 2 * h + 2]),
+        )
+        return made
+
+    delta_other = hidden(1, after(feed, act_in, first_in, att_in))
     delta_in = swap_core(delta_other)
-    *down_grad, logits_out = call(
-        down_grad_kernel,
-        "down_grad",
-        400,
-        6,
-        [SCALARS, VMEM, VMEM, HBM, HBM, VMEM, HBM],
-        in_vmem(shape(half, hidden_half), shape(half + NOTES, hidden_half), shape(2, classes, dtype=F32)),
-        [of(flat), of(flat), of(halved)],
-        3,
-        (after(info, delta), ramp, ramp_in, feed_back, feed_in, act, act_in),
-    )
+    delta = hidden(0, after(feed, delta_other))
 
     def first_hop(pieces, order):
         return swap(pieces[1], order[-1]) if direct else None
@@ -895,7 +888,6 @@
         sent, kept = add((after(kept, start), arrived))
         return kept, swap(sent, mask)
 
-    down_arrived = swap(down_grad[1], back_d[-1]) if direct else None
 
     def noted_hop(kept, notes, arrived, k, start):
         if not direct:
@@ -923,11 +915,24 @@
         in_vmem(*grad(hidden_half), shape(1, hidden_half, dtype=F32)),
         [of(halved)],
         1,
-        (after(first_p, down_grad[0]), first_in, delta, delta_in),
+        (after(first_back, delta), first_in, delta, delta_in),
     )
     up_grad = by_block(up_grad)
     up_arrived = first_hop(up_grad, back_u)
     block_in = swap_core(after(block_out, up_sums))
+    *down_grad, logits_out = call(
+        down_grad_kernel,
+        "down_grad",
+        400,
+        6,
+        [SCALARS, VMEM, VMEM, HBM, HBM, VMEM, HBM],
+        in_vmem(shape(half, hidden_half), shape(half + NOTES, hidden_half), shape(2, classes, dtype=F32)),
+        [of(flat), of(flat), of(halved)],
+        3,
+        (after(info, up_grad[0]), ramp, ramp_in, feed_back, feed_in, act, act_in),
+    )
+
+    down_arrived = swap(down_grad[1], back_d[-1]) if direct else None
     total, datt, branch, sums_one = call(
         functools.partial(branch_kernel, u_masks, b_masks),
         "branch",
@@ -937,7 +942,7 @@
         in_vmem(norm, row, flat, vectors),
         [of(blocks_of(hidden_half)), of(blocks_of(half)), of(halved), of(flat), of(flat), ((width, length), F32)],
         9,
-        (after(info, up_grad[0]), vec, sums_two, delta, delta_other, second, normed, root, *up, *vo),
+        (after(info, down_grad[0]), vec, sums_two, delta, delta_other, second, normed, root, *up, *vo),
     )
     branch_in, sums_in = swap_core(branch), swap_core(sums_one)
     dqk, dv, dqk_other, dv_other = call(
@@ -952,6 +957,31 @@
         (q, k, v, att, att_other, after(datt, block_in), p),
     )
     dqk_in, dv_in = swap_core(dqk_other), swap_core(dv_other)
+    (out_grad,) = call(
+        out_grad_kernel,
+        "out_grad",
+        0,
+        3,
+        [VMEM] * 4,
+        in_vmem(shape(width, half)),
+        [],
+        0,
+        (after(branch, dqk, sums_in), branch_in, att, att_in),
+    )
+    up_kept, up_arrived = next_hop(up_grad[0], up_arrived, back_u[2], out_grad)
+    input_grads = call(
+        functools.partial(input_grad_kernel, back_masks[1]),
+        "input_grad",
+        0,
+        4,
+        [SCALARS] + [VMEM] * 12,
+        in_vmem(*grad(width), *grad(part)),
+        [((width, LANES), F32)],
+        0,
+        (after(info, up_kept), sums_one, sums_in, up_sums, x_p, x_q, other_p, other_q, dqk, dqk_in, dv, dv_in, out_grad),
+    )
+    qk_grad, vo_grad = by_block(input_grads[:2]), by_block(input_grads[2:])
+    qk_arrived, vo_arrived = first_hop(qk_grad, back_a), first_hop(vo_grad, back_b)
     (input_delta,) = call(
         functools.partial(input_kernel, a_masks, b_masks),
         "input",
@@ -961,39 +991,13 @@
         in_vmem(row),
         [of(blocks_of(width)), of(blocks_of(half)), ((width, length), F32), ((width, length), F32)],
         8,
-        (info, dqk, dv, dqk_other, dv_other, total, *qk, *vo),
-    )
-    (out_grad,) = call(
-        out_grad_kernel,
-        "out_grad",
-        0,
-        3,
-        [VMEM] * 4,
-        in_vmem(shape(width, half)),
-        [],
-        0,
-        (after(branch, dqk, sums_in, input_delta), branch_in, att, att_in),
-    )
-    up_sent, up_kept = add((after(up_grad[0], out_grad), up_arrived)) if direct else (None, up_grad[0])
-    input_grads = call(
-        functools.partial(input_grad_kernel, back_masks[1]),
-        "input_grad",
-        0,
-        4,
-        [SCALARS] + [VMEM] * 12,
-        in_vmem(*grad(width), *grad(part)),
-        [((width, LANES), F32)],
-        0,
-        (after(info, up_kept), sums_one, sums_in, up_sums, x_p, x_q, other_p, other_q, dqk, dqk_in, dv, dv_in, out_grad),
-    )
-    qk_grad, vo_grad = by_block(input_grads[:2]), by_block(input_grads[2:])
-    qk_arrived, vo_arrived = first_hop(qk_grad, back_a), first_hop(vo_grad, back_b)
+        (after(info, qk_grad[0]), dqk, dv, dqk_other, dv_other, total, *qk, *vo),
+    )
     input_delta_in = swap_core(input_delta)
     down_kept, notes, down_arrived = noted_hop(down_grad[0], down_grad[1][half:], down_arrived, 2, qk_grad[0])
-    vo_kept, vo_arrived = next_hop(vo_grad[0], vo_arrived, back_b[2], down_kept)
+    up_kept, up_arrived = next_hop(up_kept, up_arrived, back_u[1], down_kept)
+    vo_kept, vo_arrived = next_hop(vo_grad[0], vo_arrived, back_b[2], up_kept)
     qk_kept, qk_arrived = next_hop(qk_grad[0], qk_arrived, back_a[2], vo_kept)
-    up_arrived = swap(after(up_sent, qk_kept), back_u[2]) if direct else None
-    down_kept, notes, down_arrived = noted_hop(down_kept, notes, down_arrived, 1, qk_kept)
     blocks_out, input_grad = call(
         arrange_kernel,
         "arrange",
@@ -1008,11 +1012,11 @@
     if direct:
         sent, kept = add((after(qk_kept, blocks_out), qk_arrived), (vo_kept, vo_arrived))
         arrived = swap(sent, back_a[1])
-        up_kept, up_arrived = next_hop(up_kept, up_arrived, back_u[1], kept)
-        down_kept, notes, down_arrived = noted_hop(down_kept, notes, down_arrived, 0, up_kept)
-        sent, kept = add((after(kept, down_kept), arrived))
+        down_kept, notes, down_arrived = noted_hop(down_kept, notes, down_arrived, 1, kept)
+        up_kept, up_arrived = next_hop(up_kept, up_arrived, back_u[0], kept)
+        sent, kept = add((after(kept, up_kept), arrived))
         arrived = swap(sent, back_a[0])
-        up_kept, up_arrived = next_hop(up_kept, up_arrived, back_u[0], kept)
+        down_kept, notes, down_arrived = noted_hop(down_kept, notes, down_arrived, 0, kept)
         down_kept, up_kept = after(down_kept, kept), after(up_kept, kept)
         down_share, up_share = down_kept + down_arrived[:rows], (up_kept + up_arrived)[0]
         (pool_grad,) = call(

time: 226 us -> 222 us (0.982)
  waiting for transfers between devices: 98.1 us -> 87.9 us
  Pallas kernels: 72.7 us -> 77.5 us
  starting transfers between devices: 35.7 us -> 40.4 us
  local copies, waits for them, and re-layouts: 5.05 us -> 2.59 us
    ppermute x30, waiting for transfers between devices: 90.3 us -> 78.4 us  [swap(): return lax.ppermute(array, 'dp', [(i, i ^ mask) for i in range(size)])]
    pallas_call x25 -> x26, Pallas kernels: 72.7 us -> 77.5 us  [call(): pl.pallas_call(body, name=name, in_specs=in_specs, out_specs=[spec for _,...]
    ppermute x30, starting transfers between devices: 31.2 us -> 36 us  [swap(): return lax.ppermute(array, 'dp', [(i, i ^ mask) for i in range(size)])]
    unnamed x68 -> x56, local copies, waits for them, and re-layouts: 2.6 us -> 0.13 us
  transfers between devices with their start and end apart: 50 -> 50, of which waited for: 22 -> 24; matrix products, arithmetic and copies ran while one was open for 5% -> 5% of each run, Pallas kernels for 30% -> 35%
where the time goes in v3:
time: 222 us; the launch traced here: 218 us
  waiting for transfers between devices  87.9 us (40%)
  Pallas kernels  77.5 us (35%)
  starting transfers between devices  40.4 us (18%)
  other arithmetic  8.56 us (4%)
  local copies, waits for them, and re-layouts  2.59 us (1%)
    ppermute x30, waiting for transfers between devices, swap(): return lax.ppermute(array, 'dp', [(i, i ^ mask) for i in range(size)])  78.4 us
    pallas_call x26, Pallas kernels, call(): pl.pallas_call(body, name=name, in_specs=in_specs, out_specs=[spec for _,...  77.5 us
    ppermute x30, starting transfers between devices, swap(): return lax.ppermute(array, 'dp', [(i, i ^ mask) for i in range(size)])  36 us
    ppermute x20, waiting for transfers between devices, swap_core(): return lax.ppermute(array, 'tensor', [(0, 1), (1, 0)])  9.49 us
    concatenate x12, other arithmetic, join(): return jnp.concatenate([left, right], 0)  4.61 us
  transfers between devices with their start and end apart: 50, of which 24 were waited for; matrix products, arithmetic and copies ran while one was open for 5% of the time, Pallas kernels for 35%

profile of v3, /device:TPU:0, one launch (start us, length us, event | category | flops | bytes accessed | tf_op | source)
XLA Modules:
  0.0 218.5 jit_solution(18367980984803836561)
XLA Ops:
  0.7 0.9 slice_bitcast_fusion
  1.6 4.1 %collective-permute-start = (bf16[1,48,768]{2,1,0:T(8,128)(2,1)S(1)}, bf16[1,48,768]{2,1,0:T(8,128)(2,1)S(1)}, u32[]{:S(2)}, u32[]{:S(2)}) collective-permute-start(bf16[1,48,768]{2,1,0:T(8,128)(2,1)S(1)} %fusion.6), channel_id=1, source_target_pairs={{0,16},{2,18},{4,20},{6,22},{8,24},{10,26},{12,28},{14,30},{16,0},... | collective-permute-start | bytes 221192 | tf_op jit(solution)/shard_map/ppermute | solution.py:579
  5.7 1.6 concatenate.61
  7.9 0.8 maximum_bitcast_fusion.1
  9.6 1.2 collective-permute-start.3
  10.8 4.4 %collective-permute-done.1 = bf16[1,48,896]{2,1,0:T(8,128)(2,1)S(1)} collective-permute-done((bf16[1,48,896]{2,1,0:T(8,128)(2,1)S(1)}, bf16[1,48,896]{2,1,0:T(8,128)(2,1)S(1)}, u32[]{:S(2)}, u32[]{:S(2)}) %collective-permute-start.1) | collective-permute-done | bytes 86048 | tf_op jit(solution)/shard_map/ppermute | solution.py:579
  15.3 0.9 maximum_bitcast_fusion
  16.2 1.8 collective-permute-start.11
  18.0 2.0 collective-permute-start.4
  20.0 1.6 collective-permute-start.6
  22.2 2.6 %collective-permute-done.4 = bf16[2,48,896]{2,1,0:T(8,128)(2,1)S(1)} collective-permute-done((bf16[2,48,896]{2,1,0:T(8,128)(2,1)S(1)}, bf16[2,48,896]{2,1,0:T(8,128)(2,1)S(1)}, u32[]{:S(2)}, u32[]{:S(2)}) %collective-permute-start.4) | collective-permute-done | bytes 172064 | tf_op jit(solution)/shard_map/ppermute | solution.py:579
  25.5 0.8 pad_maximum_fusion.6
  26.3 1.5 collective-permute-start.7
  27.8 2.2 collective-permute-start.12
  30.1 1.5 collective-permute-start.9
  31.6 5.0 %collective-permute-done.5 = bf16[2,48,1536]{2,1,0:T(8,128)(2,1)S(1)} collective-permute-done((bf16[2,48,1536]{2,1,0:T(8,128)(2,1)S(1)}, bf16[2,48,1536]{2,1,0:T(8,128)(2,1)S(1)}, u32[]{:S(2)}, u32[]{:S(2)}) %collective-permute-start.5) | collective-permute-done | bytes 294944 | tf_op jit(solution)/shard_map/ppermute | solution.py:579
  36.6 0.9 pad_maximum_fusion.4
  37.5 1.8 collective-permute-start.8
  39.8 1.9 prepare.1
  41.8 4.3 %collective-permute-done.12 = bf16[2,48,1920]{2,1,0:T(8,128)(2,1)} collective-permute-done((bf16[2,48,1920]{2,1,0:T(8,128)(2,1)}, bf16[2,48,1920]{2,1,0:T(8,128)(2,1)}, u32[]{:S(2)}, u32[]{:S(2)}) %collective-permute-start.12) | collective-permute-done | bytes 368672 | tf_op jit(solution)/shard_map/ppermute | solution.py:579
  46.1 1.2 pad_maximum_fusion.2
  47.3 4.4 %collective-permute-done.8 = bf16[4,48,1536]{2,1,0:T(8,128)(2,1)} collective-permute-done((bf16[4,48,1536]{2,1,0:T(8,128)(2,1)}, bf16[4,48,1536]{2,1,0:T(8,128)(2,1)}, u32[]{:S(2)}, u32[]{:S(2)}) %collective-permute-start.8) | collective-permute-done | bytes 589856 | tf_op jit(solution)/shard_map/ppermute | solution.py:579
  51.7 1.3 pad_maximum_fusion.1
  53.0 4.5 %collective-permute-done.10 = bf16[8,48,896]{2,1,0:T(8,128)(2,1)S(1)} collective-permute-done((bf16[8,48,896]{2,1,0:T(8,128)(2,1)S(1)}, bf16[8,48,896]{2,1,0:T(8,128)(2,1)S(1)}, u32[]{:S(2)}, u32[]{:S(2)}) %collective-permute-start.10) | collective-permute-done | bytes 688160 | tf_op jit(solution)/shard_map/ppermute | solution.py:579
  57.5 2.3 %collective-permute-start.18 = (bf16[8,48,1536]{2,1,0:T(8,128)(2,1)S(1)}, bf16[8,48,1536]{2,1,0:T(8,128)(2,1)S(1)}, u32[]{:S(2)}, u32[]{:S(2)}) collective-permute-start(bf16[8,48,1536]{2,1,0:T(8,128)(2,1)S(1)} %pad_maximum_fusion.1), channel_id=1, source_target_pairs={{0,2},{2,0},{4,6},{6,4},{8,10},{10,8},{12,14},{14,12},{16,18},{18,... | collective-permute-start | bytes 3538952 | tf_op jit(solution)/shard_map/ppermute | solution.py:579
  60.4 3.6 %collective-permute-done.13 = bf16[4,48,1920]{2,1,0:T(8,128)(2,1)S(1)} collective-permute-done((bf16[4,48,1920]{2,1,0:T(8,128)(2,1)S(1)}, bf16[4,48,1920]{2,1,0:T(8,128)(2,1)S(1)}, u32[]{:S(2)}, u32[]{:S(2)}) %collective-permute-start.13) | collective-permute-done | bytes 737312 | tf_op jit(solution)/shard_map/ppermute | solution.py:579
  65.0 1.2 collective-permute-done.15
  66.2 13.5 %attend.1 = (bf16[512,768]{1,0:T(8,128)(2,1)S(1)}, bf16[512,768]{1,0:T(8,128)(2,1)S(1)}, bf16[512,768]{1,0:T(8,128)(2,1)S(1)}, bf16[512,384]{1,0:T(8,128)(2,1)S(...) custom-call(s32[6]{0:T(128)S(1)} %pad_add_fusion.info, ...), custom_call_target="tpu_custom_call" | custom-call | bytes 1024 | tf_op jit(solution)/shard_map/attend/pallas_call | solution.py:550
  79.8 3.2 %collective-permute-done.18 = bf16[8,48,1536]{2,1,0:T(8,128)(2,1)S(1)} collective-permute-done((bf16[8,48,1536]{2,1,0:T(8,128)(2,1)S(1)}, bf16[8,48,1536]{2,1,0:T(8,128)(2,1)S(1)}, u32[]{:S(2)}, u32[]{:S(2)}) %collective-permute-start.18) | collective-permute-done | bytes 1179680 | tf_op jit(solution)/shard_map/ppermute | solution.py:579
  83.5 2.3 %collective-permute-done.20 = bf16[8,48,1536]{2,1,0:T(8,128)(2,1)S(1)} collective-permute-done((bf16[8,48,1536]{2,1,0:T(8,128)(2,1)S(1)}, bf16[8,48,1536]{2,1,0:T(8,128)(2,1)S(1)}, u32[]{:S(2)}, u32[]{:S(2)}) %collective-permute-start.20) | collective-permute-done | bytes 1179680 | tf_op jit(solution)/shard_map/ppermute | solution.py:583
  85.8 6.3 %up.1 = (bf16[512,1536]{1,0:T(8,128)(2,1)S(1)}, bf16[512,1536]{1,0:T(8,128)(2,1)S(1)}, bf16[512,3072]{1,0:T(8,128)(2,1)S(1)}) custom-call(f32[16,768]{1,0:T(8,128)S(1)} %get-tuple-element.145.vec, bf16[768,512]{1,0:T(8,128)(2,1)S(1)} %get-tuple-element.146.first_p, bf16[384,1536]{1,0:T(8,128)(2,1)S(1)} %bitcast.83, bf16[384,1536]{1,0:T(8,128)(2,1)S(1)} %bitcast.98, ...), custom_call_target="tpu_custom_call" | custom-call | bytes 1024 | tf_op jit(solution)/shard_map/up/pallas_call | solution.py:550
  92.2 6.7 %collective-permute-done.21 = bf16[8,48,1920]{2,1,0:T(8,128)(2,1)S(1)} collective-permute-done((bf16[8,48,1920]{2,1,0:T(8,128)(2,1)S(1)}, bf16[8,48,1920]{2,1,0:T(8,128)(2,1)S(1)}, u32[]{:S(2)}, u32[]{:S(2)}) %collective-permute-start.21) | collective-permute-done | bytes 1474592 | tf_op jit(solution)/shard_map/ppermute | solution.py:579
  100.0 2.2 %collective-permute-done.23 = bf16[8,48,1920]{2,1,0:T(8,128)(2,1)S(1)} collective-permute-done((bf16[8,48,1920]{2,1,0:T(8,128)(2,1)S(1)}, bf16[8,48,1920]{2,1,0:T(8,128)(2,1)S(1)}, u32[]{:S(2)}, u32[]{:S(2)}) %collective-permute-start.23) | collective-permute-done | bytes 1474592 | tf_op jit(solution)/shard_map/ppermute | solution.py:583
  102.2 9.1 %ramp.1 = (bf16[512,768]{1,0:T(8,128)(2,1)}, f32[8,768]{1,0:T(8,128)}, bf16[768,512]{1,0:T(8,128)(2,1)S(1)}, bf16[768,512]{1,0:T(8,128)(2,1)}, f32[512,768]{1,0:T(8,128)S(1)}, /*index=5*/f32[8,768]{1,0:T(8,128)S(1)}) custom-call(s32[6]{0:T(128)S(1)} %pad_add_fusion.info, f32[3]{0:T(128)S(1)} %convert_element_type.20.class_bias, ...), custom_call_target="tpu_custom_call" | custom-call | flops 17250000896 | bytes 1024 | tf_op jit(solution)/shard_map/ramp/pallas_call | solution.py:550
  111.9 3.0 %hidden.2.other_delta = bf16[512,1536]{1,0:T(8,128)(2,1)} custom-call(bf16[768,512]{1,0:T(8,128)(2,1)S(1)} %get-tuple-element.156.feed_r, bf16[512,3072]{1,0:T(8,128)(2,1)S(1)} %get-tuple-element.155.slope, bf16[384,1920]{1,0:T(8,128)(2,1)S(1)} %bitcast.120, bf16[384,1920]{1,0:T(8,128)(2,1)S(1)} %bitcast.123), custom_call_target="tpu_custom_call" | custom-call | flops 460000002048 | bytes 1024 | tf_op jit(solution)/shard_map/hidden/pallas_call | solution.py:550
  115.1 1.8 hidden.3.right.delta
  117.0 1.8 collective-permute-done.27.right_other_in
  118.7 5.2 %up_grad.1 = (bf16[384,1536]{1,0:T(8,128)(2,1)S(1)}, bf16[384,1536]{1,0:T(8,128)(2,1)}, f32[1,1536]{1,0:T(1,128)S(1)}) custom-call(bf16[768,512]{1,0:T(8,128)(2,1)S(1)} %get-tuple-element.157.left, bf16[768,512]{1,0:T(8,128)(2,1)S(1)} %collective-permute-done.25.left_other, bf16[512,1536]{1,0:T(8,128)(2,1)S(1)} %hidden.3.right.delta, ...), custom_call_target="tpu_custom_call" | custom-call | bytes 1024 | tf_op jit(solution)/shard_map/up_grad/pallas_call | solution.py:550
  124.2 5.4 %down_grad.1 = (bf16[384,1536]{1,0:T(8,128)(2,1)S(1)}, bf16[400,1536]{1,0:T(8,128)(2,1)S(1)}, f32[2,3]{1,0:T(2,128)}) custom-call(s32[6]{0:T(128)S(1)} %pad_add_fusion.info, f32[8,768]{1,0:T(8,128)} %get-tuple-element.160.ramp, f32[8,768]{1,0:T(8,128)} %collective-permute-done.28.ramp_other, bf16[768,512]{1,0:T(8,128)(2,1)} %get-tuple-element.161.left_in, ...), custom_call_target="tpu_custom_call" | custom-call | flops 460000002048 | bytes 1024 | tf_op jit(solution)/shard_map/down_grad/pallas_call | solution.py:550
  129.6 1.5 collective-permute-start.36
  131.1 8.6 %branch.1 = (f32[512,768]{1,0:T(8,128)S(1)}, bf16[512,768]{1,0:T(8,128)(2,1)S(1)}, bf16[768,512]{1,0:T(8,128)(2,1)S(1)}, f32[16,768]{1,0:T(8,128)S(1)}) custom-call(s32[6]{0:T(128)S(1)} %pad_add_fusion.info, f32[16,768]{1,0:T(8,128)S(1)} %get-tuple-element.145.vec, f32[8,768]{1,0:T(8,128)S(1)} %get-tuple-element.164.sums_in, ...), custom_call_target="tpu_custom_call" | custom-call | bytes 1024 | tf_op jit(solution)/shard_map/branch/pallas_call | solution.py:550
  139.8 6.9 %back.1 = (bf16[512,768]{1,0:T(8,128)(2,1)S(1)}, bf16[512,384]{1,0:T(8,128)(2,1)S(1)}, bf16[512,768]{1,0:T(8,128)(2,1)S(1)}, bf16[512,384]{1,0:T(8,128)(2,1)S(1)}) custom-call(bf16[512,768]{1,0:T(8,128)(2,1)S(1)} %get-tuple-element.169.q, bf16[512,768]{1,0:T(8,128)(2,1)S(1)} %get-tuple-element.170.k, bf16[512,768]{1,0:T(8,128)(2,1)S(1)} %get-tuple-element.171.v, ...), custom_call_target="tpu_custom_call" | custom-call | bytes 1024 | tf_op jit(solution)/shard_map/back/pallas_call | solution.py:550
  147.3 1.9 collective-permute-done.31.sums_other
  149.6 1.0 out_grad.1
  150.6 2.1 collective-permute-done.33.refs_1_
  152.7 1.4 hop.7
  154.1 3.1 %input_grad.1 = (bf16[384,768]{1,0:T(8,128)(2,1)S(1)}, bf16[384,768]{1,0:T(8,128)(2,1)S(1)}, bf16[384,896]{1,0:T(8,128)(2,1)S(1)}, bf16[384,896]{1,0:T(8,128)(2,1)S(1)}) custom-call(s32[6]{0:T(128)S(1)} %pad_add_fusion.info, f32[16,768]{1,0:T(8,128)S(1)} %get-tuple-element.180.sums_in, f32[16,768]{1,0:T(8,128)S(1)} %collective-permute-done.31.sums_other, ...), custom_call_target="tpu_custom_call" | custom-call | bytes 1024 | tf_op jit(solution)/shard_map/input_grad/pallas_call | solution.py:550
  157.9 1.1 collective-permute-start.39
  159.0 4.0 %input.1.grad_own = bf16[512,768]{1,0:T(8,128)(2,1)S(1)} custom-call(s32[6]{0:T(128)S(1)} %pad_add_fusion.info, bf16[512,768]{1,0:T(8,128)(2,1)S(1)} %get-tuple-element.179.qk.qk_own, bf16[512,384]{1,0:T(8,128)(2,1)S(1)} %get-tuple-element.191.values.v_own, bf16[512,768]{1,0:T(8,128)(2,1)S(1)} %get-tuple-element.190.qk_other, ...), custom_call_target="tpu_custom_call" | custom-call | bytes 1024 | tf_op jit(solution)/shard_map/input/pallas_call | solution.py:550
  163.3 1.8 collective-permute-start.45
  165.1 8.7 %collective-permute-done.37.refs_1_ = bf16[4,48,1536]{2,1,0:T(8,128)(2,1)S(1)} collective-permute-done((bf16[4,48,1536]{2,1,0:T(8,128)(2,1)S(1)}, bf16[4,48,1536]{2,1,0:T(8,128)(2,1)S(1)}, u32[]{:S(2)}, u32[]{:S(2)}) %collective-permute-start.37) | collective-permute-done | bytes 589856 | tf_op jit(solution)/shard_map/ppermute | solution.py:579
  174.3 0.9 collective-permute-start.42
  175.3 1.2 collective-permute-start.41
  176.5 3.4 %arrange.1 = (bf16[2,512,768]{2,1,0:T(8,128)(2,1)}, bf16[2,512,768]{2,1,0:T(8,128)(2,1)}) custom-call(s32[6]{0:T(128)S(1)} %pad_add_fusion.info, bf16[512,768]{1,0:T(8,128)(2,1)} %get-tuple-element.176.block_own, bf16[512,768]{1,0:T(8,128)(2,1)} %collective-permute-done.30.block_other, bf16[512,768]{1,0:T(8,128)(2,1)S(1)} %input.1.grad_own, ...), custom_call_target="tpu_custom_call" | custom-call | bytes 1024 | tf_op jit(solution)/shard_map/arrange/pallas_call | solution.py:550
  179.9 2.4 %collective-permute-done.41.refs_1_ = bf16[4,48,768]{2,1,0:T(8,128)(2,1)S(1)} collective-permute-done((bf16[4,48,768]{2,1,0:T(8,128)(2,1)S(1)}, bf16[4,48,768]{2,1,0:T(8,128)(2,1)S(1)}, u32[]{:S(2)}, u32[]{:S(2)}) %collective-permute-start.41) | collective-permute-done | bytes 294944 | tf_op jit(solution)/shard_map/ppermute | solution.py:579
  183.0 9.3 %collective-permute-done.45.arrived = bf16[208,1536]{1,0:T(8,128)(2,1)S(1)} collective-permute-done((bf16[208,1536]{1,0:T(8,128)(2,1)S(1)}, bf16[208,1536]{1,0:T(8,128)(2,1)S(1)}, u32[]{:S(2)}, u32[]{:S(2)}) %collective-permute-start.45) | collective-permute-done | bytes 639008 | tf_op jit(solution)/shard_map/ppermute | solution.py:579
  192.5 2.0 collective-permute-start.44
  194.5 1.0 collective-permute-start.48
  195.5 10.2 %collective-permute-done.44.refs_1_ = bf16[2,48,1664]{2,1,0:T(8,128)(2,1)S(1)} collective-permute-done((bf16[2,48,1664]{2,1,0:T(8,128)(2,1)S(1)}, bf16[2,48,1664]{2,1,0:T(8,128)(2,1)S(1)}, u32[]{:S(2)}, u32[]{:S(2)}) %collective-permute-start.44) | collective-permute-done | bytes 319520 | tf_op jit(solution)/shard_map/ppermute | solution.py:579
  205.8 2.7 %collective-permute-start.49 = (bf16[1,48,1664]{2,1,0:T(8,128)(2,1)S(1)}, bf16[1,48,1664]{2,1,0:T(8,128)(2,1)S(1)}, u32[]{:S(2)}, u32[]{:S(2)}) collective-permute-start(bf16[1,48,1664]{2,1,0:T(8,128)(2,1)S(1)} %get-tuple-element.234), channel_id=1, source_target_pairs={{0,16},{2,18},{4,20},{6,22},{8,24},{10,26},{12,28},{14,30},{16,0},... | collective-permute-start | bytes 479240 | tf_op jit(solution)/shard_map/ppermute | solution.py:579
  208.5 1.3 collective-permute-start.47
  210.6 4.6 %collective-permute-done.47 = bf16[64,1536]{1,0:T(8,128)(2,1)S(1)} collective-permute-done((bf16[64,1536]{1,0:T(8,128)(2,1)S(1)}, bf16[64,1536]{1,0:T(8,128)(2,1)S(1)}, u32[]{:S(2)}, u32[]{:S(2)}) %collective-permute-start.47) | collective-permute-done | bytes 196640 | tf_op jit(solution)/shard_map/ppermute | solution.py:579
  216.0 1.5 ramp_grad.1
  217.4 0.8 finish.1
  (147 shorter events, 12.8 us)
Async XLA Ops:
  0.7 21.5 %copy-start.24 = (bf16[48,1536]{1,0:T(8,128)(2,1)S(1)}, bf16[48,1536]{1,0:T(8,128)(2,1)}, u32[]{:S(2)}) copy-start(bf16[48,1536]{1,0:T(8,128)(2,1)} %param.30) | copy-start | bytes 442372
  1.6 8.0 %collective-permute-start = (bf16[1,48,768]{2,1,0:T(8,128)(2,1)S(1)}, bf16[1,48,768]{2,1,0:T(8,128)(2,1)S(1)}, u32[]{:S(2)}, u32[]{:S(2)}) collective-permute-start(bf16[1,48,768]{2,1,0:T(8,128)(2,1)S(1)} %fusion.6), channel_id=1, source_target_pairs={{0,16},{2,18},{4,20},{6,22},{8,24},{10,26},{12,28},{14,30},{16,0},... | collective-permute-start | bytes 221192 | tf_op jit(solution)/shard_map/ppermute | solution.py:579
  8.7 6.5 %collective-permute-start.1 = (bf16[1,48,896]{2,1,0:T(8,128)(2,1)S(1)}, bf16[1,48,896]{2,1,0:T(8,128)(2,1)S(1)}, u32[]{:S(2)}, u32[]{:S(2)}) collective-permute-start(bf16[1,48,896]{2,1,0:T(8,128)(2,1)S(1)} %maximum_bitcast_fusion.1), channel_id=1, source_target_pairs={{0,16},{2,18},{4,20},{6,22},{8,24},{10,26},{12,28},{14,30},{16,0},... | collective-permute-start | bytes 258056 | tf_op jit(solution)/shard_map/ppermute | solution.py:579
  9.6 10.4 %collective-permute-start.3 = (bf16[2,48,768]{2,1,0:T(8,128)(2,1)S(1)}, bf16[2,48,768]{2,1,0:T(8,128)(2,1)S(1)}, u32[]{:S(2)}, u32[]{:S(2)}) collective-permute-start(bf16[2,48,768]{2,1,0:T(8,128)(2,1)S(1)} %pad_maximum_fusion.11), channel_id=1, source_target_pairs={{0,8},{2,10},{4,12},{6,14},{8,0},{10,2},{12,4},{14,6},{16,24},{18,... | collective-permute-start | bytes 442376 | tf_op jit(solution)/shard_map/ppermute | solution.py:579
  15.2 7.0 %collective-permute-start.2 = (bf16[1,48,1536]{2,1,0:T(8,128)(2,1)}, bf16[1,48,1536]{2,1,0:T(8,128)(2,1)S(1)}, u32[]{:S(2)}, u32[]{:S(2)}) collective-permute-start(bf16[1,48,1536]{2,1,0:T(8,128)(2,1)} %bitcast.127), channel_id=1, source_target_pairs={{0,16},{2,18},{4,20},{6,22},{8,24},{10,26},{12,28},{14,30},{16,0},... | collective-permute-start | bytes 442376 | tf_op jit(solution)/shard_map/ppermute | solution.py:579
  16.2 9.3 %collective-permute-start.11 = (bf16[1,48,1920]{2,1,0:T(8,128)(2,1)S(1)}, bf16[1,48,1920]{2,1,0:T(8,128)(2,1)S(1)}, u32[]{:S(2)}, u32[]{:S(2)}) collective-permute-start(bf16[1,48,1920]{2,1,0:T(8,128)(2,1)S(1)} %maximum_bitcast_fusion), channel_id=1, source_target_pairs={{0,2},{2,0},{4,6},{6,4},{8,10},{10,8},{12,14},{14,12},{16,18},{18,... | collective-permute-start | bytes 552968 | tf_op jit(solution)/shard_map/ppermute | solution.py:579
  18.0 6.9 %collective-permute-start.4 = (bf16[2,48,896]{2,1,0:T(8,128)(2,1)S(1)}, bf16[2,48,896]{2,1,0:T(8,128)(2,1)S(1)}, u32[]{:S(2)}, u32[]{:S(2)}) collective-permute-start(bf16[2,48,896]{2,1,0:T(8,128)(2,1)S(1)} %pad_maximum_fusion.10), channel_id=1, source_target_pairs={{0,8},{2,10},{4,12},{6,14},{8,0},{10,2},{12,4},{14,6},{16,24},{18,... | collective-permute-start | bytes 516104 | tf_op jit(solution)/shard_map/ppermute | solution.py:579
  20.0 10.0 %collective-permute-start.6 = (bf16[4,48,768]{2,1,0:T(8,128)(2,1)S(1)}, bf16[4,48,768]{2,1,0:T(8,128)(2,1)S(1)}, u32[]{:S(2)}, u32[]{:S(2)}) collective-permute-start(bf16[4,48,768]{2,1,0:T(8,128)(2,1)S(1)} %pad_maximum_fusion.9), channel_id=1, source_target_pairs={{0,4},{2,6},{4,0},{6,2},{8,12},{10,14},{12,8},{14,10},{16,20},{18,... | collective-permute-start | bytes 884744 | tf_op jit(solution)/shard_map/ppermute | solution.py:579
  24.9 11.6 %collective-permute-start.5 = (bf16[2,48,1536]{2,1,0:T(8,128)(2,1)S(1)}, bf16[2,48,1536]{2,1,0:T(8,128)(2,1)S(1)}, u32[]{:S(2)}, u32[]{:S(2)}) collective-permute-start(bf16[2,48,1536]{2,1,0:T(8,128)(2,1)S(1)} %pad_maximum_fusion.8), channel_id=1, source_target_pairs={{0,8},{2,10},{4,12},{6,14},{8,0},{10,2},{12,4},{14,6},{16,24},{18,... | collective-permute-start | bytes 884744 | tf_op jit(solution)/shard_map/ppermute | solution.py:579
  26.3 11.2 %collective-permute-start.7 = (bf16[4,48,896]{2,1,0:T(8,128)(2,1)S(1)}, bf16[4,48,896]{2,1,0:T(8,128)(2,1)S(1)}, u32[]{:S(2)}, u32[]{:S(2)}) collective-permute-start(bf16[4,48,896]{2,1,0:T(8,128)(2,1)S(1)} %pad_maximum_fusion.7), channel_id=1, source_target_pairs={{0,4},{2,6},{4,0},{6,2},{8,12},{10,14},{12,8},{14,10},{16,20},{18,... | collective-permute-start | bytes 1032200 | tf_op jit(solution)/shard_map/ppermute | solution.py:579
  27.8 18.2 %collective-permute-start.12 = (bf16[2,48,1920]{2,1,0:T(8,128)(2,1)}, bf16[2,48,1920]{2,1,0:T(8,128)(2,1)}, u32[]{:S(2)}, u32[]{:S(2)}) collective-permute-start(bf16[2,48,1920]{2,1,0:T(8,128)(2,1)} %pad_maximum_fusion.6), channel_id=1, source_target_pairs={{0,16},{2,18},{4,20},{6,22},{8,24},{10,26},{12,28},{14,30},{16,0},... | collective-permute-start | bytes 1105928 | tf_op jit(solution)/shard_map/ppermute | solution.py:579
  30.0 9.7 %copy-start.25 = (s32[2,1]{0,1:T(1,128)S(1)}, s32[2,1]{0,1:T(1,128)}, u32[]{:S(2)}) copy-start(s32[2,1]{0,1:T(1,128)} %param.22) | copy-start | bytes 28
  30.0 9.7 %copy-start.26 = (s32[2,1]{0,1:T(1,128)S(1)}, s32[2,1]{0,1:T(1,128)}, u32[]{:S(2)}) copy-start(s32[2,1]{0,1:T(1,128)} %param.21) | copy-start | bytes 28
  30.1 9.8 %copy-start.2 = (bf16[2,1,512,768]{3,2,1,0:T(8,128)(2,1)S(1)}, bf16[2,1,512,768]{3,2,1,0:T(8,128)(2,1)}, u32[]{:S(2)}) copy-start(bf16[2,1,512,768]{3,2,1,0:T(8,128)(2,1)} %param.20) | copy-start | bytes 4718596
  30.1 17.2 %collective-permute-start.9 = (bf16[8,48,768]{2,1,0:T(8,128)(2,1)S(1)}, bf16[8,48,768]{2,1,0:T(8,128)(2,1)}, u32[]{:S(2)}, u32[]{:S(2)}) collective-permute-start(bf16[8,48,768]{2,1,0:T(8,128)(2,1)S(1)} %pad_maximum_fusion.5), channel_id=1, source_target_pairs={{0,2},{2,0},{4,6},{6,4},{8,10},{10,8},{12,14},{14,12},{16,18},{18,... | collective-permute-start | bytes 1769480 | tf_op jit(solution)/shard_map/ppermute | solution.py:579
  37.5 14.1 %collective-permute-start.8 = (bf16[4,48,1536]{2,1,0:T(8,128)(2,1)}, bf16[4,48,1536]{2,1,0:T(8,128)(2,1)}, u32[]{:S(2)}, u32[]{:S(2)}) collective-permute-start(bf16[4,48,1536]{2,1,0:T(8,128)(2,1)} %pad_maximum_fusion.4), channel_id=1, source_target_pairs={{0,4},{2,6},{4,0},{6,2},{8,12},{10,14},{12,8},{14,10},{16,20},{18,... | collective-permute-start | bytes 1769480 | tf_op jit(solution)/shard_map/ppermute | solution.py:579
  39.3 18.2 %collective-permute-start.10 = (bf16[8,48,896]{2,1,0:T(8,128)(2,1)S(1)}, bf16[8,48,896]{2,1,0:T(8,128)(2,1)S(1)}, u32[]{:S(2)}, u32[]{:S(2)}) collective-permute-start(bf16[8,48,896]{2,1,0:T(8,128)(2,1)S(1)} %pad_maximum_fusion.3), channel_id=1, source_target_pairs={{0,2},{2,0},{4,6},{6,4},{8,10},{10,8},{12,14},{14,12},{16,18},{18,... | collective-permute-start | bytes 2064392 | tf_op jit(solution)/shard_map/ppermute | solution.py:579
  47.2 16.7 %collective-permute-start.13 = (bf16[4,48,1920]{2,1,0:T(8,128)(2,1)S(1)}, bf16[4,48,1920]{2,1,0:T(8,128)(2,1)S(1)}, u32[]{:S(2)}, u32[]{:S(2)}) collective-permute-start(bf16[4,48,1920]{2,1,0:T(8,128)(2,1)S(1)} %pad_maximum_fusion.2), channel_id=1, source_target_pairs={{0,8},{2,10},{4,12},{6,14},{8,0},{10,2},{12,4},{14,6},{16,24},{18,... | collective-permute-start | bytes 2211848 | tf_op jit(solution)/shard_map/ppermute | solution.py:579
  57.5 25.4 %collective-permute-start.18 = (bf16[8,48,1536]{2,1,0:T(8,128)(2,1)S(1)}, bf16[8,48,1536]{2,1,0:T(8,128)(2,1)S(1)}, u32[]{:S(2)}, u32[]{:S(2)}) collective-permute-start(bf16[8,48,1536]{2,1,0:T(8,128)(2,1)S(1)} %pad_maximum_fusion.1), channel_id=1, source_target_pairs={{0,2},{2,0},{4,6},{6,4},{8,10},{10,8},{12,14},{14,12},{16,18},{18,... | collective-permute-start | bytes 3538952 | tf_op jit(solution)/shard_map/ppermute | solution.py:579
  59.9 4.3 %collective-permute-start.14 = (bf16[8,48,768]{2,1,0:T(8,128)(2,1)S(1)}, bf16[8,48,768]{2,1,0:T(8,128)(2,1)S(1)}, u32[]{:S(2)}, u32[]{:S(2)}) collective-permute-start(bf16[8,48,768]{2,1,0:T(8,128)(2,1)S(1)} %pad_maximum_fusion.5), channel_id=1, source_target_pairs={{0,1},{1,0},{2,3},{3,2},{4,5},{5,4},{6,7},{7,6},{8,9},{9,8},{10,11... | collective-permute-start | bytes 1769480 | tf_op jit(solution)/shard_map/ppermute | solution.py:583
  59.9 4.9 %collective-permute-start.16 = (bf16[8,48,896]{2,1,0:T(8,128)(2,1)S(1)}, bf16[8,48,896]{2,1,0:T(8,128)(2,1)S(1)}, u32[]{:S(2)}, u32[]{:S(2)}) collective-permute-start(bf16[8,48,896]{2,1,0:T(8,128)(2,1)S(1)} %pad_maximum_fusion.3), channel_id=1, source_target_pairs={{0,1},{1,0},{2,3},{3,2},{4,5},{5,4},{6,7},{7,6},{8,9},{9,8},{10,11... | collective-permute-start | bytes 2064392 | tf_op jit(solution)/shard_map/ppermute | solution.py:583
  60.4 5.8 %collective-permute-start.17 = (bf16[8,48,896]{2,1,0:T(8,128)(2,1)S(1)}, bf16[8,48,896]{2,1,0:T(8,128)(2,1)S(1)}, u32[]{:S(2)}, u32[]{:S(2)}) collective-permute-start(bf16[8,48,896]{2,1,0:T(8,128)(2,1)S(1)} %collective-permute-done.10), channel_id=1, source_target_pairs={{0,1},{1,0},{2,3},{3,2},{4,5},{5,4},{6,7},{7,6},{8,9},{9,8},{10,11... | collective-permute-start | bytes 2064392 | tf_op jit(solution)/shard_map/ppermute | solution.py:583
  64.0 2.2 %collective-permute-start.15 = (bf16[8,48,768]{2,1,0:T(8,128)(2,1)}, bf16[8,48,768]{2,1,0:T(8,128)(2,1)S(1)}, u32[]{:S(2)}, u32[]{:S(2)}) collective-permute-start(bf16[8,48,768]{2,1,0:T(8,128)(2,1)} %collective-permute-done.9), channel_id=1, source_target_pairs={{0,1},{1,0},{2,3},{3,2},{4,5},{5,4},{6,7},{7,6},{8,9},{9,8},{10,11... | collective-permute-start | bytes 1769480 | tf_op jit(solution)/shard_map/ppermute | solution.py:583
  64.2 15.6 %copy-start.13 = (bf16[8,48,768]{2,1,0:T(8,128)(2,1)}, bf16[8,48,768]{2,1,0:T(8,128)(2,1)S(1)}, u32[]{:S(2)}) copy-start(bf16[8,48,768]{2,1,0:T(8,128)(2,1)S(1)} %collective-permute-done.14) | copy-start | bytes 1769476
  64.2 34.8 %collective-permute-start.21 = (bf16[8,48,1920]{2,1,0:T(8,128)(2,1)S(1)}, bf16[8,48,1920]{2,1,0:T(8,128)(2,1)S(1)}, u32[]{:S(2)}, u32[]{:S(2)}) collective-permute-start(bf16[8,48,1920]{2,1,0:T(8,128)(2,1)S(1)} %pad_maximum_fusion), channel_id=1, source_target_pairs={{0,4},{2,6},{4,0},{6,2},{8,12},{10,14},{12,8},{14,10},{16,20},{18,... | collective-permute-start | bytes 4423688 | tf_op jit(solution)/shard_map/ppermute | solution.py:579
  64.8 15.0 %copy-start.3 = (bf16[8,48,896]{2,1,0:T(8,128)(2,1)}, bf16[8,48,896]{2,1,0:T(8,128)(2,1)S(1)}, u32[]{:S(2)}) copy-start(bf16[8,48,896]{2,1,0:T(8,128)(2,1)S(1)} %collective-permute-done.16) | copy-start | bytes 2064388
  64.8 18.7 %collective-permute-start.19 = (bf16[8,48,1536]{2,1,0:T(8,128)(2,1)S(1)}, bf16[8,48,1536]{2,1,0:T(8,128)(2,1)S(1)}, u32[]{:S(2)}, u32[]{:S(2)}) collective-permute-start(bf16[8,48,1536]{2,1,0:T(8,128)(2,1)S(1)} %pad_maximum_fusion.1), channel_id=1, source_target_pairs={{0,1},{1,0},{2,3},{3,2},{4,5},{5,4},{6,7},{7,6},{8,9},{9,8},{10,11... | collective-permute-start | bytes 3538952 | tf_op jit(solution)/shard_map/ppermute | solution.py:583
  66.2 13.5 %copy-start.15 = (bf16[8,48,768]{2,1,0:T(8,128)(2,1)}, bf16[8,48,768]{2,1,0:T(8,128)(2,1)S(1)}, u32[]{:S(2)}) copy-start(bf16[8,48,768]{2,1,0:T(8,128)(2,1)S(1)} %collective-permute-done.15) | copy-start | bytes 1769476
  66.2 13.5 %copy-start.5 = (bf16[8,48,896]{2,1,0:T(8,128)(2,1)}, bf16[8,48,896]{2,1,0:T(8,128)(2,1)S(1)}, u32[]{:S(2)}) copy-start(bf16[8,48,896]{2,1,0:T(8,128)(2,1)S(1)} %collective-permute-done.17) | copy-start | bytes 2064388
  79.7 19.7 %copy-start.17 = (bf16[512,384]{1,0:T(8,128)(2,1)}, bf16[512,384]{1,0:T(8,128)(2,1)S(1)}, u32[]{:S(2)}) copy-start(bf16[512,384]{1,0:T(8,128)(2,1)S(1)} %get-tuple-element.153.att_other) | copy-start | bytes 1179652
  83.0 9.2 %copy-start.7 = (bf16[8,48,1536]{2,1,0:T(8,128)(2,1)}, bf16[8,48,1536]{2,1,0:T(8,128)(2,1)S(1)}, u32[]{:S(2)}) copy-start(bf16[8,48,1536]{2,1,0:T(8,128)(2,1)S(1)} %collective-permute-done.18) | copy-start | bytes 3538948
  83.0 2.8 %collective-permute-start.20 = (bf16[8,48,1536]{2,1,0:T(8,128)(2,1)S(1)}, bf16[8,48,1536]{2,1,0:T(8,128)(2,1)S(1)}, u32[]{:S(2)}, u32[]{:S(2)}) collective-permute-start(bf16[8,48,1536]{2,1,0:T(8,128)(2,1)S(1)} %collective-permute-done.18), channel_id=1, source_target_pairs={{0,1},{1,0},{2,3},{3,2},{4,5},{5,4},{6,7},{7,6},{8,9},{9,8},{10,11... | collective-permute-start | bytes 3538952 | tf_op jit(solution)/shard_map/ppermute | solution.py:583
  83.0 17.0 %collective-permute-start.22 = (bf16[8,48,1920]{2,1,0:T(8,128)(2,1)S(1)}, bf16[8,48,1920]{2,1,0:T(8,128)(2,1)S(1)}, u32[]{:S(2)}, u32[]{:S(2)}) collective-permute-start(bf16[8,48,1920]{2,1,0:T(8,128)(2,1)S(1)} %pad_maximum_fusion), channel_id=1, source_target_pairs={{0,1},{1,0},{2,3},{3,2},{4,5},{5,4},{6,7},{7,6},{8,9},{9,8},{10,11... | collective-permute-start | bytes 4423688 | tf_op jit(solution)/shard_map/ppermute | solution.py:583
  85.8 13.1 %copy-start.27 = (bf16[3]{0:T(256)(128)(2,1)S(1)}, bf16[3]{0:T(256)(128)(2,1)}, u32[]{:S(2)}) copy-start(bf16[3]{0:T(256)(128)(2,1)} %param.39) | copy-start | bytes 22
  85.8 16.4 %copy-start.21 = (bf16[2,1,512,768]{3,2,1,0:T(8,128)(2,1)S(1)}, bf16[2,1,512,768]{3,2,1,0:T(8,128)(2,1)}, u32[]{:S(2)}) copy-start(bf16[2,1,512,768]{3,2,1,0:T(8,128)(2,1)} %param.23) | copy-start | bytes 4718596
  98.9 3.3 %collective-permute-start.23 = (bf16[8,48,1920]{2,1,0:T(8,128)(2,1)S(1)}, bf16[8,48,1920]{2,1,0:T(8,128)(2,1)S(1)}, u32[]{:S(2)}, u32[]{:S(2)}) collective-permute-start(bf16[8,48,1920]{2,1,0:T(8,128)(2,1)S(1)} %collective-permute-done.21), channel_id=1, source_target_pairs={{0,1},{1,0},{2,3},{3,2},{4,5},{5,4},{6,7},{7,6},{8,9},{9,8},{10,11... | collective-permute-start | bytes 4423688 | tf_op jit(solution)/shard_map/ppermute | solution.py:583
  98.9 12.9 %collective-permute-start.25 = (bf16[768,512]{1,0:T(8,128)(2,1)S(1)}, bf16[768,512]{1,0:T(8,128)(2,1)S(1)}, u32[]{:S(2)}, u32[]{:S(2)}) collective-permute-start(bf16[768,512]{1,0:T(8,128)(2,1)S(1)} %get-tuple-element.157.left), channel_id=1, source_target_pairs={{0,1},{1,0},{2,3},{3,2},{4,5},{5,4},{6,7},{7,6},{8,9},{9,8},{10,11... | collective-permute-start | bytes 2359304 | tf_op jit(solution)/shard_map/ppermute | solution.py:583
  99.4 12.4 %collective-permute-start.26 = (bf16[512,384]{1,0:T(8,128)(2,1)S(1)}, bf16[512,384]{1,0:T(8,128)(2,1)S(1)}, u32[]{:S(2)}, u32[]{:S(2)}) collective-permute-start(bf16[512,384]{1,0:T(8,128)(2,1)S(1)} %get-tuple-element.153.att_other), channel_id=1, source_target_pairs={{0,1},{1,0},{2,3},{3,2},{4,5},{5,4},{6,7},{7,6},{8,9},{9,8},{10,11... | collective-permute-start | bytes 1179656 | tf_op jit(solution)/shard_map/ppermute | solution.py:583
  99.5 12.4 %collective-permute-start.24 = (bf16[512,1536]{1,0:T(8,128)(2,1)S(1)}, bf16[512,1536]{1,0:T(8,128)(2,1)S(1)}, u32[]{:S(2)}, u32[]{:S(2)}) collective-permute-start(bf16[512,1536]{1,0:T(8,128)(2,1)S(1)} %get-tuple-element.150.other_active), channel_id=1, source_target_pairs={{0,1},{1,0},{2,3},{3,2},{4,5},{5,4},{6,7},{7,6},{8,9},{9,8},{10,11... | collective-permute-start | bytes 4718600 | tf_op jit(solution)/shard_map/ppermute | solution.py:583
  111.3 12.8 %collective-permute-start.28 = (f32[8,768]{1,0:T(8,128)}, f32[8,768]{1,0:T(8,128)}, u32[]{:S(2)}, u32[]{:S(2)}) collective-permute-start(f32[8,768]{1,0:T(8,128)} %get-tuple-element.160.ramp), channel_id=1, source_target_pairs={{0,1},{1,0},{2,3},{3,2},{4,5},{5,4},{6,7},{7,6},{8,9},{9,8},{10,11... | collective-permute-start | bytes 73736 | tf_op jit(solution)/shard_map/ppermute | solution.py:583
  111.5 12.6 %collective-permute-start.29 = (bf16[768,512]{1,0:T(8,128)(2,1)}, bf16[768,512]{1,0:T(8,128)(2,1)}, u32[]{:S(2)}, u32[]{:S(2)}) collective-permute-start(bf16[768,512]{1,0:T(8,128)(2,1)} %get-tuple-element.161.left_in), channel_id=1, source_target_pairs={{0,1},{1,0},{2,3},{3,2},{4,5},{5,4},{6,7},{7,6},{8,9},{9,8},{10,11... | collective-permute-start | bytes 2359304 | tf_op jit(solution)/shard_map/ppermute | solution.py:583
  114.9 3.8 %collective-permute-start.27 = (bf16[512,1536]{1,0:T(8,128)(2,1)}, bf16[512,1536]{1,0:T(8,128)(2,1)}, u32[]{:S(2)}, u32[]{:S(2)}) collective-permute-start(bf16[512,1536]{1,0:T(8,128)(2,1)} %hidden.2.other_delta), channel_id=1, source_target_pairs={{0,1},{1,0},{2,3},{3,2},{4,5},{5,4},{6,7},{7,6},{8,9},{9,8},{10,11... | collective-permute-start | bytes 4718600 | tf_op jit(solution)/shard_map/ppermute | solution.py:583
  123.9 15.8 %collective-permute-start.30 = (bf16[512,768]{1,0:T(8,128)(2,1)}, bf16[512,768]{1,0:T(8,128)(2,1)}, u32[]{:S(2)}, u32[]{:S(2)}) collective-permute-start(bf16[512,768]{1,0:T(8,128)(2,1)} %get-tuple-element.176.block_own), channel_id=1, source_target_pairs={{0,1},{1,0},{2,3},{3,2},{4,5},{5,4},{6,7},{7,6},{8,9},{9,8},{10,11... | collective-permute-start | bytes 2359304 | tf_op jit(solution)/shard_map/ppermute | solution.py:583
  124.1 28.6 %collective-permute-start.33 = (bf16[8,48,1536]{2,1,0:T(8,128)(2,1)}, bf16[8,48,1536]{2,1,0:T(8,128)(2,1)}, u32[]{:S(2)}, u32[]{:S(2)}) collective-permute-start(bf16[8,48,1536]{2,1,0:T(8,128)(2,1)} %bitcast.44), channel_id=1, source_target_pairs={{0,2},{2,0},{4,6},{6,4},{8,10},{10,8},{12,14},{14,12},{16,18},{18,... | collective-permute-start | bytes 3538952 | tf_op jit(solution)/shard_map/ppermute | solution.py:579
  129.6 33.5 %collective-permute-start.36 = (bf16[400,1536]{1,0:T(8,128)(2,1)S(1)}, bf16[400,1536]{1,0:T(8,128)(2,1)S(1)}, u32[]{:S(2)}, u32[]{:S(2)}) collective-permute-start(bf16[400,1536]{1,0:T(8,128)(2,1)S(1)} %get-tuple-element.195), channel_id=1, source_target_pairs={{0,4},{2,6},{4,0},{6,2},{8,12},{10,14},{12,8},{14,10},{16,20},{18,... | collective-permute-start | bytes 3686408 | tf_op jit(solution)/shard_map/ppermute | solution.py:579
  139.7 9.9 %collective-permute-start.32 = (bf16[768,512]{1,0:T(8,128)(2,1)S(1)}, bf16[768,512]{1,0:T(8,128)(2,1)S(1)}, u32[]{:S(2)}, u32[]{:S(2)}) collective-permute-start(bf16[768,512]{1,0:T(8,128)(2,1)S(1)} %get-tuple-element.181.branch_t), channel_id=1, source_target_pairs={{0,1},{1,0},{2,3},{3,2},{4,5},{5,4},{6,7},{7,6},{8,9},{9,8},{10,11... | collective-permute-start | bytes 2359304 | tf_op jit(solution)/shard_map/ppermute | solution.py:583
  139.8 9.9 %copy-start.20 = (bf16[512,384]{1,0:T(8,128)(2,1)S(1)}, bf16[512,384]{1,0:T(8,128)(2,1)}, u32[]{:S(2)}) copy-start(bf16[512,384]{1,0:T(8,128)(2,1)} %copy-done.19) | copy-start | bytes 1179652
  146.7 7.4 %collective-permute-start.34 = (bf16[512,768]{1,0:T(8,128)(2,1)S(1)}, bf16[512,768]{1,0:T(8,128)(2,1)S(1)}, u32[]{:S(2)}, u32[]{:S(2)}) collective-permute-start(bf16[512,768]{1,0:T(8,128)(2,1)S(1)} %get-tuple-element.190.qk_other), channel_id=1, source_target_pairs={{0,1},{1,0},{2,3},{3,2},{4,5},{5,4},{6,7},{7,6},{8,9},{9,8},{10,11... | collective-permute-start | bytes 2359304 | tf_op jit(solution)/shard_map/ppermute | solution.py:583
  147.2 2.0 collective-permute-start.31
  149.2 4.8 %collective-permute-start.35 = (bf16[512,384]{1,0:T(8,128)(2,1)S(1)}, bf16[512,384]{1,0:T(8,128)(2,1)S(1)}, u32[]{:S(2)}, u32[]{:S(2)}) collective-permute-start(bf16[512,384]{1,0:T(8,128)(2,1)S(1)} %get-tuple-element.192.v_other), channel_id=1, source_target_pairs={{0,1},{1,0},{2,3},{3,2},{4,5},{5,4},{6,7},{7,6},{8,9},{9,8},{10,11... | collective-permute-start | bytes 1179656 | tf_op jit(solution)/shard_map/ppermute | solution.py:583
  157.2 17.0 %collective-permute-start.38 = (bf16[8,48,896]{2,1,0:T(8,128)(2,1)S(1)}, bf16[8,48,896]{2,1,0:T(8,128)(2,1)S(1)}, u32[]{:S(2)}, u32[]{:S(2)}) collective-permute-start(bf16[8,48,896]{2,1,0:T(8,128)(2,1)S(1)} %bitcast.124), channel_id=1, source_target_pairs={{0,2},{2,0},{4,6},{6,4},{8,10},{10,8},{12,14},{14,12},{16,18},{18,... | collective-permute-start | bytes 2064392 | tf_op jit(solution)/shard_map/ppermute | solution.py:579
  157.6 16.3 %collective-permute-start.37 = (bf16[4,48,1536]{2,1,0:T(8,128)(2,1)S(1)}, bf16[4,48,1536]{2,1,0:T(8,128)(2,1)S(1)}, u32[]{:S(2)}, u32[]{:S(2)}) collective-permute-start(bf16[4,48,1536]{2,1,0:T(8,128)(2,1)S(1)} %get-tuple-element.199), channel_id=1, source_target_pairs={{0,8},{2,10},{4,12},{6,14},{8,0},{10,2},{12,4},{14,6},{16,24},{18,... | collective-permute-start | bytes 1769480 | tf_op jit(solution)/shard_map/ppermute | solution.py:579
  157.9 17.3 %collective-permute-start.39 = (bf16[8,48,768]{2,1,0:T(8,128)(2,1)S(1)}, bf16[8,48,768]{2,1,0:T(8,128)(2,1)S(1)}, u32[]{:S(2)}, u32[]{:S(2)}) collective-permute-start(bf16[8,48,768]{2,1,0:T(8,128)(2,1)S(1)} %bitcast.125), channel_id=1, source_target_pairs={{0,4},{2,6},{4,0},{6,2},{8,12},{10,14},{12,8},{14,10},{16,20},{18,... | collective-permute-start | bytes 1769480 | tf_op jit(solution)/shard_map/ppermute | solution.py:579
  163.0 13.5 %collective-permute-start.40 = (bf16[512,768]{1,0:T(8,128)(2,1)S(1)}, bf16[512,768]{1,0:T(8,128)(2,1)S(1)}, u32[]{:S(2)}, u32[]{:S(2)}) collective-permute-start(bf16[512,768]{1,0:T(8,128)(2,1)S(1)} %input.1.grad_own), channel_id=1, source_target_pairs={{0,1},{1,0},{2,3},{3,2},{4,5},{5,4},{6,7},{7,6},{8,9},{9,8},{10,11... | collective-permute-start | bytes 2359304 | tf_op jit(solution)/shard_map/ppermute | solution.py:583
  163.3 29.0 %collective-permute-start.45 = (bf16[208,1536]{1,0:T(8,128)(2,1)S(1)}, bf16[208,1536]{1,0:T(8,128)(2,1)S(1)}, u32[]{:S(2)}, u32[]{:S(2)}) collective-permute-start(bf16[208,1536]{1,0:T(8,128)(2,1)S(1)} %get-tuple-element.223), channel_id=1, source_target_pairs={{0,8},{2,10},{4,12},{6,14},{8,0},{10,2},{12,4},{14,6},{16,24},{18,... | collective-permute-start | bytes 1916936 | tf_op jit(solution)/shard_map/ppermute | solution.py:579
  174.3 8.7 %collective-permute-start.42 = (bf16[4,48,896]{2,1,0:T(8,128)(2,1)S(1)}, bf16[4,48,896]{2,1,0:T(8,128)(2,1)S(1)}, u32[]{:S(2)}, u32[]{:S(2)}) collective-permute-start(bf16[4,48,896]{2,1,0:T(8,128)(2,1)S(1)} %get-tuple-element.215), channel_id=1, source_target_pairs={{0,4},{2,6},{4,0},{6,2},{8,12},{10,14},{12,8},{14,10},{16,20},{18,... | collective-permute-start | bytes 1032200 | tf_op jit(solution)/shard_map/ppermute | solution.py:579
  175.3 7.0 %collective-permute-start.41 = (bf16[4,48,768]{2,1,0:T(8,128)(2,1)S(1)}, bf16[4,48,768]{2,1,0:T(8,128)(2,1)S(1)}, u32[]{:S(2)}, u32[]{:S(2)}) collective-permute-start(bf16[4,48,768]{2,1,0:T(8,128)(2,1)S(1)} %get-tuple-element.214), channel_id=1, source_target_pairs={{0,2},{2,0},{4,6},{6,4},{8,10},{10,8},{12,14},{14,12},{16,18},{18,... | collective-permute-start | bytes 884744 | tf_op jit(solution)/shard_map/ppermute | solution.py:579
  176.5 18.0 %collective-permute-start.43 = (bf16[2,48,1536]{2,1,0:T(8,128)(2,1)S(1)}, bf16[2,48,1536]{2,1,0:T(8,128)(2,1)S(1)}, u32[]{:S(2)}, u32[]{:S(2)}) collective-permute-start(bf16[2,48,1536]{2,1,0:T(8,128)(2,1)S(1)} %get-tuple-element.218), channel_id=1, source_target_pairs={{0,16},{2,18},{4,20},{6,22},{8,24},{10,26},{12,28},{14,30},{16,0},... | collective-permute-start | bytes 884744 | tf_op jit(solution)/shard_map/ppermute | solution.py:579
  192.4 16.1 %collective-permute-start.46 = (bf16[112,1536]{1,0:T(8,128)(2,1)S(1)}, bf16[112,1536]{1,0:T(8,128)(2,1)S(1)}, u32[]{:S(2)}, u32[]{:S(2)}) collective-permute-start(bf16[112,1536]{1,0:T(8,128)(2,1)S(1)} %get-tuple-element.225), channel_id=1, source_target_pairs={{0,16},{2,18},{4,20},{6,22},{8,24},{10,26},{12,28},{14,30},{16,0},... | collective-permute-start | bytes 1032200 | tf_op jit(solution)/shard_map/ppermute | solution.py:579
  192.5 13.2 %collective-permute-start.44 = (bf16[2,48,1664]{2,1,0:T(8,128)(2,1)S(1)}, bf16[2,48,1664]{2,1,0:T(8,128)(2,1)S(1)}, u32[]{:S(2)}, u32[]{:S(2)}) collective-permute-start(bf16[2,48,1664]{2,1,0:T(8,128)(2,1)S(1)} %get-tuple-element.221), channel_id=1, source_target_pairs={{0,8},{2,10},{4,12},{6,14},{8,0},{10,2},{12,4},{14,6},{16,24},{18,... | collective-permute-start | bytes 958472 | tf_op jit(solution)/shard_map/ppermute | solution.py:579
  194.5 15.3 %collective-permute-start.48 = (bf16[1,48,1536]{2,1,0:T(8,128)(2,1)S(1)}, bf16[1,48,1536]{2,1,0:T(8,128)(2,1)S(1)}, u32[]{:S(2)}, u32[]{:S(2)}) collective-permute-start(bf16[1,48,1536]{2,1,0:T(8,128)(2,1)S(1)} %get-tuple-element.232), channel_id=1, source_target_pairs={{0,4},{2,6},{4,0},{6,2},{8,12},{10,14},{12,8},{14,10},{16,20},{18,... | collective-permute-start | bytes 442376 | tf_op jit(solution)/shard_map/ppermute | solution.py:579
  205.7 12.5 %copy-start.1 = (bf16[48,768]{1,0:T(8,128)(2,1)S(1)}, bf16[48,768]{1,0:T(8,128)(2,1)}, u32[]{:S(2)}) copy-start(bf16[48,768]{1,0:T(8,128)(2,1)} %param.36) | copy-start | bytes 221188
  205.8 11.7 %collective-permute-start.49 = (bf16[1,48,1664]{2,1,0:T(8,128)(2,1)S(1)}, bf16[1,48,1664]{2,1,0:T(8,128)(2,1)S(1)}, u32[]{:S(2)}, u32[]{:S(2)}) collective-permute-start(bf16[1,48,1664]{2,1,0:T(8,128)(2,1)S(1)} %get-tuple-element.234), channel_id=1, source_target_pairs={{0,16},{2,18},{4,20},{6,22},{8,24},{10,26},{12,28},{14,30},{16,0},... | collective-permute-start | bytes 479240 | tf_op jit(solution)/shard_map/ppermute | solution.py:579
  208.5 6.7 %collective-permute-start.47 = (bf16[64,1536]{1,0:T(8,128)(2,1)S(1)}, bf16[64,1536]{1,0:T(8,128)(2,1)S(1)}, u32[]{:S(2)}, u32[]{:S(2)}) collective-permute-start(bf16[64,1536]{1,0:T(8,128)(2,1)S(1)} %get-tuple-element.230), channel_id=1, source_target_pairs={{0,2},{2,0},{4,6},{6,4},{8,10},{10,8},{12,14},{14,12},{16,18},{18,... | collective-permute-start | bytes 589832 | tf_op jit(solution)/shard_map/ppermute | solution.py:579
  (14 other events, 89.5 us)
